TPU v7x, 32 devices: a whole 2x2x4 slice. The times are simulated.
32 devices in a mesh: parts: 2 (over y), seq: 8 (over z, x), head: 2 (over core).
Axes of the slice: x: 2, y: 2, z: 4, core: 2. Of those that a mesh axis runs over, the one named last changes fastest.
Arguments:
- frames: bfloat16 [4096, 1024], P(('parts', 'seq'), 'head'), parts along dimension 0, may hold values from -40 to 40
- w_query: bfloat16 [1024, 1024], P(None, 'head'), may hold values from -0.1875 to 0.1875
- w_key: bfloat16 [1024, 1024], P(None, 'head'), may hold values from -0.1875 to 0.1875
- w_value: bfloat16 [1024, 1024], P(None, 'head'), may hold values from -0.1875 to 0.1875
- down_bank: bfloat16 [8, 1024, 128], P(None, 'seq'), may hold values from -0.1875 to 0.1875
- up_bank: bfloat16 [8, 128, 1024], P(None, 'seq', 'head'), may hold values from -0.75 to 0.75
- bank_row: int32 [8], replicated, may hold values from 0 to 7, each once
- lang_ids: int32 [16], P('parts'), parts along dimension 0, may hold values from 0 to 7, as said below
- seg_ids: int32 [16], P('parts'), parts along dimension 0, may hold values from 0 to 1, as said below
- lookback: int32 [16], P('parts'), parts along dimension 0, may hold values from 0 to 3, as said below
Outputs:
- context: bfloat16 [4096, 1024], P(('parts', 'seq'), 'head'), parts along dimension 0
There are 2 independent parts, one for each index of `parts`. A program takes and returns all parts, laid end to end along the dimension named above; an argument that names none is the same for every part. Nothing has to cross between parts.
Inputs may be any that keep to these rules, and one draw needn't show every extreme that they name: `seg_ids`: blocks of one utterance are consecutive: the number is 0 at the first block and never falls; the largest number is reached at the last block. `lang_ids`: all blocks of one utterance have the same language; the last utterance has language 8 - 1. `bank_row`: each language names a different bank row. `lookback`: the value 3 is reached in every draw.
All inputs are finite; a program needn't handle non-finite values.
Results may differ from a plain program's by a relative error of at most 0.0093.
Values may be sent and summed in bfloat16 or wider, within the bound.
No kernel may reach another device: no remote copies, remote signals or barrier semaphores. Data moves between devices by JAX's collectives and lax.ppermute only.
A program may use at most 64 MiB of HBM per device.

v0:
```python
import jax
import jax.numpy as jnp
from jax import lax
from jax.sharding import PartitionSpec as P

HD = 64


NEG_LARGE = -1e30


def from_behind(block, axis, distance):
    devices = range(lax.axis_size(axis))
    route = [(i - distance, i) for i in devices if i - distance in devices]
    return lax.ppermute(block, axis, route)


def block_rules(seg_ids, lookback, position, distance, blocks_dev, block_len):
    query_first = position * blocks_dev
    key_first = (position - distance) * blocks_dev
    counter = jnp.arange(blocks_dev, dtype=jnp.int32)
    query_blocks = query_first + counter
    key_blocks = key_first + counter
    query_seg = lax.dynamic_slice_in_dim(seg_ids, query_first, blocks_dev)
    query_reach = lax.dynamic_slice_in_dim(lookback, query_first, blocks_dev)
    key_seg = lax.dynamic_slice_in_dim(seg_ids, jnp.maximum(key_first, 0), blocks_dev)
    allowed = key_blocks[None, :] >= query_blocks[:, None] - query_reach[:, None]
    allowed = allowed & (key_blocks[None, :] <= query_blocks[:, None])
    allowed = allowed & (key_seg[None, :] == query_seg[:, None]) & (key_blocks[None, :] >= 0)
    frames_dev = blocks_dev * block_len
    expanded = jnp.broadcast_to(
        allowed[:, None, :, None], (blocks_dev, block_len, blocks_dev, block_len)
    )
    return (jnp.any(allowed), expanded.reshape(frames_dev, frames_dev))


def attend(carried, query_heads, pair, allowed):
    run_max, run_sum, run_acc = carried
    frames_dev = query_heads.shape[0]
    heads_dev = query_heads.shape[1]
    key_heads = pair[0].reshape(frames_dev, heads_dev, HD)
    value_heads = pair[1].reshape(frames_dev, heads_dev, HD)
    scores = jnp.einsum(
        "qhe,khe->hqk", query_heads, key_heads, preferred_element_type=jnp.float32
    ) * HD ** (-0.5)
    masked = jnp.where(allowed[None], scores, NEG_LARGE)
    new_max = jnp.maximum(run_max, jnp.max(masked, axis=2))
    factor = jnp.exp(run_max - new_max)
    weights = jnp.where(allowed[None], jnp.exp(masked - new_max[:, :, None]), 0.0)
    new_sum = run_sum * factor + jnp.sum(weights, axis=2)
    update = jnp.einsum(
        "hqk,khe->hqe",
        weights.astype(jnp.bfloat16),
        value_heads,
        preferred_element_type=jnp.float32,
    )
    return (new_max, new_sum, run_acc * factor[:, :, None] + update)


def body(
    frames, w_query, w_key, w_value, down_bank, up_bank, bank_row, lang_ids, seg_ids, lookback
):
    seq_count = lax.axis_size("seq")
    position = lax.axis_index("seq")
    frames_dev = frames.shape[0]
    blocks_dev = lang_ids.shape[0] // seq_count
    block_len = frames_dev // blocks_dev
    model_width = w_query.shape[0]
    columns = w_query.shape[1]
    heads_dev = columns // HD
    rank_two = down_bank.shape[2]
    rank_half = rank_two // 2
    wanted = jnp.transpose(jnp.take(bank_row, lang_ids, axis=0).reshape(seq_count, blocks_dev))
    down_send = jnp.take(down_bank, wanted, axis=0)
    up_send = jnp.take(up_bank, wanted, axis=0)
    down_got, up_got = (
        lax.all_to_all(down_send, "seq", split_axis=1, concat_axis=2, tiled=True),
        lax.all_to_all(up_send, "seq", split_axis=1, concat_axis=2, tiled=True),
    )
    down_mine = down_got.reshape(blocks_dev, model_width, rank_two)
    up_mine = up_got.reshape(blocks_dev, rank_two, columns)
    gathered = lax.all_gather(frames, "head", axis=1, tiled=True)
    queries = jnp.dot(gathered, w_query, preferred_element_type=jnp.float32).astype(jnp.bfloat16)
    block_rows = gathered.reshape(blocks_dev, block_len, model_width)
    lowrank = jnp.einsum(
        "bfd,bdr->bfr", block_rows, down_mine, preferred_element_type=jnp.float32
    ).astype(jnp.bfloat16)
    key_extra = jnp.einsum(
        "bfr,brc->bfc",
        lowrank[:, :, :rank_half],
        up_mine[:, :rank_half],
        preferred_element_type=jnp.float32,
    )
    value_extra = jnp.einsum(
        "bfr,brc->bfc",
        lowrank[:, :, rank_half:],
        up_mine[:, rank_half:],
        preferred_element_type=jnp.float32,
    )
    own_keys = (
        jnp.dot(gathered, w_key, preferred_element_type=jnp.float32)
        + key_extra.reshape(frames_dev, columns)
    ).astype(jnp.bfloat16)
    own_values = (
        jnp.dot(gathered, w_value, preferred_element_type=jnp.float32)
        + value_extra.reshape(frames_dev, columns)
    ).astype(jnp.bfloat16)
    own_pair = jnp.stack([own_keys, own_values])
    query_heads = queries.reshape(frames_dev, heads_dev, HD)
    initial = (
        jnp.full((heads_dev, frames_dev), NEG_LARGE, jnp.float32),
        jnp.zeros((heads_dev, frames_dev), jnp.float32),
        jnp.zeros((heads_dev, frames_dev, HD), jnp.float32),
    )

    def visit_tile(carried, pair, distance):
        nonempty, allowed = block_rules(
            seg_ids, lookback, position, distance, blocks_dev, block_len
        )
        return attend(carried, query_heads, pair, allowed)

    carried = visit_tile(initial, own_pair, 0)
    moving = own_pair
    for distance in range(1, 4):
        moving = from_behind(moving, "seq", 1)
        carried = visit_tile(carried, moving, distance)
    run_max, run_sum, run_acc = carried
    context = (run_acc / run_sum[:, :, None]).astype(jnp.bfloat16)
    return jnp.transpose(context, (1, 0, 2)).reshape(frames_dev, columns)


def solution(mesh):
    in_specs = (
        P(("parts", "seq"), "head"),
        P(None, "head"),
        P(None, "head"),
        P(None, "head"),
        P(None, "seq", None),
        P(None, "seq", "head"),
        P(),
        P("parts"),
        P("parts"),
        P("parts"),
    )
    out_specs = P(("parts", "seq"), "head")
    return jax.shard_map(body, mesh=mesh, in_specs=in_specs, out_specs=out_specs, check_vma=False)
```

profile of v0, /device:TPU:24, one launch (start us, length us, event | category | flops | bytes accessed | tf_op | source)
XLA Modules:
  0.0 89.0 jit_solution(13994182844518407746)
XLA Ops:
  2.8 1.5 %gather_fusion.1 = bf16[8,128,128]{2,1,0:T(8,128)(2,1)S(1)} fusion(bf16[8,128,128]{2,1,0:T(8,128)(2,1)} %param.14, s32[1024]{0:T(1024)S(1)} %pad_clamp_fusion), kind=kCustom, calls=%fused_computation.1 | custom fusion | bytes 524320 | tf_op jit(solution)/shard_map/jit(_take)/gather | solution.py:74
  5.1 6.0 %all-to-all-start = ((bf16[1,8,128,128]{3,2,0,1:T(8,128)(2,1)}), bf16[1,8,128,128]{3,2,0,1:T(8,128)(2,1)S(1)}, u32[]{:S(2)}, u32[]{:S(2)}) async-start(bf16[1,8,128,128]{3,2,0,1:T(8,128)(2,1)} %bitcast_select_fusion), calls=%async_computation | async-start | bytes 524288 | tf_op jit(solution)/shard_map/all_to_all | solution.py:77
  19.3 6.0 %all-to-all-start.1 = ((bf16[1,8,16,512]{3,2,0,1:T(8,128)(2,1)}), bf16[1,8,16,512]{3,2,0,1:T(8,128)(2,1)S(1)}, u32[]{:S(2)}, u32[]{:S(2)}) async-start(bf16[1,8,16,512]{3,2,0,1:T(8,128)(2,1)} %bitcast_select_fusion.1), calls=%async_computation.1 | async-start | bytes 262144 | tf_op jit(solution)/shard_map/all_to_all | solution.py:78
  25.3 2.2 %all_gather.3 = bf16[256,1024]{1,0:T(8,128)(2,1)S(1)} all-gather(bf16[256,512]{1,0:T(8,128)(2,1)S(1)} %copy-done.5), channel_id=1, replica_groups=mesh['parts'=2,'seq'=8,'head'=2] {'head'}, dimensions={1}, use_global_device_ids=true | all-gather | bytes 786432 | tf_op jit(solution)/shard_map/all_gather | solution.py:82
  27.8 1.6 %all-to-all-done.1 = bf16[1,8,16,512]{3,2,0,1:T(8,128)(2,1)S(1)} async-done(((bf16[1,8,16,512]{3,2,0,1:T(8,128)(2,1)}), bf16[1,8,16,512]{3,2,0,1:T(8,128)(2,1)S(1)}, u32[]{:S(2)}, u32[]{:S(2)}) %all-to-all-start.1) | async-done | bytes 131104 | tf_op jit(solution)/shard_map/all_to_all | solution.py:78
  31.6 3.0 %collective-permute-start = (bf16[2,256,512]{2,1,0:T(8,128)(2,1)}, bf16[2,256,512]{2,1,0:T(8,128)(2,1)}, u32[]{:S(2)}, u32[]{:S(2)}) collective-permute-start(bf16[2,256,512]{2,1,0:T(8,128)(2,1)} %pad_maximum_fusion), channel_id=1, source_target_pairs={{0,2},{2,4},{4,6},{6,8},{8,10},{10,12},{12,14},{1,3},{3,5},{5,7},{... | collective-permute-start | bytes 1572872 | tf_op jit(solution)/shard_map/ppermute | solution.py:15
  37.0 1.4 %fusion = (f32[8,256]{1,0:T(8,128)S(1)}, f32[8,256,256]{1,2,0:T(8,128)S(1)}) fusion(pred[]{:T(512)} %bitcast.3, bf16[256,8,64]{0,2,1:T(8,128)(2,1)S(1)} %bitcast.158, bf16[256,8,64]{0,2,1:T(8,128)(2,1)} %bitcast.165), kind=kOutput, calls=%fused_computation.11 | convolution fusion | flops 68679680 | bytes 2629633 | tf_op jit(solution)/shard_map/qhe,khe->hqk/dot_general | solution.py:43
  38.4 8.7 %collective-permute-done = bf16[2,256,512]{2,1,0:T(8,128)(2,1)} collective-permute-done((bf16[2,256,512]{2,1,0:T(8,128)(2,1)}, bf16[2,256,512]{2,1,0:T(8,128)(2,1)}, u32[]{:S(2)}, u32[]{:S(2)}) %collective-permute-start) | collective-permute-done | bytes 524320 | tf_op jit(solution)/shard_map/ppermute | solution.py:15
  47.1 2.5 %collective-permute-start.1 = (bf16[2,256,512]{2,1,0:T(8,128)(2,1)}, bf16[2,256,512]{2,1,0:T(8,128)(2,1)}, u32[]{:S(2)}, u32[]{:S(2)}) collective-permute-start(bf16[2,256,512]{2,1,0:T(8,128)(2,1)} %collective-permute-done), channel_id=1, source_target_pairs={{0,2},{2,4},{4,6},{6,8},{8,10},{10,12},{12,14},{1,3},{3,5},{5,7},{... | collective-permute-start | bytes 1572872 | tf_op jit(solution)/shard_map/ppermute | solution.py:15
  49.6 1.9 %fusion.71 = (bf16[1,256,512]{2,1,0:T(8,128)(2,1)}, bf16[1,256,512]{2,1,0:T(8,128)(2,1)}) fusion(bf16[2,256,512]{2,1,0:T(8,128)(2,1)} %collective-permute-done), kind=kLoop, calls=%fused_computation.108 | loop fusion | bytes 1048576 | tf_op jit(solution)/shard_map/slice | solution.py:42
  51.5 1.8 %copy.47 = bf16[1,256,512]{1,2,0:T(8,128)(2,1)} copy(bf16[1,256,512]{2,1,0:T(8,128)(2,1)} %get-tuple-element.17) | data formatting | bytes 524288 | tf_op jit(solution)/shard_map/slice | solution.py:42
  53.3 1.8 %copy.46 = bf16[1,256,512]{1,2,0:T(8,128)(2,1)} copy(bf16[1,256,512]{2,1,0:T(8,128)(2,1)} %get-tuple-element.18) | data formatting | bytes 524288 | tf_op jit(solution)/shard_map/slice | solution.py:41
  55.0 2.8 %fusion.1 = (f32[8,256]{1,0:T(8,128)S(1)}, f32[8,256,256]{1,2,0:T(8,128)}) fusion(pred[]{:T(512)} %bitcast.22, bf16[256,8,64]{0,2,1:T(8,128)(2,1)S(1)} %bitcast.159, bf16[256,8,64]{0,2,1:T(8,128)(2,1)} %bitcast.166), kind=kOutput, calls=%fused_computation.12 | convolution fusion | flops 68679680 | bytes 2629633 | tf_op jit(solution)/shard_map/qhe,khe->hqk/dot_general | solution.py:43
  57.8 3.9 %collective-permute-done.1 = bf16[2,256,512]{2,1,0:T(8,128)(2,1)} collective-permute-done((bf16[2,256,512]{2,1,0:T(8,128)(2,1)}, bf16[2,256,512]{2,1,0:T(8,128)(2,1)}, u32[]{:S(2)}, u32[]{:S(2)}) %collective-permute-start.1) | collective-permute-done | bytes 524320 | tf_op jit(solution)/shard_map/ppermute | solution.py:15
  61.7 1.9 %collective-permute-start.2 = (bf16[2,256,512]{2,1,0:T(8,128)(2,1)}, bf16[2,256,512]{2,1,0:T(8,128)(2,1)}, u32[]{:S(2)}, u32[]{:S(2)}) collective-permute-start(bf16[2,256,512]{2,1,0:T(8,128)(2,1)} %collective-permute-done.1), channel_id=1, source_target_pairs={{0,2},{2,4},{4,6},{6,8},{8,10},{10,12},{12,14},{1,3},{3,5},{5,7},{... | collective-permute-start | bytes 1572872 | tf_op jit(solution)/shard_map/ppermute | solution.py:15
  63.6 1.9 %fusion.70 = (bf16[1,256,512]{2,1,0:T(8,128)(2,1)}, bf16[1,256,512]{2,1,0:T(8,128)(2,1)}) fusion(bf16[2,256,512]{2,1,0:T(8,128)(2,1)} %collective-permute-done.1), kind=kLoop, calls=%fused_computation.107 | loop fusion | bytes 1048576 | tf_op jit(solution)/shard_map/slice | solution.py:42
  65.5 1.8 %copy.50 = bf16[1,256,512]{1,2,0:T(8,128)(2,1)} copy(bf16[1,256,512]{2,1,0:T(8,128)(2,1)} %get-tuple-element.15) | data formatting | bytes 524288 | tf_op jit(solution)/shard_map/slice | solution.py:42
  67.3 1.8 %copy.49 = bf16[1,256,512]{1,2,0:T(8,128)(2,1)} copy(bf16[1,256,512]{2,1,0:T(8,128)(2,1)} %get-tuple-element.16) | data formatting | bytes 524288 | tf_op jit(solution)/shard_map/slice | solution.py:41
  69.1 2.8 %fusion.2 = (f32[8,256]{1,0:T(8,128)S(1)}, f32[8,256,256]{1,2,0:T(8,128)}) fusion(pred[]{:T(512)} %bitcast.31, bf16[256,8,64]{0,2,1:T(8,128)(2,1)S(1)} %bitcast.160, bf16[256,8,64]{0,2,1:T(8,128)(2,1)} %bitcast.167), kind=kOutput, calls=%fused_computation.13 | convolution fusion | flops 68679680 | bytes 2629633 | tf_op jit(solution)/shard_map/qhe,khe->hqk/dot_general | solution.py:43
  71.8 3.5 %collective-permute-done.2 = bf16[2,256,512]{2,1,0:T(8,128)(2,1)} collective-permute-done((bf16[2,256,512]{2,1,0:T(8,128)(2,1)}, bf16[2,256,512]{2,1,0:T(8,128)(2,1)}, u32[]{:S(2)}, u32[]{:S(2)}) %collective-permute-start.2) | collective-permute-done | bytes 524320 | tf_op jit(solution)/shard_map/ppermute | solution.py:15
  75.3 1.9 %fusion.69 = (bf16[1,256,512]{2,1,0:T(8,128)(2,1)}, bf16[1,256,512]{2,1,0:T(8,128)(2,1)}) fusion(bf16[2,256,512]{2,1,0:T(8,128)(2,1)} %collective-permute-done.2), kind=kLoop, calls=%fused_computation.106 | loop fusion | bytes 1048576 | tf_op jit(solution)/shard_map/slice | solution.py:42
  77.2 1.8 %copy.53 = bf16[1,256,512]{1,2,0:T(8,128)(2,1)} copy(bf16[1,256,512]{2,1,0:T(8,128)(2,1)} %get-tuple-element.13) | data formatting | bytes 524288 | tf_op jit(solution)/shard_map/slice | solution.py:42
  79.0 1.8 %copy.52 = bf16[1,256,512]{1,2,0:T(8,128)(2,1)} copy(bf16[1,256,512]{2,1,0:T(8,128)(2,1)} %get-tuple-element.14) | data formatting | bytes 524288 | tf_op jit(solution)/shard_map/slice | solution.py:41
  80.8 1.6 %fusion.3 = (f32[8,256]{1,0:T(8,128)S(1)}, f32[8,256,256]{1,2,0:T(8,128)S(1)}) fusion(pred[]{:T(512)} %bitcast.38, bf16[256,8,64]{0,2,1:T(8,128)(2,1)S(1)} %bitcast.161, bf16[256,8,64]{0,2,1:T(8,128)(2,1)} %bitcast.164), kind=kOutput, calls=%fused_computation.14 | convolution fusion | flops 68679680 | bytes 2629633 | tf_op jit(solution)/shard_map/qhe,khe->hqk/dot_general | solution.py:43
  (56 shorter events, 17.4 us)
Async XLA Ops:
  0.0 29.9 %copy-start = (bf16[1024,512]{1,0:T(8,128)(2,1)S(1)}, bf16[1024,512]{1,0:T(8,128)(2,1)}, u32[]{:S(2)}) copy-start(bf16[1024,512]{1,0:T(8,128)(2,1)} %param.13) | copy-start | bytes 3145732
  0.0 11.2 %copy-start.12 = (s32[8]{0:T(128)S(1)}, s32[8]{0:T(128)}, u32[]{:S(2)}) copy-start(s32[8]{0:T(128)} %param.19) | copy-start | bytes 100
  0.0 12.3 %copy-start.11 = (s32[8]{0:T(128)S(1)}, s32[8]{0:T(128)}, u32[]{:S(2)}) copy-start(s32[8]{0:T(128)} %param.18) | copy-start | bytes 100
  0.0 18.0 %copy-start.10 = (bf16[8,16,512]{2,1,0:T(8,128)(2,1)S(1)}, bf16[8,16,512]{2,1,0:T(8,128)(2,1)}, u32[]{:S(2)}) copy-start(bf16[8,16,512]{2,1,0:T(8,128)(2,1)} %param.15) | copy-start | bytes 393220
  0.0 25.3 %copy-start.5 = (bf16[256,512]{1,0:T(8,128)(2,1)S(1)}, bf16[256,512]{1,0:T(8,128)(2,1)}, u32[]{:S(2)}) copy-start(bf16[256,512]{1,0:T(8,128)(2,1)} %param.10) | copy-start | bytes 786436
  5.1 14.2 %all-to-all-start = ((bf16[1,8,128,128]{3,2,0,1:T(8,128)(2,1)}), bf16[1,8,128,128]{3,2,0,1:T(8,128)(2,1)S(1)}, u32[]{:S(2)}, u32[]{:S(2)}) async-start(bf16[1,8,128,128]{3,2,0,1:T(8,128)(2,1)} %bitcast_select_fusion), calls=%async_computation | async-start | bytes 524288 | tf_op jit(solution)/shard_map/all_to_all | solution.py:77
  19.3 10.1 %all-to-all-start.1 = ((bf16[1,8,16,512]{3,2,0,1:T(8,128)(2,1)}), bf16[1,8,16,512]{3,2,0,1:T(8,128)(2,1)S(1)}, u32[]{:S(2)}, u32[]{:S(2)}) async-start(bf16[1,8,16,512]{3,2,0,1:T(8,128)(2,1)} %bitcast_select_fusion.1), calls=%async_computation.1 | async-start | bytes 262144 | tf_op jit(solution)/shard_map/all_to_all | solution.py:78
  27.5 2.9 %copy-start.4 = (bf16[1024,512]{1,0:T(8,128)(2,1)S(1)}, bf16[1024,512]{1,0:T(8,128)(2,1)}, u32[]{:S(2)}) copy-start(bf16[1024,512]{1,0:T(8,128)(2,1)} %param.12) | copy-start | bytes 3145732
  30.3 4.3 %copy-start.3 = (bf16[1024,512]{1,0:T(8,128)(2,1)S(1)}, bf16[1024,512]{1,0:T(8,128)(2,1)}, u32[]{:S(2)}) copy-start(bf16[1024,512]{1,0:T(8,128)(2,1)} %param.11) | copy-start | bytes 3145732
  31.6 15.5 %collective-permute-start = (bf16[2,256,512]{2,1,0:T(8,128)(2,1)}, bf16[2,256,512]{2,1,0:T(8,128)(2,1)}, u32[]{:S(2)}, u32[]{:S(2)}) collective-permute-start(bf16[2,256,512]{2,1,0:T(8,128)(2,1)} %pad_maximum_fusion), channel_id=1, source_target_pairs={{0,2},{2,4},{4,6},{6,8},{8,10},{10,12},{12,14},{1,3},{3,5},{5,7},{... | collective-permute-start | bytes 1572872 | tf_op jit(solution)/shard_map/ppermute | solution.py:15
  47.1 14.6 %collective-permute-start.1 = (bf16[2,256,512]{2,1,0:T(8,128)(2,1)}, bf16[2,256,512]{2,1,0:T(8,128)(2,1)}, u32[]{:S(2)}, u32[]{:S(2)}) collective-permute-start(bf16[2,256,512]{2,1,0:T(8,128)(2,1)} %collective-permute-done), channel_id=1, source_target_pairs={{0,2},{2,4},{4,6},{6,8},{8,10},{10,12},{12,14},{1,3},{3,5},{5,7},{... | collective-permute-start | bytes 1572872 | tf_op jit(solution)/shard_map/ppermute | solution.py:15
  61.7 13.6 %collective-permute-start.2 = (bf16[2,256,512]{2,1,0:T(8,128)(2,1)}, bf16[2,256,512]{2,1,0:T(8,128)(2,1)}, u32[]{:S(2)}, u32[]{:S(2)}) collective-permute-start(bf16[2,256,512]{2,1,0:T(8,128)(2,1)} %collective-permute-done.1), channel_id=1, source_target_pairs={{0,2},{2,4},{4,6},{6,8},{8,10},{10,12},{12,14},{1,3},{3,5},{5,7},{... | collective-permute-start | bytes 1572872 | tf_op jit(solution)/shard_map/ppermute | solution.py:15
  80.8 1.7 %copy-start.2 = (f32[8,256,256]{1,2,0:T(8,128)S(1)}, f32[8,256,256]{1,2,0:T(8,128)}, u32[]{:S(2)}) copy-start(f32[8,256,256]{1,2,0:T(8,128)} %get-tuple-element.30) | copy-start | bytes 6291460
  82.4 1.6 %copy-start.1 = (f32[8,256,256]{1,2,0:T(8,128)S(1)}, f32[8,256,256]{1,2,0:T(8,128)}, u32[]{:S(2)}) copy-start(f32[8,256,256]{1,2,0:T(8,128)} %get-tuple-element.32) | copy-start | bytes 6291460
  84.0 1.1 %copy-start.6 = (bf16[256,512]{0,1:T(8,128)(2,1)S(1)}, bf16[256,512]{0,1:T(8,128)(2,1)}, u32[]{:S(2)}) copy-start(bf16[256,512]{0,1:T(8,128)(2,1)} %copy.44) | copy-start | bytes 786436
  85.1 1.0 %copy-start.7 = (bf16[1,256,512]{1,2,0:T(8,128)(2,1)S(1)}, bf16[1,256,512]{1,2,0:T(8,128)(2,1)}, u32[]{:S(2)}) copy-start(bf16[1,256,512]{1,2,0:T(8,128)(2,1)} %copy.47) | copy-start | bytes 786436
  85.7 1.0 %copy-start.8 = (bf16[1,256,512]{1,2,0:T(8,128)(2,1)S(1)}, bf16[1,256,512]{1,2,0:T(8,128)(2,1)}, u32[]{:S(2)}) copy-start(bf16[1,256,512]{1,2,0:T(8,128)(2,1)} %copy.50) | copy-start | bytes 786436
  86.6 1.0 %copy-start.9 = (bf16[1,256,512]{1,2,0:T(8,128)(2,1)S(1)}, bf16[1,256,512]{1,2,0:T(8,128)(2,1)}, u32[]{:S(2)}) copy-start(bf16[1,256,512]{1,2,0:T(8,128)(2,1)} %copy.53) | copy-start | bytes 786436
where the time goes:
time: 89.9 us; the launch traced here: 89 us
  local copies, waits for them, and re-layouts  25.1 us (28%)
  starting transfers between devices  19.4 us (22%)
  waiting for transfers between devices  17.7 us (20%)
  matrix products  12.9 us (14%)
  between operations  5.86 us (7%)
  other arithmetic  5.85 us (7%)
  blocking collectives  2.17 us (2%)
    ppermute x3, waiting for transfers between devices, from_behind(): return lax.ppermute(block, axis, route)  16.1 us
    slice x6, local copies, waits for them, and re-layouts, attend(): value_heads = pair[1].reshape(frames_dev, heads_dev, HD)  11 us
    dot_general x4, matrix products, attend(): jnp.einsum('qhe,khe->hqk', query_heads, key_heads, preferred_element_type...  8.55 us
    ppermute x3, starting transfers between devices, from_behind(): return lax.ppermute(block, axis, route)  7.39 us
    all_to_all x1, starting transfers between devices, body(): lax.all_to_all(down_send, 'seq', split_axis=1, concat_axis=2, tiled=True)  6.03 us
    all_to_all x1, starting transfers between devices, body(): lax.all_to_all(up_send, 'seq', split_axis=1, concat_axis=2, tiled=True)  6 us
    slice x3, local copies, waits for them, and re-layouts, attend(): key_heads = pair[0].reshape(frames_dev, heads_dev, HD)  5.36 us
    dot_general x4, matrix products, attend(): jnp.einsum('hqk,khe->hqe', weights.astype(jnp.bfloat16), value_heads, pre...  2.27 us
  transfers between devices with their start and end apart: 5, of which 4 were waited for; matrix products, arithmetic and copies ran while one was open for 26% of the time, Pallas kernels for 0%

commit v1 on v0

v1 whole, which is shorter than its diff:
```python
import functools

import jax
import jax.numpy as jnp
from jax import lax
from jax.experimental import pallas as pl
from jax.experimental.pallas import tpu as pltpu
from jax.sharding import PartitionSpec as P

HD = 64
LANES = 128
LOOK = 3
NEG_LARGE = -1e30
F32 = jnp.float32
BF16 = jnp.bfloat16

VMEM = functools.partial(pl.BlockSpec, memory_space=pltpu.VMEM)
SMEM = functools.partial(pl.BlockSpec, memory_space=pltpu.SMEM)
ANY = functools.partial(pl.BlockSpec, memory_space=pl.ANY)


def mm(a, b):
    return jnp.dot(a, b, preferred_element_type=F32)


def reach(seg_ref, look_ref, position):
    count = jnp.int32(0)
    for distance in range(1, LOOK + 1):
        earlier = jnp.maximum(position - distance, 0)
        allowed = (
            (position >= distance)
            & (look_ref[position] >= distance)
            & (seg_ref[earlier] == seg_ref[position])
        )
        count = count + allowed.astype(jnp.int32)
    return count


def pack_kernel(row_ref, lang_ref, down_ref, up_ref, out_ref, sems):
    head = lax.axis_index("head")
    count = out_ref.shape[0]
    half = down_ref.shape[1] // 2
    depth = up_ref.shape[1]
    chunks = up_ref.shape[2] // LANES

    def copies(j):
        row = row_ref[lang_ref[j]]
        yield pltpu.make_async_copy(
            down_ref.at[row, pl.ds(pl.multiple_of(head * half, half), half), :],
            out_ref.at[j, pl.ds(0, half), :],
            sems.at[j, 0],
        )
        for c in range(chunks):
            yield pltpu.make_async_copy(
                up_ref.at[row, :, pl.ds(c * LANES, LANES)],
                out_ref.at[j, pl.ds(half + c * depth, depth), :],
                sems.at[j, c + 1],
            )

    @pl.loop(0, count)
    def _(j):
        for copy in copies(j):
            copy.start()

    @pl.loop(0, count)
    def _(j):
        for copy in copies(j):
            copy.wait()


def pack(bank_row, lang_ids, down_bank, up_bank, count):
    rows = down_bank.shape[1] // 2 + up_bank.shape[1] * (up_bank.shape[2] // LANES)
    return pl.pallas_call(
        pack_kernel,
        out_shape=jax.ShapeDtypeStruct((count, rows, LANES), BF16),
        in_specs=[SMEM(), SMEM(), ANY(), ANY()],
        out_specs=ANY(),
        scratch_shapes=[pltpu.SemaphoreType.DMA((count, 1 + up_bank.shape[2] // LANES))],
    )(bank_row, lang_ids, down_bank, up_bank)


def keys_values(first, second, head, wk_ref, wv_ref, down_ref, up_ref):
    half = first.shape[1]
    mine = pl.ds(pl.multiple_of(head * half, half), half)
    other = pl.ds(pl.multiple_of((1 - head) * half, half), half)
    lowrank = mm(first, down_ref[mine, :]) + mm(second, down_ref[other, :])
    lowrank = lowrank.astype(BF16)
    lane = lax.broadcasted_iota(jnp.int32, lowrank.shape, 1)
    split = lowrank.shape[1] // 2
    zero = jnp.zeros_like(lowrank)
    low_key = jnp.where(lane < split, lowrank, zero)
    low_value = jnp.where(lane < split, zero, lowrank)
    up = up_ref[...]
    keys = mm(first, wk_ref[mine, :]) + mm(second, wk_ref[other, :]) + mm(low_key, up)
    values = mm(first, wv_ref[mine, :]) + mm(second, wv_ref[other, :]) + mm(low_value, up)
    return keys.astype(BF16), values.astype(BF16)


def attend(q_ref, keys, values, acc_ref, max_ref, opening):
    rows = q_ref.shape[0]
    heads = acc_ref.shape[0]
    lane = lax.broadcasted_iota(jnp.int32, (rows, LANES), 1)
    for i in range(heads):
        cols = slice(i // 2 * LANES, (i // 2 + 1) * LANES)
        inside = (lane < HD) if i % 2 == 0 else (lane >= HD)
        q = q_ref[:, cols]
        q = jnp.where(inside, q, jnp.zeros_like(q))
        scores = lax.dot_general(
            q, keys[:, cols], (((1,), (1,)), ((), ())), preferred_element_type=F32
        )
        v = values[:, cols]
        v = jnp.where(inside[: v.shape[0]], v, jnp.ones_like(v))
        top = jnp.max(scores, axis=1, keepdims=True)
        if not opening:
            before = max_ref[i][:, :1]
            top = jnp.maximum(top, before)
        weights = jnp.exp(scores - top).astype(BF16)
        update = mm(weights, v)
        if not opening:
            update = acc_ref[i] * jnp.exp(before - top) + update
        acc_ref[i] = update
        max_ref[i] = jnp.broadcast_to(top, (rows, LANES))


def finish(acc_ref, out_ref):
    rows = out_ref.shape[0]
    heads = acc_ref.shape[0]
    lane = lax.broadcasted_iota(jnp.int32, (rows, LANES), 1)
    for pair in range(heads // 2):
        even = acc_ref[2 * pair]
        odd = acc_ref[2 * pair + 1]
        total = jnp.where(lane < HD, odd, even)
        total = pltpu.roll(total, HD, 1)
        value = jnp.where(lane < HD, even, odd)
        out_ref[:, pair * LANES : (pair + 1) * LANES] = (value / total).astype(BF16)


def early_kernel(
    packed, seg_ref, look_ref, a0, b0, a1, b1, a2, b2, got, other, wq, wk, wv,
    q_ref, acc_ref, max_ref, down_ref, up_ref,
):
    head = lax.axis_index("head")
    position = lax.axis_index("seq")
    count = reach(seg_ref, look_ref, position)
    if packed:
        half = other.shape[1]
        depth = up_ref.shape[0] // got.shape[0]
        for j in range(got.shape[0]):
            base = j * 2 * half
            down_ref[pl.ds(pl.multiple_of(base + head * half, half), half), :] = got[j, :half, :]
            down_ref[pl.ds(pl.multiple_of(base + (1 - head) * half, half), half), :] = other[j]
        for c in range(up_ref.shape[1] // LANES):
            piece = got[:, half + c * depth : half + (c + 1) * depth, :]
            up_ref[:, c * LANES : (c + 1) * LANES] = piece.reshape(up_ref.shape[0], LANES)
    else:
        down_ref[...] = got[...]
        up_ref[...] = other[...]
    width = a0.shape[1]
    mine = pl.ds(pl.multiple_of(head * width, width), width)
    others = pl.ds(pl.multiple_of((1 - head) * width, width), width)
    queries = (mm(a0[...], wq[mine, :]) + mm(b0[...], wq[others, :])).astype(BF16)
    q_ref[...] = queries * jnp.asarray(HD**-0.5, BF16)
    for distance, (a, b) in enumerate(((a0, b0), (a1, b1), (a2, b2))):

        def visit(a=a, b=b, opening=distance == 0):
            keys, values = keys_values(a[...], b[...], head, wk, wv, down_ref, up_ref)
            attend(q_ref, keys, values, acc_ref, max_ref, opening)

        if distance:
            pl.when(count >= distance)(visit)
        else:
            visit()


def late_kernel(
    seg_ref, look_ref, a3, b3, q_ref, acc_in, max_in, down_ref, up_ref, wk, wv,
    out_ref, acc_ref, max_ref,
):
    head = lax.axis_index("head")
    position = lax.axis_index("seq")
    count = reach(seg_ref, look_ref, position)

    @pl.when(count >= LOOK)
    def _():
        acc_ref[...] = acc_in[...]
        max_ref[...] = max_in[...]
        keys, values = keys_values(a3[...], b3[...], head, wk, wv, down_ref, up_ref)
        attend(q_ref, keys, values, acc_ref, max_ref, False)
        finish(acc_ref, out_ref)

    @pl.when(count < LOOK)
    def _():
        finish(acc_in, out_ref)


def body(
    frames, w_query, w_key, w_value, down_bank, up_bank, bank_row, lang_ids, seg_ids, lookback
):
    count = lax.axis_size("seq")
    rows, width = frames.shape
    columns = w_query.shape[1]
    heads = columns // HD
    model_width = w_query.shape[0]
    rank_two = down_bank.shape[2]

    def shift(x, distance):
        return lax.ppermute(x, "seq", [(i, (i + distance) % count) for i in range(count)])

    def swap(x):
        return lax.ppermute(x, "head", [(0, 1), (1, 0)])

    a0 = frames
    a2 = shift(a0, 2)
    a1 = shift(a0, 1)
    a3 = shift(a2, 1)
    b0, b1, b2, b3 = swap(a0), swap(a1), swap(a2), swap(a3)

    packed = down_bank.shape[1] % 32 == 0 and up_bank.shape[1] % 16 == 0
    if packed:
        sent = pack(bank_row, lang_ids, down_bank, up_bank, count)
        got = lax.all_to_all(sent, "seq", split_axis=0, concat_axis=0, tiled=True)
        other = swap(got[:, : down_bank.shape[1] // 2, :])
    else:
        wanted = jnp.take(bank_row, lang_ids, axis=0)
        got = lax.all_to_all(
            jnp.take(down_bank, wanted, axis=0), "seq", split_axis=0, concat_axis=0, tiled=True
        ).reshape(model_width, rank_two)
        other = lax.all_to_all(
            jnp.take(up_bank, wanted, axis=0), "seq", split_axis=0, concat_axis=0, tiled=True
        ).reshape(rank_two, columns)

    state = jax.ShapeDtypeStruct((heads, rows, LANES), F32)
    q, acc, top, down, up = pl.pallas_call(
        functools.partial(early_kernel, packed),
        out_shape=(
            jax.ShapeDtypeStruct((rows, columns), BF16),
            state,
            state,
            jax.ShapeDtypeStruct((model_width, rank_two), BF16),
            jax.ShapeDtypeStruct((rank_two, columns), BF16),
        ),
        in_specs=[SMEM(), SMEM()] + [VMEM()] * 11,
        out_specs=(VMEM(),) * 5,
        compiler_params=pltpu.CompilerParams(vmem_limit_bytes=32 * 1024 * 1024),
    )(seg_ids, lookback, a0, b0, a1, b1, a2, b2, got, other, w_query, w_key, w_value)
    return pl.pallas_call(
        late_kernel,
        out_shape=jax.ShapeDtypeStruct((rows, columns), BF16),
        in_specs=[SMEM(), SMEM()] + [VMEM()] * 9,
        out_specs=VMEM(),
        scratch_shapes=[pltpu.VMEM(state.shape, F32)] * 2,
        compiler_params=pltpu.CompilerParams(vmem_limit_bytes=32 * 1024 * 1024),
    )(seg_ids, lookback, a3, b3, q, acc, top, down, up, w_key, w_value)


def solution(mesh):
    in_specs = (
        P(("parts", "seq"), "head"),
        P(None, "head"),
        P(None, "head"),
        P(None, "head"),
        P(None, "seq", None),
        P(None, "seq", "head"),
        P(),
        P("parts"),
        P("parts"),
        P("parts"),
    )
    out_specs = P(("parts", "seq"), "head")
    return jax.shard_map(body, mesh=mesh, in_specs=in_specs, out_specs=out_specs, check_vma=False)
```

time: 89.9 us -> 56.5 us (0.63)
  the two profiles are of different devices: /device:TPU:24 before, /device:TPU:23 now
where the time goes in v1:
time: 56.5 us; the launch traced here: 55.9 us
  Pallas kernels  28.2 us (50%)
  starting transfers between devices  15 us (27%)
  waiting for transfers between devices  10.2 us (18%)
  local copies, waits for them, and re-layouts  2.48 us (4%)
    pallas_call x1, Pallas kernels, body(): pl.pallas_call(functools.partial(early_kernel, packed), out_shape=(jax.Sh...  11.9 us
    pallas_call x1, Pallas kernels, pack(): pl.pallas_call(pack_kernel, out_shape=jax.ShapeDtypeStruct((count, rows,...  10.1 us
    ppermute x3, waiting for transfers between devices, shift(): lax.ppermute(x, 'seq', [(i, (i + distance) % count) for i in range(count)])  9.19 us
    ppermute x5, starting transfers between devices, swap(): return lax.ppermute(x, 'head', [(0, 1), (1, 0)])  6.64 us
    pallas_call x1, Pallas kernels, body(): pl.pallas_call(late_kernel, out_shape=jax.ShapeDtypeStruct((rows, columns...  6.2 us
    all_to_all x1, starting transfers between devices, body(): got = lax.all_to_all(sent, 'seq', split_axis=0, concat_axis=0, tiled=True)  4.68 us
    ppermute x3, starting transfers between devices, shift(): lax.ppermute(x, 'seq', [(i, (i + distance) % count) for i in range(count)])  3.66 us
    unnamed x14, local copies, waits for them, and re-layouts  2.47 us
  transfers between devices with their start and end apart: 9, of which 3 were waited for; matrix products, arithmetic and copies ran while one was open for 0% of the time, Pallas kernels for 39%

profile of v1, /device:TPU:23, one launch (start us, length us, event | category | flops | bytes accessed | tf_op | source)
XLA Modules:
  0.0 55.9 jit_solution(14651268424191741025)
XLA Ops:
  0.0 1.3 %collective-permute-start = (bf16[256,512]{1,0:T(8,128)(2,1)}, bf16[256,512]{1,0:T(8,128)(2,1)S(1)}, u32[]{:S(2)}, u32[]{:S(2)}) collective-permute-start(bf16[256,512]{1,0:T(8,128)(2,1)} %a0.1), channel_id=1, source_target_pairs={{0,4},{2,6},{4,8},{6,10},{8,12},{10,14},{12,0},{14,2},{1,5},{3,7},... | collective-permute-start | bytes 786440 | tf_op jit(solution)/shard_map/ppermute | solution.py:207
  1.3 10.1 %shard_map.100 = bf16[8,128,128]{2,1,0:T(8,128)(2,1)} custom-call(s32[8]{0:T(128)} %row_ref.1, s32[8]{0:T(128)} %lang_ref.1, bf16[8,128,128]{2,1,0:T(8,128)(2,1)} %down_ref.1, bf16[8,16,512]{2,1,0:T(8,128)(2,1)} %up_ref.1), custom_call_target="tpu_custom_call" | custom-call | tf_op jit(solution)/shard_map/pallas_call | solution.py:73
  11.4 0.0 copy-start.4
  11.4 4.7 %all-to-all-start = ((bf16[8,128,128]{2,1,0:T(8,128)(2,1)}), bf16[8,128,128]{2,1,0:T(8,128)(2,1)S(1)}, u32[]{:S(2)}, u32[]{:S(2)}) async-start(bf16[8,128,128]{2,1,0:T(8,128)(2,1)} %shard_map.100), calls=%async_computation | async-start | bytes 524288 | tf_op jit(solution)/shard_map/all_to_all | solution.py:221
  16.1 1.2 %collective-permute-start.4 = (bf16[256,512]{1,0:T(8,128)(2,1)}, bf16[256,512]{1,0:T(8,128)(2,1)S(1)}, u32[]{:S(2)}, u32[]{:S(2)}) collective-permute-start(bf16[256,512]{1,0:T(8,128)(2,1)} %a0.1), channel_id=1, source_target_pairs={{0,2},{2,4},{4,6},{6,8},{8,10},{10,12},{12,14},{14,0},{1,3},{3,5},... | collective-permute-start | bytes 786440 | tf_op jit(solution)/shard_map/ppermute | solution.py:207
  17.3 0.0 collective-permute-done.a2
  17.3 1.2 %collective-permute-start.1 = (bf16[256,512]{1,0:T(8,128)(2,1)S(1)}, bf16[256,512]{1,0:T(8,128)(2,1)S(1)}, u32[]{:S(2)}, u32[]{:S(2)}) collective-permute-start(bf16[256,512]{1,0:T(8,128)(2,1)S(1)} %collective-permute-done.a2), channel_id=1, source_target_pairs={{0,2},{2,4},{4,6},{6,8},{8,10},{10,12},{12,14},{14,0},{1,3},{3,5},... | collective-permute-start | bytes 786440 | tf_op jit(solution)/shard_map/ppermute | solution.py:207
  18.5 2.1 %collective-permute-start.3 = (bf16[256,512]{1,0:T(8,128)(2,1)}, bf16[256,512]{1,0:T(8,128)(2,1)S(1)}, u32[]{:S(2)}, u32[]{:S(2)}) collective-permute-start(bf16[256,512]{1,0:T(8,128)(2,1)} %a0.1), channel_id=1, source_target_pairs={{0,1},{1,0},{2,3},{3,2},{4,5},{5,4},{6,7},{7,6},{8,9},{9,8},{10,11... | collective-permute-start | bytes 786440 | tf_op jit(solution)/shard_map/ppermute | solution.py:210
  20.5 0.0 collective-permute-start.6
  20.5 5.5 %collective-permute-done.4.a1 = bf16[256,512]{1,0:T(8,128)(2,1)S(1)} collective-permute-done((bf16[256,512]{1,0:T(8,128)(2,1)}, bf16[256,512]{1,0:T(8,128)(2,1)S(1)}, u32[]{:S(2)}, u32[]{:S(2)}) %collective-permute-start.4) | collective-permute-done | bytes 262176 | tf_op jit(solution)/shard_map/ppermute | solution.py:207
  26.0 1.8 %collective-permute-start.5 = (bf16[256,512]{1,0:T(8,128)(2,1)S(1)}, bf16[256,512]{1,0:T(8,128)(2,1)S(1)}, u32[]{:S(2)}, u32[]{:S(2)}) collective-permute-start(bf16[256,512]{1,0:T(8,128)(2,1)S(1)} %collective-permute-done.4.a1), channel_id=1, source_target_pairs={{0,1},{1,0},{2,3},{3,2},{4,5},{5,4},{6,7},{7,6},{8,9},{9,8},{10,11... | collective-permute-start | bytes 786440 | tf_op jit(solution)/shard_map/ppermute | solution.py:210
  27.8 3.7 %collective-permute-done.1.a3 = bf16[256,512]{1,0:T(8,128)(2,1)S(1)} collective-permute-done((bf16[256,512]{1,0:T(8,128)(2,1)S(1)}, bf16[256,512]{1,0:T(8,128)(2,1)S(1)}, u32[]{:S(2)}, u32[]{:S(2)}) %collective-permute-start.1) | collective-permute-done | bytes 262176 | tf_op jit(solution)/shard_map/ppermute | solution.py:207
  31.5 1.1 %collective-permute-start.2 = (bf16[256,512]{1,0:T(8,128)(2,1)S(1)}, bf16[256,512]{1,0:T(8,128)(2,1)S(1)}, u32[]{:S(2)}, u32[]{:S(2)}) collective-permute-start(bf16[256,512]{1,0:T(8,128)(2,1)S(1)} %collective-permute-done.1.a3), channel_id=1, source_target_pairs={{0,1},{1,0},{2,3},{3,2},{4,5},{5,4},{6,7},{7,6},{8,9},{9,8},{10,11... | collective-permute-start | bytes 786440 | tf_op jit(solution)/shard_map/ppermute | solution.py:210
  32.7 1.6 %collective-permute-start.7 = (bf16[8,64,128]{2,1,0:T(8,128)(2,1)S(1)}, bf16[8,64,128]{2,1,0:T(8,128)(2,1)S(1)}, u32[]{:S(2)}, u32[]{:S(2)}) collective-permute-start(bf16[8,64,128]{2,1,0:T(8,128)(2,1)S(1)} %slice.4), channel_id=1, source_target_pairs={{0,1},{1,0},{2,3},{3,2},{4,5},{5,4},{6,7},{7,6},{8,9},{9,8},{10,11... | collective-permute-start | bytes 393224 | tf_op jit(solution)/shard_map/ppermute | solution.py:210
  34.3 0.0 collective-permute-done.3.b0
  34.3 0.0 collective-permute-done.6.b2
  34.3 0.0 collective-permute-done.5.b1
  34.3 1.0 %collective-permute-done.7.other = bf16[8,64,128]{2,1,0:T(8,128)(2,1)S(1)} collective-permute-done((bf16[8,64,128]{2,1,0:T(8,128)(2,1)S(1)}, bf16[8,64,128]{2,1,0:T(8,128)(2,1)S(1)}, u32[]{:S(2)}, u32[]{:S(2)}) %collective-permute-start.7) | collective-permute-done | bytes 131104 | tf_op jit(solution)/shard_map/ppermute | solution.py:210
  35.3 0.0 copy-start.1
  35.3 1.2 %copy-done.1 = bf16[1024,512]{1,0:T(8,128)(2,1)S(1)} copy-done((bf16[1024,512]{1,0:T(8,128)(2,1)S(1)}, bf16[1024,512]{1,0:T(8,128)(2,1)}, u32[]{:S(2)}) %copy-start.1) | copy-done | bytes 1048600
  36.5 1.2 %copy-done.3 = bf16[1024,512]{1,0:T(8,128)(2,1)S(1)} copy-done((bf16[1024,512]{1,0:T(8,128)(2,1)S(1)}, bf16[1024,512]{1,0:T(8,128)(2,1)}, u32[]{:S(2)}) %copy-start.3) | copy-done | bytes 1048600
  37.8 11.9 %shard_map.101 = (bf16[256,512]{1,0:T(8,128)(2,1)S(1)}, f32[8,256,128]{2,1,0:T(8,128)S(1)}, f32[8,256,128]{2,1,0:T(8,128)S(1)}, bf16[1024,128]{1,0:T(8,128)(2,1)S(1)}, bf16[128,512]{1,0:T(8,128)(2,1)S(1)}) custom-call(s32[8]{0:T(128)S(1)} %copy-done.5, s32[8]{0:T(128)S(1)} %copy-done.6, bf16[256,512]{1,0:T(8,128)(2,1)S(1)} %copy-done.4, ...), custom_call_target="tpu_custom_call" | custom-call | tf_op jit(solution)/shard_map/pallas_call | solution.py:233
  49.7 0.0 copy-done.2
  49.7 6.2 %shard_map.102 = bf16[256,512]{1,0:T(8,128)(2,1)} custom-call(s32[8]{0:T(128)S(1)} %copy-done.5, s32[8]{0:T(128)S(1)} %copy-done.6, bf16[256,512]{1,0:T(8,128)(2,1)S(1)} %collective-permute-done.1.a3, bf16[256,512]{1,0:T(8,128)(2,1)S(1)} %collective-permute-done.2.b3, bf16[256,512]{1,0:T(8,128)(2,1)S(1)} %get-tuple-element.10.q_ref, ...), custom_call_target="tpu_custom_call" | custom-call | tf_op jit(solution)/shard_map/pallas_call | solution.py:246
  (12 shorter events, 0.0 us)
Async XLA Ops:
  0.0 35.3 %copy-start = (bf16[1024,512]{1,0:T(8,128)(2,1)S(1)}, bf16[1024,512]{1,0:T(8,128)(2,1)}, u32[]{:S(2)}) copy-start(bf16[1024,512]{1,0:T(8,128)(2,1)} %wk.3) | copy-start | bytes 3145732
  0.0 17.3 %collective-permute-start = (bf16[256,512]{1,0:T(8,128)(2,1)}, bf16[256,512]{1,0:T(8,128)(2,1)S(1)}, u32[]{:S(2)}, u32[]{:S(2)}) collective-permute-start(bf16[256,512]{1,0:T(8,128)(2,1)} %a0.1), channel_id=1, source_target_pairs={{0,4},{2,6},{4,8},{6,10},{8,12},{10,14},{12,0},{14,2},{1,5},{3,7},... | collective-permute-start | bytes 786440 | tf_op jit(solution)/shard_map/ppermute | solution.py:207
  11.4 23.9 %copy-start.4 = (bf16[256,512]{1,0:T(8,128)(2,1)S(1)}, bf16[256,512]{1,0:T(8,128)(2,1)}, u32[]{:S(2)}) copy-start(bf16[256,512]{1,0:T(8,128)(2,1)} %a0.1) | copy-start | bytes 786436
  11.4 21.2 %all-to-all-start = ((bf16[8,128,128]{2,1,0:T(8,128)(2,1)}), bf16[8,128,128]{2,1,0:T(8,128)(2,1)S(1)}, u32[]{:S(2)}, u32[]{:S(2)}) async-start(bf16[8,128,128]{2,1,0:T(8,128)(2,1)} %shard_map.100), calls=%async_computation | async-start | bytes 524288 | tf_op jit(solution)/shard_map/all_to_all | solution.py:221
  16.1 19.2 %copy-start.5 = (s32[8]{0:T(128)S(1)}, s32[8]{0:T(128)}, u32[]{:S(2)}) copy-start(s32[8]{0:T(128)} %seg_ref.3) | copy-start | bytes 100
  16.1 19.2 %copy-start.6 = (s32[8]{0:T(128)S(1)}, s32[8]{0:T(128)}, u32[]{:S(2)}) copy-start(s32[8]{0:T(128)} %look_ref.3) | copy-start | bytes 100
  16.1 9.9 %collective-permute-start.4 = (bf16[256,512]{1,0:T(8,128)(2,1)}, bf16[256,512]{1,0:T(8,128)(2,1)S(1)}, u32[]{:S(2)}, u32[]{:S(2)}) collective-permute-start(bf16[256,512]{1,0:T(8,128)(2,1)} %a0.1), channel_id=1, source_target_pairs={{0,2},{2,4},{4,6},{6,8},{8,10},{10,12},{12,14},{14,0},{1,3},{3,5},... | collective-permute-start | bytes 786440 | tf_op jit(solution)/shard_map/ppermute | solution.py:207
  17.3 14.3 %collective-permute-start.1 = (bf16[256,512]{1,0:T(8,128)(2,1)S(1)}, bf16[256,512]{1,0:T(8,128)(2,1)S(1)}, u32[]{:S(2)}, u32[]{:S(2)}) collective-permute-start(bf16[256,512]{1,0:T(8,128)(2,1)S(1)} %collective-permute-done.a2), channel_id=1, source_target_pairs={{0,2},{2,4},{4,6},{6,8},{8,10},{10,12},{12,14},{14,0},{1,3},{3,5},... | collective-permute-start | bytes 786440 | tf_op jit(solution)/shard_map/ppermute | solution.py:207
  18.5 15.8 %collective-permute-start.3 = (bf16[256,512]{1,0:T(8,128)(2,1)}, bf16[256,512]{1,0:T(8,128)(2,1)S(1)}, u32[]{:S(2)}, u32[]{:S(2)}) collective-permute-start(bf16[256,512]{1,0:T(8,128)(2,1)} %a0.1), channel_id=1, source_target_pairs={{0,1},{1,0},{2,3},{3,2},{4,5},{5,4},{6,7},{7,6},{8,9},{9,8},{10,11... | collective-permute-start | bytes 786440 | tf_op jit(solution)/shard_map/ppermute | solution.py:210
  20.5 13.8 %collective-permute-start.6 = (bf16[256,512]{1,0:T(8,128)(2,1)S(1)}, bf16[256,512]{1,0:T(8,128)(2,1)S(1)}, u32[]{:S(2)}, u32[]{:S(2)}) collective-permute-start(bf16[256,512]{1,0:T(8,128)(2,1)S(1)} %collective-permute-done.a2), channel_id=1, source_target_pairs={{0,1},{1,0},{2,3},{3,2},{4,5},{5,4},{6,7},{7,6},{8,9},{9,8},{10,11... | collective-permute-start | bytes 786440 | tf_op jit(solution)/shard_map/ppermute | solution.py:210
  26.0 8.3 %collective-permute-start.5 = (bf16[256,512]{1,0:T(8,128)(2,1)S(1)}, bf16[256,512]{1,0:T(8,128)(2,1)S(1)}, u32[]{:S(2)}, u32[]{:S(2)}) collective-permute-start(bf16[256,512]{1,0:T(8,128)(2,1)S(1)} %collective-permute-done.4.a1), channel_id=1, source_target_pairs={{0,1},{1,0},{2,3},{3,2},{4,5},{5,4},{6,7},{7,6},{8,9},{9,8},{10,11... | collective-permute-start | bytes 786440 | tf_op jit(solution)/shard_map/ppermute | solution.py:210
  31.5 18.1 %collective-permute-start.2 = (bf16[256,512]{1,0:T(8,128)(2,1)S(1)}, bf16[256,512]{1,0:T(8,128)(2,1)S(1)}, u32[]{:S(2)}, u32[]{:S(2)}) collective-permute-start(bf16[256,512]{1,0:T(8,128)(2,1)S(1)} %collective-permute-done.1.a3), channel_id=1, source_target_pairs={{0,1},{1,0},{2,3},{3,2},{4,5},{5,4},{6,7},{7,6},{8,9},{9,8},{10,11... | collective-permute-start | bytes 786440 | tf_op jit(solution)/shard_map/ppermute | solution.py:210
  32.7 2.6 %collective-permute-start.7 = (bf16[8,64,128]{2,1,0:T(8,128)(2,1)S(1)}, bf16[8,64,128]{2,1,0:T(8,128)(2,1)S(1)}, u32[]{:S(2)}, u32[]{:S(2)}) collective-permute-start(bf16[8,64,128]{2,1,0:T(8,128)(2,1)S(1)} %slice.4), channel_id=1, source_target_pairs={{0,1},{1,0},{2,3},{3,2},{4,5},{5,4},{6,7},{7,6},{8,9},{9,8},{10,11... | collective-permute-start | bytes 393224 | tf_op jit(solution)/shard_map/ppermute | solution.py:210
  35.3 1.2 %copy-start.1 = (bf16[1024,512]{1,0:T(8,128)(2,1)S(1)}, bf16[1024,512]{1,0:T(8,128)(2,1)}, u32[]{:S(2)}) copy-start(bf16[1024,512]{1,0:T(8,128)(2,1)} %wv.3) | copy-start | bytes 3145732
  36.5 1.2 %copy-start.3 = (bf16[1024,512]{1,0:T(8,128)(2,1)S(1)}, bf16[1024,512]{1,0:T(8,128)(2,1)}, u32[]{:S(2)}) copy-start(bf16[1024,512]{1,0:T(8,128)(2,1)} %wq.1) | copy-start | bytes 3145732
  37.8 11.9 %copy-start.2 = (bf16[1024,512]{1,0:T(8,128)(2,1)S(1)}, bf16[1024,512]{1,0:T(8,128)(2,1)}, u32[]{:S(2)}) copy-start(bf16[1024,512]{1,0:T(8,128)(2,1)} %wv.3) | copy-start | bytes 3145732

commit v2 on v1

v2 whole, which is shorter than its diff:
```python
import functools

import jax
import jax.numpy as jnp
from jax import lax
from jax.experimental import pallas as pl
from jax.experimental.pallas import tpu as pltpu
from jax.sharding import PartitionSpec as P

HD = 64
LANES = 128
LOOK = 3
VMEM_BYTES = 8 * 1024 * 1024
F32 = jnp.float32
BF16 = jnp.bfloat16

VMEM = functools.partial(pl.BlockSpec, memory_space=pltpu.VMEM)
SMEM = functools.partial(pl.BlockSpec, memory_space=pltpu.SMEM)


def mm(a, b):
    return jnp.dot(a, b, preferred_element_type=F32)


def reach(seg_ref, look_ref, position):
    count = jnp.int32(0)
    for distance in range(1, LOOK + 1):
        earlier = jnp.maximum(position - distance, 0)
        allowed = (
            (position >= distance)
            & (look_ref[position] >= distance)
            & (seg_ref[earlier] == seg_ref[position])
        )
        count = count + allowed.astype(jnp.int32)
    return count


def pack_kernel(row_ref, lang_ref, down_ref, up_ref, out_ref):
    head = lax.axis_index("head")
    half = down_ref.shape[1] // 2
    depth = up_ref.shape[1]
    mine = pl.ds(pl.multiple_of(head * half, half), half)
    for j in range(out_ref.shape[0]):
        row = row_ref[lang_ref[j]]
        out_ref[j, :half, :] = down_ref[row, mine, :]
        for c in range(up_ref.shape[2] // LANES):
            out_ref[j, half + c * depth : half + (c + 1) * depth, :] = up_ref[
                row, :, c * LANES : (c + 1) * LANES
            ]


def pack(bank_row, lang_ids, down_bank, up_bank, count):
    rows = down_bank.shape[1] // 2 + up_bank.shape[1] * (up_bank.shape[2] // LANES)
    return pl.pallas_call(
        pack_kernel,
        out_shape=jax.ShapeDtypeStruct((count, rows, LANES), BF16),
        in_specs=[SMEM(), SMEM(), VMEM(), VMEM()],
        out_specs=VMEM(),
        compiler_params=pltpu.CompilerParams(vmem_limit_bytes=VMEM_BYTES),
    )(bank_row, lang_ids, down_bank, up_bank)


def halves(head, width):
    mine = pl.ds(pl.multiple_of(head * width, width), width)
    other = pl.ds(pl.multiple_of((1 - head) * width, width), width)
    return mine, other


def query_kernel(a, b, wq, q_ref):
    mine, other = halves(lax.axis_index("head"), a.shape[1])
    queries = (mm(a[...], wq[mine, :]) + mm(b[...], wq[other, :])).astype(BF16)
    q_ref[...] = (queries * jnp.asarray(HD**-0.5, BF16)).T


def unpack(got, other, down_ref, up_ref):
    head = lax.axis_index("head")
    half = other.shape[1]
    depth = up_ref.shape[0] // got.shape[0]
    for j in range(got.shape[0]):
        for part, source in ((head, got), (1 - head, other)):
            place = pl.ds(pl.multiple_of(j * 2 * half + part * half, half), half)
            down_ref[place, :] = source[j, :half, :]
    for c in range(up_ref.shape[1] // LANES):
        piece = got[:, half + c * depth : half + (c + 1) * depth, :]
        up_ref[:, c * LANES : (c + 1) * LANES] = piece.reshape(up_ref.shape[0], LANES)


def keys_values(a, b, wk, wv, down_ref, up_ref):
    mine, other = halves(lax.axis_index("head"), a.shape[1])
    first, second = a[...], b[...]
    lowrank = mm(first, down_ref[mine, :]) + mm(second, down_ref[other, :])
    lowrank = lowrank.astype(BF16)
    lane = lax.broadcasted_iota(jnp.int32, lowrank.shape, 1)
    split = lowrank.shape[1] // 2
    zero = jnp.zeros_like(lowrank)
    low_key = jnp.where(lane < split, lowrank, zero)
    low_value = jnp.where(lane < split, zero, lowrank)
    up = up_ref[...]
    keys = mm(first, wk[mine, :]) + mm(second, wk[other, :]) + mm(low_key, up)
    values = mm(first, wv[mine, :]) + mm(second, wv[other, :]) + mm(low_value, up)
    return keys.astype(BF16), values.astype(BF16)


def attend(q_ref, keys, values, before, after):
    turned = values.T
    ones = jnp.ones((16, turned.shape[1]), BF16)
    acc_ref, max_ref = after
    for i in range(acc_ref.shape[0]):
        rows = slice(i * HD, (i + 1) * HD)
        q = q_ref[rows, :]
        zero = jnp.zeros_like(q)
        q = jnp.concatenate([q, zero] if i % 2 == 0 else [zero, q], axis=0)
        scores = mm(keys[:, i // 2 * LANES : (i // 2 + 1) * LANES], q)
        top = jnp.max(scores, axis=0, keepdims=True)
        if before is not None:
            old = before[1][i : i + 1, :]
            top = jnp.maximum(top, old)
        weights = jnp.exp(scores - top).astype(BF16)
        update = mm(jnp.concatenate([turned[rows, :], ones], axis=0), weights)
        update = update[: acc_ref.shape[1], :]
        if before is not None:
            update = before[0][i] * jnp.exp(old - top) + update
        acc_ref[i] = update
        max_ref[i : i + 1, :] = top


def finish(acc_ref, out_ref):
    for pair in range(acc_ref.shape[0] // 2):
        parts = []
        for i in (2 * pair, 2 * pair + 1):
            parts.append(acc_ref[i, :HD, :] / acc_ref[i, HD : HD + 1, :])
        out_ref[:, pair * LANES : (pair + 1) * LANES] = (
            jnp.concatenate(parts, axis=0).T.astype(BF16)
        )


def opening_kernel(packed, got, other, a, b, q_ref, wk, wv, acc_ref, max_ref, down_ref, up_ref):
    if packed:
        unpack(got, other, down_ref, up_ref)
    else:
        down_ref[...] = got[...]
        up_ref[...] = other[...]
    keys, values = keys_values(a, b, wk, wv, down_ref, up_ref)
    attend(q_ref, keys, values, None, (acc_ref, max_ref))


def block_kernel(
    distance, closing, seg_ref, look_ref, a, b, q_ref, wk, wv, down_ref, up_ref, acc_in, max_in, *outs
):
    count = reach(seg_ref, look_ref, lax.axis_index("seq"))
    if closing:
        out_ref, acc_ref, max_ref = outs
    else:
        acc_ref, max_ref = outs

    @pl.when(count >= distance)
    def _():
        keys, values = keys_values(a, b, wk, wv, down_ref, up_ref)
        attend(q_ref, keys, values, (acc_in, max_in), (acc_ref, max_ref))
        if closing:
            finish(acc_ref, out_ref)

    @pl.when(count < distance)
    def _():
        if closing:
            finish(acc_in, out_ref)
        else:
            acc_ref[...] = acc_in[...]
            max_ref[...] = max_in[...]


def body(
    frames, w_query, w_key, w_value, down_bank, up_bank, bank_row, lang_ids, seg_ids, lookback
):
    count = lax.axis_size("seq")
    rows, width = frames.shape
    columns = w_query.shape[1]
    heads = columns // HD
    model_width = w_query.shape[0]
    rank_two = down_bank.shape[2]
    params = pltpu.CompilerParams(vmem_limit_bytes=VMEM_BYTES)

    def shift(x, distance):
        return lax.ppermute(x, "seq", [(i, (i + distance) % count) for i in range(count)])

    def swap(x):
        return lax.ppermute(x, "head", [(0, 1), (1, 0)])

    a0 = frames
    a2 = shift(a0, 2)
    a1 = shift(a0, 1)
    a3 = shift(a2, 1)
    b0, b1, b2, b3 = swap(a0), swap(a1), swap(a2), swap(a3)

    packed = down_bank.shape[1] % 32 == 0 and up_bank.shape[1] % 16 == 0
    if packed:
        sent = pack(bank_row, lang_ids, down_bank, up_bank, count)
        got = lax.all_to_all(sent, "seq", split_axis=0, concat_axis=0, tiled=True)
        other = swap(got[:, : down_bank.shape[1] // 2, :])
    else:
        wanted = jnp.take(bank_row, lang_ids, axis=0)
        got = lax.all_to_all(
            jnp.take(down_bank, wanted, axis=0), "seq", split_axis=0, concat_axis=0, tiled=True
        ).reshape(model_width, rank_two)
        other = lax.all_to_all(
            jnp.take(up_bank, wanted, axis=0), "seq", split_axis=0, concat_axis=0, tiled=True
        ).reshape(rank_two, columns)

    q = pl.pallas_call(
        query_kernel,
        out_shape=jax.ShapeDtypeStruct((columns, rows), BF16),
        in_specs=[VMEM()] * 3,
        out_specs=VMEM(),
        compiler_params=params,
    )(a0, b0, w_query)
    state = (
        jax.ShapeDtypeStruct((heads, HD + 8, rows), F32),
        jax.ShapeDtypeStruct((heads, rows), F32),
    )
    acc, top, down, up = pl.pallas_call(
        functools.partial(opening_kernel, packed),
        out_shape=state
        + (
            jax.ShapeDtypeStruct((model_width, rank_two), BF16),
            jax.ShapeDtypeStruct((rank_two, columns), BF16),
        ),
        in_specs=[VMEM()] * 7,
        out_specs=(VMEM(),) * 4,
        compiler_params=params,
    )(got, other, a0, b0, q, w_key, w_value)
    for distance, a, b in ((2, a2, b2), (1, a1, b1), (3, a3, b3)):
        closing = distance == LOOK
        result = pl.pallas_call(
            functools.partial(block_kernel, distance, closing),
            out_shape=jax.ShapeDtypeStruct((rows, columns), BF16) if closing else state,
            in_specs=[SMEM(), SMEM()] + [VMEM()] * 9,
            out_specs=VMEM() if closing else (VMEM(), VMEM()),
            scratch_shapes=[pltpu.VMEM(s.shape, F32) for s in state] if closing else [],
            compiler_params=params,
        )(seg_ids, lookback, a, b, q, w_key, w_value, down, up, acc, top)
        if not closing:
            acc, top = result
    return result


def solution(mesh):
    in_specs = (
        P(("parts", "seq"), "head"),
        P(None, "head"),
        P(None, "head"),
        P(None, "head"),
        P(None, "seq", None),
        P(None, "seq", "head"),
        P(),
        P("parts"),
        P("parts"),
        P("parts"),
    )
    out_specs = P(("parts", "seq"), "head")
    return jax.shard_map(body, mesh=mesh, in_specs=in_specs, out_specs=out_specs, check_vma=False)
```

time: 56.5 us -> 47.4 us (0.84)
  the two profiles are of different devices: /device:TPU:23 before, /device:TPU:11 now
where the time goes in v2:
time: 47.4 us; the launch traced here: 47.3 us
  Pallas kernels  17.9 us (38%)
  starting transfers between devices  13.6 us (29%)
  waiting for transfers between devices  10.6 us (22%)
  local copies, waits for them, and re-layouts  5.06 us (11%)
    pallas_call x3, Pallas kernels, body(): pl.pallas_call(functools.partial(block_kernel, distance, closing), out_sh...  13 us
    ppermute x3, waiting for transfers between devices, shift(): lax.ppermute(x, 'seq', [(i, (i + distance) % count) for i in range(count)])  10.6 us
    ppermute x5, starting transfers between devices, swap(): return lax.ppermute(x, 'head', [(0, 1), (1, 0)])  5.07 us
    unnamed x20, local copies, waits for them, and re-layouts  5.05 us
    all_to_all x1, starting transfers between devices, body(): got = lax.all_to_all(sent, 'seq', split_axis=0, concat_axis=0, tiled=True)  4.78 us
    ppermute x3, starting transfers between devices, shift(): lax.ppermute(x, 'seq', [(i, (i + distance) % count) for i in range(count)])  3.72 us
    pallas_call x1, Pallas kernels, body(): pl.pallas_call(functools.partial(opening_kernel, packed), out_shape=state...  3.07 us
    pallas_call x1, Pallas kernels, pack(): pl.pallas_call(pack_kernel, out_shape=jax.ShapeDtypeStruct((count, rows,...  1.28 us
  transfers between devices with their start and end apart: 9, of which 2 were waited for; matrix products, arithmetic and copies ran while one was open for 0% of the time, Pallas kernels for 28%

profile of v2, /device:TPU:11, one launch (start us, length us, event | category | flops | bytes accessed | tf_op | source)
XLA Modules:
  0.0 47.3 jit_solution(9803756443866220238)
XLA Ops:
  0.0 1.3 %collective-permute-start = (bf16[256,512]{1,0:T(8,128)(2,1)}, bf16[256,512]{1,0:T(8,128)(2,1)}, u32[]{:S(2)}, u32[]{:S(2)}) collective-permute-start(bf16[256,512]{1,0:T(8,128)(2,1)} %a.3), channel_id=1, source_target_pairs={{0,4},{2,6},{4,8},{6,10},{8,12},{10,14},{12,0},{14,2},{1,5},{3,7},... | collective-permute-start | bytes 786440 | tf_op jit(solution)/shard_map/ppermute | solution.py:184
  1.3 0.9 %copy-done.4 = bf16[8,128,128]{2,1,0:T(8,128)(2,1)S(1)} copy-done((bf16[8,128,128]{2,1,0:T(8,128)(2,1)S(1)}, bf16[8,128,128]{2,1,0:T(8,128)(2,1)}, u32[]{:S(2)}) %copy-start.4) | copy-done | bytes 262168
  2.2 0.9 %copy-done.5 = bf16[8,16,512]{2,1,0:T(8,128)(2,1)S(1)} copy-done((bf16[8,16,512]{2,1,0:T(8,128)(2,1)S(1)}, bf16[8,16,512]{2,1,0:T(8,128)(2,1)}, u32[]{:S(2)}) %copy-start.5) | copy-done | bytes 131096
  3.2 0.7 %copy-done.8 = s32[8]{0:T(128)S(1)} copy-done((s32[8]{0:T(128)S(1)}, s32[8]{0:T(128)}, u32[]{:S(2)}) %copy-start.8) | copy-done | bytes 56
  3.8 0.7 %copy-done.9 = s32[8]{0:T(128)S(1)} copy-done((s32[8]{0:T(128)S(1)}, s32[8]{0:T(128)}, u32[]{:S(2)}) %copy-start.9) | copy-done | bytes 56
  4.5 1.3 %shard_map.101 = bf16[8,128,128]{2,1,0:T(8,128)(2,1)} custom-call(s32[8]{0:T(128)S(1)} %copy-done.8, s32[8]{0:T(128)S(1)} %copy-done.9, bf16[8,128,128]{2,1,0:T(8,128)(2,1)S(1)} %copy-done.4, bf16[8,16,512]{2,1,0:T(8,128)(2,1)S(1)} %copy-done.5), custom_call_target="tpu_custom_call" | custom-call | tf_op jit(solution)/shard_map/pallas_call | solution.py:54
  5.8 4.8 %all-to-all-start = ((bf16[8,128,128]{2,1,0:T(8,128)(2,1)}), bf16[8,128,128]{2,1,0:T(8,128)(2,1)S(1)}, u32[]{:S(2)}, u32[]{:S(2)}) async-start(bf16[8,128,128]{2,1,0:T(8,128)(2,1)} %shard_map.101), calls=%async_computation | async-start | bytes 524288 | tf_op jit(solution)/shard_map/all_to_all | solution.py:198
  10.5 1.2 %collective-permute-start.5 = (bf16[256,512]{1,0:T(8,128)(2,1)S(1)}, bf16[256,512]{1,0:T(8,128)(2,1)S(1)}, u32[]{:S(2)}, u32[]{:S(2)}) collective-permute-start(bf16[256,512]{1,0:T(8,128)(2,1)S(1)} %copy-done.2), channel_id=1, source_target_pairs={{0,2},{2,4},{4,6},{6,8},{8,10},{10,12},{12,14},{14,0},{1,3},{3,5},... | collective-permute-start | bytes 786440 | tf_op jit(solution)/shard_map/ppermute | solution.py:184
  11.8 1.2 %collective-permute-start.1 = (bf16[256,512]{1,0:T(8,128)(2,1)}, bf16[256,512]{1,0:T(8,128)(2,1)S(1)}, u32[]{:S(2)}, u32[]{:S(2)}) collective-permute-start(bf16[256,512]{1,0:T(8,128)(2,1)} %collective-permute-done.a), channel_id=1, source_target_pairs={{0,2},{2,4},{4,6},{6,8},{8,10},{10,12},{12,14},{14,0},{1,3},{3,5},... | collective-permute-start | bytes 786440 | tf_op jit(solution)/shard_map/ppermute | solution.py:184
  13.0 2.1 %collective-permute-start.3 = (bf16[256,512]{1,0:T(8,128)(2,1)S(1)}, bf16[256,512]{1,0:T(8,128)(2,1)S(1)}, u32[]{:S(2)}, u32[]{:S(2)}) collective-permute-start(bf16[256,512]{1,0:T(8,128)(2,1)S(1)} %copy-done.2), channel_id=1, source_target_pairs={{0,1},{1,0},{2,3},{3,2},{4,5},{5,4},{6,7},{7,6},{8,9},{9,8},{10,11... | collective-permute-start | bytes 786440 | tf_op jit(solution)/shard_map/ppermute | solution.py:187
  15.0 6.7 %collective-permute-done.5.a = bf16[256,512]{1,0:T(8,128)(2,1)S(1)} collective-permute-done((bf16[256,512]{1,0:T(8,128)(2,1)S(1)}, bf16[256,512]{1,0:T(8,128)(2,1)S(1)}, u32[]{:S(2)}, u32[]{:S(2)}) %collective-permute-start.5) | collective-permute-done | bytes 262176 | tf_op jit(solution)/shard_map/ppermute | solution.py:184
  21.8 1.8 %collective-permute-start.6 = (bf16[256,512]{1,0:T(8,128)(2,1)S(1)}, bf16[256,512]{1,0:T(8,128)(2,1)}, u32[]{:S(2)}, u32[]{:S(2)}) collective-permute-start(bf16[256,512]{1,0:T(8,128)(2,1)S(1)} %collective-permute-done.5.a), channel_id=1, source_target_pairs={{0,1},{1,0},{2,3},{3,2},{4,5},{5,4},{6,7},{7,6},{8,9},{9,8},{10,11... | collective-permute-start | bytes 786440 | tf_op jit(solution)/shard_map/ppermute | solution.py:187
  23.6 3.9 %collective-permute-done.1.a = bf16[256,512]{1,0:T(8,128)(2,1)S(1)} collective-permute-done((bf16[256,512]{1,0:T(8,128)(2,1)}, bf16[256,512]{1,0:T(8,128)(2,1)S(1)}, u32[]{:S(2)}, u32[]{:S(2)}) %collective-permute-start.1) | collective-permute-done | bytes 262176 | tf_op jit(solution)/shard_map/ppermute | solution.py:184
  27.5 1.1 %collective-permute-start.2 = (bf16[256,512]{1,0:T(8,128)(2,1)S(1)}, bf16[256,512]{1,0:T(8,128)(2,1)}, u32[]{:S(2)}, u32[]{:S(2)}) collective-permute-start(bf16[256,512]{1,0:T(8,128)(2,1)S(1)} %collective-permute-done.1.a), channel_id=1, source_target_pairs={{0,1},{1,0},{2,3},{3,2},{4,5},{5,4},{6,7},{7,6},{8,9},{9,8},{10,11... | collective-permute-start | bytes 786440 | tf_op jit(solution)/shard_map/ppermute | solution.py:187
  28.6 0.1 collective-permute-start.4
  28.7 1.2 %copy-done.3 = bf16[1024,512]{1,0:T(8,128)(2,1)S(1)} copy-done((bf16[1024,512]{1,0:T(8,128)(2,1)S(1)}, bf16[1024,512]{1,0:T(8,128)(2,1)}, u32[]{:S(2)}) %copy-start.3) | copy-done | bytes 1048600
  29.9 0.5 %shard_map.100.q_ref = bf16[512,256]{1,0:T(8,128)(2,1)S(1)} custom-call(bf16[256,512]{1,0:T(8,128)(2,1)S(1)} %copy-done.2, bf16[256,512]{1,0:T(8,128)(2,1)S(1)} %collective-permute-done.3.b, bf16[1024,512]{1,0:T(8,128)(2,1)S(1)} %copy-done.3), custom_call_target="tpu_custom_call" | custom-call | tf_op jit(solution)/shard_map/pallas_call | solution.py:209
  30.5 3.1 %shard_map.102 = (f32[8,72,256]{2,1,0:T(8,128)S(1)}, f32[8,256]{1,0:T(8,128)S(1)}, bf16[1024,128]{1,0:T(8,128)(2,1)S(1)}, bf16[128,512]{1,0:T(8,128)(2,1)S(1)}) custom-call(bf16[8,128,128]{2,1,0:T(8,128)(2,1)S(1)} %all-to-all-done.got, bf16[8,64,128]{2,1,0:T(8,128)(2,1)S(1)} %collective-permute-done.4.other, bf16[256,512]{1,0:T(8,128)(2,1)S(1)} %copy-done.2, ...), custom_call_target="tpu_custom_call" | custom-call | tf_op jit(solution)/shard_map/pallas_call | solution.py:220
  33.6 0.0 copy-start.7
  33.6 0.6 %copy-done.6 = s32[8]{0:T(128)S(1)} copy-done((s32[8]{0:T(128)S(1)}, s32[8]{0:T(128)}, u32[]{:S(2)}) %copy-start.6) | copy-done | bytes 56
  34.2 0.0 copy-done.7
  34.2 4.1 %shard_map.103 = (f32[8,72,256]{2,1,0:T(8,128)S(1)}, f32[8,256]{1,0:T(8,128)S(1)}) custom-call(s32[8]{0:T(128)S(1)} %copy-done.6, s32[8]{0:T(128)S(1)} %copy-done.7, bf16[256,512]{1,0:T(8,128)(2,1)} %collective-permute-done.a, bf16[256,512]{1,0:T(8,128)(2,1)} %collective-permute-done.7.b, bf16[512,256]{1,0:T(8,128)(2,1)S(1)} %shard_map.100.q_ref, ...), custom_call_target="tpu_custom_call" | custom-call | tf_op jit(solution)/shard_map/pallas_call | solution.py:233
  38.4 4.1 %shard_map.104 = (f32[8,72,256]{2,1,0:T(8,128)S(1)}, f32[8,256]{1,0:T(8,128)S(1)}) custom-call(s32[8]{0:T(128)S(1)} %copy-done.6, s32[8]{0:T(128)S(1)} %copy-done.7, bf16[256,512]{1,0:T(8,128)(2,1)S(1)} %collective-permute-done.5.a, bf16[256,512]{1,0:T(8,128)(2,1)} %collective-permute-done.6.b, bf16[512,256]{1,0:T(8,128)(2,1)S(1)} %shard_map.100.q_ref, ...), custom_call_target="tpu_custom_call" | custom-call | tf_op jit(solution)/shard_map/pallas_call | solution.py:233
  42.5 4.8 %shard_map.105 = bf16[256,512]{1,0:T(8,128)(2,1)} custom-call(s32[8]{0:T(128)S(1)} %copy-done.6, s32[8]{0:T(128)S(1)} %copy-done.7, bf16[256,512]{1,0:T(8,128)(2,1)S(1)} %collective-permute-done.1.a, bf16[256,512]{1,0:T(8,128)(2,1)} %collective-permute-done.2.b, bf16[512,256]{1,0:T(8,128)(2,1)S(1)} %shard_map.100.q_ref, bf16[1024,512]{1,0:T(8,128)(2,1)S(1)} %copy-done, ...), custom_call_target="tpu_custom_call" | custom-call | tf_op jit(solution)/shard_map/pallas_call | solution.py:233
  (21 shorter events, 0.1 us)
Async XLA Ops:
  0.0 11.8 %collective-permute-start = (bf16[256,512]{1,0:T(8,128)(2,1)}, bf16[256,512]{1,0:T(8,128)(2,1)}, u32[]{:S(2)}, u32[]{:S(2)}) collective-permute-start(bf16[256,512]{1,0:T(8,128)(2,1)} %a.3), channel_id=1, source_target_pairs={{0,4},{2,6},{4,8},{6,10},{8,12},{10,14},{12,0},{14,2},{1,5},{3,7},... | collective-permute-start | bytes 786440 | tf_op jit(solution)/shard_map/ppermute | solution.py:184
  1.3 0.9 %copy-start.4 = (bf16[8,128,128]{2,1,0:T(8,128)(2,1)S(1)}, bf16[8,128,128]{2,1,0:T(8,128)(2,1)}, u32[]{:S(2)}) copy-start(bf16[8,128,128]{2,1,0:T(8,128)(2,1)} %down_ref.1) | copy-start | bytes 786436
  2.2 0.9 %copy-start.5 = (bf16[8,16,512]{2,1,0:T(8,128)(2,1)S(1)}, bf16[8,16,512]{2,1,0:T(8,128)(2,1)}, u32[]{:S(2)}) copy-start(bf16[8,16,512]{2,1,0:T(8,128)(2,1)} %up_ref.1) | copy-start | bytes 393220
  3.2 0.7 %copy-start.8 = (s32[8]{0:T(128)S(1)}, s32[8]{0:T(128)}, u32[]{:S(2)}) copy-start(s32[8]{0:T(128)} %row_ref.1) | copy-start | bytes 100
  3.8 0.7 %copy-start.9 = (s32[8]{0:T(128)S(1)}, s32[8]{0:T(128)}, u32[]{:S(2)}) copy-start(s32[8]{0:T(128)} %lang_ref.1) | copy-start | bytes 100
  5.7 4.8 %copy-start.2 = (bf16[256,512]{1,0:T(8,128)(2,1)S(1)}, bf16[256,512]{1,0:T(8,128)(2,1)}, u32[]{:S(2)}) copy-start(bf16[256,512]{1,0:T(8,128)(2,1)} %a.3) | copy-start | bytes 786436
  5.8 22.9 %all-to-all-start = ((bf16[8,128,128]{2,1,0:T(8,128)(2,1)}), bf16[8,128,128]{2,1,0:T(8,128)(2,1)S(1)}, u32[]{:S(2)}, u32[]{:S(2)}) async-start(bf16[8,128,128]{2,1,0:T(8,128)(2,1)} %shard_map.101), calls=%async_computation | async-start | bytes 524288 | tf_op jit(solution)/shard_map/all_to_all | solution.py:198
  10.5 19.9 %copy-start = (bf16[1024,512]{1,0:T(8,128)(2,1)S(1)}, bf16[1024,512]{1,0:T(8,128)(2,1)}, u32[]{:S(2)}) copy-start(bf16[1024,512]{1,0:T(8,128)(2,1)} %wk.7) | copy-start | bytes 3145732
  10.5 19.9 %copy-start.1 = (bf16[1024,512]{1,0:T(8,128)(2,1)S(1)}, bf16[1024,512]{1,0:T(8,128)(2,1)}, u32[]{:S(2)}) copy-start(bf16[1024,512]{1,0:T(8,128)(2,1)} %wv.7) | copy-start | bytes 3145732
  10.5 11.2 %collective-permute-start.5 = (bf16[256,512]{1,0:T(8,128)(2,1)S(1)}, bf16[256,512]{1,0:T(8,128)(2,1)S(1)}, u32[]{:S(2)}, u32[]{:S(2)}) collective-permute-start(bf16[256,512]{1,0:T(8,128)(2,1)S(1)} %copy-done.2), channel_id=1, source_target_pairs={{0,2},{2,4},{4,6},{6,8},{8,10},{10,12},{12,14},{14,0},{1,3},{3,5},... | collective-permute-start | bytes 786440 | tf_op jit(solution)/shard_map/ppermute | solution.py:184
  11.8 15.7 %collective-permute-start.1 = (bf16[256,512]{1,0:T(8,128)(2,1)}, bf16[256,512]{1,0:T(8,128)(2,1)S(1)}, u32[]{:S(2)}, u32[]{:S(2)}) collective-permute-start(bf16[256,512]{1,0:T(8,128)(2,1)} %collective-permute-done.a), channel_id=1, source_target_pairs={{0,2},{2,4},{4,6},{6,8},{8,10},{10,12},{12,14},{14,0},{1,3},{3,5},... | collective-permute-start | bytes 786440 | tf_op jit(solution)/shard_map/ppermute | solution.py:184
  13.0 15.7 %collective-permute-start.3 = (bf16[256,512]{1,0:T(8,128)(2,1)S(1)}, bf16[256,512]{1,0:T(8,128)(2,1)S(1)}, u32[]{:S(2)}, u32[]{:S(2)}) collective-permute-start(bf16[256,512]{1,0:T(8,128)(2,1)S(1)} %copy-done.2), channel_id=1, source_target_pairs={{0,1},{1,0},{2,3},{3,2},{4,5},{5,4},{6,7},{7,6},{8,9},{9,8},{10,11... | collective-permute-start | bytes 786440 | tf_op jit(solution)/shard_map/ppermute | solution.py:187
  15.0 18.5 %collective-permute-start.7 = (bf16[256,512]{1,0:T(8,128)(2,1)}, bf16[256,512]{1,0:T(8,128)(2,1)}, u32[]{:S(2)}, u32[]{:S(2)}) collective-permute-start(bf16[256,512]{1,0:T(8,128)(2,1)} %collective-permute-done.a), channel_id=1, source_target_pairs={{0,1},{1,0},{2,3},{3,2},{4,5},{5,4},{6,7},{7,6},{8,9},{9,8},{10,11... | collective-permute-start | bytes 786440 | tf_op jit(solution)/shard_map/ppermute | solution.py:187
  21.8 16.6 %collective-permute-start.6 = (bf16[256,512]{1,0:T(8,128)(2,1)S(1)}, bf16[256,512]{1,0:T(8,128)(2,1)}, u32[]{:S(2)}, u32[]{:S(2)}) collective-permute-start(bf16[256,512]{1,0:T(8,128)(2,1)S(1)} %collective-permute-done.5.a), channel_id=1, source_target_pairs={{0,1},{1,0},{2,3},{3,2},{4,5},{5,4},{6,7},{7,6},{8,9},{9,8},{10,11... | collective-permute-start | bytes 786440 | tf_op jit(solution)/shard_map/ppermute | solution.py:187
  27.5 15.0 %collective-permute-start.2 = (bf16[256,512]{1,0:T(8,128)(2,1)S(1)}, bf16[256,512]{1,0:T(8,128)(2,1)}, u32[]{:S(2)}, u32[]{:S(2)}) collective-permute-start(bf16[256,512]{1,0:T(8,128)(2,1)S(1)} %collective-permute-done.1.a), channel_id=1, source_target_pairs={{0,1},{1,0},{2,3},{3,2},{4,5},{5,4},{6,7},{7,6},{8,9},{9,8},{10,11... | collective-permute-start | bytes 786440 | tf_op jit(solution)/shard_map/ppermute | solution.py:187
  28.6 1.8 %collective-permute-start.4 = (bf16[8,64,128]{2,1,0:T(8,128)(2,1)S(1)}, bf16[8,64,128]{2,1,0:T(8,128)(2,1)S(1)}, u32[]{:S(2)}, u32[]{:S(2)}) collective-permute-start(bf16[8,64,128]{2,1,0:T(8,128)(2,1)S(1)} %slice.4), channel_id=1, source_target_pairs={{0,1},{1,0},{2,3},{3,2},{4,5},{5,4},{6,7},{7,6},{8,9},{9,8},{10,11... | collective-permute-start | bytes 393224 | tf_op jit(solution)/shard_map/ppermute | solution.py:187
  28.7 1.2 %copy-start.3 = (bf16[1024,512]{1,0:T(8,128)(2,1)S(1)}, bf16[1024,512]{1,0:T(8,128)(2,1)}, u32[]{:S(2)}) copy-start(bf16[1024,512]{1,0:T(8,128)(2,1)} %wq.1) | copy-start | bytes 3145732
  33.6 0.7 %copy-start.6 = (s32[8]{0:T(128)S(1)}, s32[8]{0:T(128)}, u32[]{:S(2)}) copy-start(s32[8]{0:T(128)} %seg_ref.5) | copy-start | bytes 100
  33.6 0.7 %copy-start.7 = (s32[8]{0:T(128)S(1)}, s32[8]{0:T(128)}, u32[]{:S(2)}) copy-start(s32[8]{0:T(128)} %look_ref.5) | copy-start | bytes 100

commit v3 on v2

v3 whole, which is shorter than its diff:
```python
import functools

import jax
import jax.numpy as jnp
from jax import lax
from jax.experimental import pallas as pl
from jax.experimental.pallas import tpu as pltpu
from jax.sharding import PartitionSpec as P

HD = 64
LANES = 128
LOOK = 3
VMEM_BYTES = 8 * 1024 * 1024
F32 = jnp.float32
BF16 = jnp.bfloat16

VMEM = functools.partial(pl.BlockSpec, memory_space=pltpu.VMEM)
HBM = functools.partial(pl.BlockSpec, memory_space=pltpu.HBM)


def mm(a, b):
    return jnp.dot(a, b, preferred_element_type=F32)


def reach(seg_ref, look_ref, position):
    count = jnp.int32(0)
    for distance in range(1, LOOK + 1):
        earlier = jnp.maximum(position - distance, 0)
        allowed = (
            (position >= distance)
            & (look_ref[position] >= distance)
            & (seg_ref[earlier] == seg_ref[position])
        )
        count = count + allowed.astype(jnp.int32)
    return count


def rules_kernel(
    packed, row_hbm, lang_hbm, seg_hbm, look_hbm, down_hbm, up_hbm, *refs
):
    if packed:
        reach_ref, out_ref, row, lang, seg, look, down, up, sems = refs
        pairs = [(row_hbm, row), (lang_hbm, lang), (seg_hbm, seg), (look_hbm, look)]
        pairs += [(down_hbm, down), (up_hbm, up)]
    else:
        reach_ref, seg, look, sems = refs
        pairs = [(seg_hbm, seg), (look_hbm, look)]
    copies = [pltpu.make_async_copy(a, b, sems.at[k]) for k, (a, b) in enumerate(pairs)]
    for copy in copies:
        copy.start()
    for copy in copies:
        copy.wait()
    count = reach(seg, look, lax.axis_index("seq"))
    reach_ref[...] = jnp.full(reach_ref.shape, count, jnp.int32)
    if packed:
        half = down.shape[1] // 2
        depth = up.shape[1]
        mine = pl.ds(pl.multiple_of(lax.axis_index("head") * half, half), half)
        for j in range(out_ref.shape[0]):
            chosen = row[lang[j]]
            out_ref[j, :half, :] = down[chosen, mine, :]
            for c in range(up.shape[2] // LANES):
                out_ref[j, half + c * depth : half + (c + 1) * depth, :] = up[
                    chosen, :, c * LANES : (c + 1) * LANES
                ]


def cost(microseconds):
    return pl.CostEstimate(flops=int(microseconds * 1e9), bytes_accessed=0, transcendentals=0)


def rules(packed, bank_row, lang_ids, seg_ids, lookback, down_bank, up_bank, count):
    rows = down_bank.shape[1] // 2 + up_bank.shape[1] * (up_bank.shape[2] // LANES)
    out_shape = [jax.ShapeDtypeStruct((8, LANES), jnp.int32)]
    tables = [seg_ids, lookback]
    scratch = []
    if packed:
        out_shape.append(jax.ShapeDtypeStruct((count, rows, LANES), BF16))
        tables = [bank_row, lang_ids] + tables
        scratch = [pltpu.VMEM(down_bank.shape, BF16), pltpu.VMEM(up_bank.shape, BF16)]
    scratch = [pltpu.SMEM(t.shape, jnp.int32) for t in tables] + scratch
    return pl.pallas_call(
        functools.partial(rules_kernel, packed),
        out_shape=out_shape,
        in_specs=[HBM()] * 6,
        out_specs=[VMEM()] * len(out_shape),
        scratch_shapes=scratch + [pltpu.SemaphoreType.DMA((len(scratch),))],
        compiler_params=pltpu.CompilerParams(vmem_limit_bytes=VMEM_BYTES),
        cost_estimate=cost(2),
    )(
        *(
            pltpu.with_memory_space_constraint(x, pltpu.HBM)
            for x in (bank_row, lang_ids, seg_ids, lookback, down_bank, up_bank)
        )
    )


def halves(head, width):
    mine = pl.ds(pl.multiple_of(head * width, width), width)
    other = pl.ds(pl.multiple_of((1 - head) * width, width), width)
    return mine, other


def query_kernel(a, b, wq, wk, wv, q_ref):
    mine, other = halves(lax.axis_index("head"), a.shape[1])
    queries = (mm(a[...], wq[mine, :]) + mm(b[...], wq[other, :])).astype(BF16)
    q_ref[...] = (queries * jnp.asarray(HD**-0.5, BF16)).T


def lower_kernel(got, b_ref, q_ref, half_ref):
    half_ref[...] = got[:, : half_ref.shape[1], :]


def unpack(got, other, down_ref, up_ref):
    head = lax.axis_index("head")
    half = other.shape[1]
    depth = up_ref.shape[0] // got.shape[0]
    for j in range(got.shape[0]):
        for part, source in ((head, got), (1 - head, other)):
            place = pl.ds(pl.multiple_of(j * 2 * half + part * half, half), half)
            down_ref[place, :] = source[j, :half, :]
    for c in range(up_ref.shape[1] // LANES):
        piece = got[:, half + c * depth : half + (c + 1) * depth, :]
        up_ref[:, c * LANES : (c + 1) * LANES] = piece.reshape(up_ref.shape[0], LANES)


def keys_values(a, b, wk, wv, down_ref, up_ref):
    mine, other = halves(lax.axis_index("head"), a.shape[1])
    first, second = a[...], b[...]
    lowrank = mm(first, down_ref[mine, :]) + mm(second, down_ref[other, :])
    lowrank = lowrank.astype(BF16)
    lane = lax.broadcasted_iota(jnp.int32, lowrank.shape, 1)
    split = lowrank.shape[1] // 2
    zero = jnp.zeros_like(lowrank)
    low_key = jnp.where(lane < split, lowrank, zero)
    low_value = jnp.where(lane < split, zero, lowrank)
    up = up_ref[...]
    keys = mm(first, wk[mine, :]) + mm(second, wk[other, :]) + mm(low_key, up)
    values = mm(first, wv[mine, :]) + mm(second, wv[other, :]) + mm(low_value, up)
    return keys.astype(BF16), values.astype(BF16)


def attend(q_ref, keys, values, before, after, weights_ref):
    turned = values.T
    ones = jnp.ones((16, turned.shape[1]), BF16)
    acc_ref, max_ref = after
    heads = acc_ref.shape[0]
    factors = []
    for i in range(heads):
        q = q_ref[i * HD : (i + 1) * HD, :]
        zero = jnp.zeros_like(q)
        q = jnp.concatenate([q, zero] if i % 2 == 0 else [zero, q], axis=0)
        scores = mm(keys[:, i // 2 * LANES : (i // 2 + 1) * LANES], q)
        top = jnp.max(scores, axis=0, keepdims=True)
        if before is not None:
            old = before[1][i : i + 1, :]
            top = jnp.maximum(top, old)
            factors.append(jnp.exp(old - top))
        weights_ref[i] = jnp.exp(scores - top).astype(BF16)
        max_ref[i : i + 1, :] = top
    for i in range(heads):
        left = jnp.concatenate([turned[i * HD : (i + 1) * HD, :], ones], axis=0)
        update = mm(left, weights_ref[i])[: acc_ref.shape[1], :]
        if before is not None:
            update = before[0][i] * factors[i] + update
        acc_ref[i] = update


def finish(acc_ref, out_ref):
    for pair in range(acc_ref.shape[0] // 2):
        parts = []
        for i in (2 * pair, 2 * pair + 1):
            parts.append(acc_ref[i, :HD, :] / acc_ref[i, HD : HD + 1, :])
        out_ref[:, pair * LANES : (pair + 1) * LANES] = (
            jnp.concatenate(parts, axis=0).T.astype(BF16)
        )


def opening_kernel(
    packed, got, other, reach_ref, a0, b0, a2_hbm, b2_hbm, a1_hbm, b1_hbm, q_ref, wk, wv,
    acc_ref, max_ref, down_ref, up_ref, token_ref, a2, b2, a1, b1, weights_ref, sems,
):
    pairs = ((a2_hbm, a2), (b2_hbm, b2), (a1_hbm, a1), (b1_hbm, b1))
    copies = [pltpu.make_async_copy(x, y, sems.at[k]) for k, (x, y) in enumerate(pairs)]
    for copy in copies:
        copy.start()
    token_ref[...] = reach_ref[...]
    if packed:
        unpack(got, other, down_ref, up_ref)
    else:
        down_ref[...] = got[...]
        up_ref[...] = other[...]
    state = (acc_ref, max_ref)
    keys, values = keys_values(a0, b0, wk, wv, down_ref, up_ref)
    attend(q_ref, keys, values, None, state, weights_ref)
    for copy in copies:
        copy.wait()
    count = reach_ref[0, 0]

    @pl.when(count >= 2)
    def _():
        keys, values = keys_values(a2, b2, wk, wv, down_ref, up_ref)
        attend(q_ref, keys, values, state, state, weights_ref)

    @pl.when((lax.axis_index("seq") % 2 == 1) & (count >= 1))
    def _():
        keys, values = keys_values(a1, b1, wk, wv, down_ref, up_ref)
        attend(q_ref, keys, values, state, state, weights_ref)


def block_kernel(
    distances, reach_ref, a, b, q_ref, wk, wv, down_ref, up_ref, acc_in, max_in,
    acc_ref, max_ref, weights_ref,
):
    odd = lax.axis_index("seq") % 2
    even_distance, odd_distance = distances
    distance = jnp.where(odd == 1, odd_distance, even_distance)

    @pl.when(reach_ref[0, 0] >= distance)
    def _():
        keys, values = keys_values(a, b, wk, wv, down_ref, up_ref)
        attend(q_ref, keys, values, (acc_in, max_in), (acc_ref, max_ref), weights_ref)


def closing_kernel(
    distances, reach_ref, a, b, q_ref, wk, wv, down_ref, up_ref, acc_in, max_in,
    out_ref, acc_ref, max_ref, weights_ref,
):
    odd = lax.axis_index("seq") % 2
    even_distance, odd_distance = distances
    distance = jnp.where(odd == 1, odd_distance, even_distance)
    needed = reach_ref[0, 0] >= distance

    @pl.when(needed)
    def _():
        keys, values = keys_values(a, b, wk, wv, down_ref, up_ref)
        attend(q_ref, keys, values, (acc_in, max_in), (acc_ref, max_ref), weights_ref)
        finish(acc_ref, out_ref)

    @pl.when(jnp.logical_not(needed))
    def _():
        finish(acc_in, out_ref)


def body(
    frames, w_query, w_key, w_value, down_bank, up_bank, bank_row, lang_ids, seg_ids, lookback
):
    count = lax.axis_size("seq")
    rows, width = frames.shape
    columns = w_query.shape[1]
    heads = columns // HD
    model_width = w_query.shape[0]
    rank_two = down_bank.shape[2]
    params = pltpu.CompilerParams(vmem_limit_bytes=VMEM_BYTES)

    def permute(x, route, name):
        with jax.named_scope(name):
            return lax.ppermute(x, "seq", route)

    def swap(x, name):
        with jax.named_scope(name + "_swap"):
            return lax.ppermute(x, "head", [(0, 1), (1, 0)])

    a0 = frames
    b0 = swap(a0, "own")
    q = pl.pallas_call(
        query_kernel,
        out_shape=jax.ShapeDtypeStruct((columns, rows), BF16),
        in_specs=[VMEM()] * 5,
        out_specs=VMEM(),
        compiler_params=params,
        cost_estimate=cost(10),
    )(a0, b0, w_query, w_key, w_value)
    near = [(i, i ^ 1) for i in range(count)]
    two = [(i, (i + 2) % count) for i in range(count)]
    rest = [(i, i + 1) for i in range(1, count - 1, 2)]

    a2 = permute(a0, two, "two")
    b2 = swap(a2, "two")
    a1 = permute(a0, near, "near")
    packed = down_bank.shape[1] % 32 == 0 and up_bank.shape[1] % 16 == 0
    reaching, *sent = rules(
        packed, bank_row, lang_ids, seg_ids, lookback, down_bank, up_bank, count
    )
    if packed:
        got = lax.all_to_all(sent[0], "seq", split_axis=0, concat_axis=0, tiled=True)
        half = pl.pallas_call(
            lower_kernel,
            out_shape=jax.ShapeDtypeStruct((count, down_bank.shape[1] // 2, LANES), BF16),
            in_specs=[VMEM()] * 3,
            out_specs=VMEM(),
            compiler_params=params,
        )(got, b2, q)
        other = swap(half, "down")
    else:
        wanted = jnp.take(bank_row, lang_ids, axis=0)
        got = lax.all_to_all(
            jnp.take(down_bank, wanted, axis=0), "seq", split_axis=0, concat_axis=0, tiled=True
        ).reshape(model_width, rank_two)
        other = lax.all_to_all(
            jnp.take(up_bank, wanted, axis=0), "seq", split_axis=0, concat_axis=0, tiled=True
        ).reshape(rank_two, columns)
    ax = permute(a2, near, "cross")
    a3 = permute(a2, rest, "rest")
    b1 = swap(a1, "near")

    state = (
        jax.ShapeDtypeStruct((heads, HD + 8, rows), F32),
        jax.ShapeDtypeStruct((heads, rows), F32),
    )
    weights = pltpu.VMEM((heads, rows, rows), BF16)
    half_frames = pltpu.VMEM((rows, width), BF16)
    acc, top, down, up, reached = pl.pallas_call(
        functools.partial(opening_kernel, packed),
        out_shape=state
        + (
            jax.ShapeDtypeStruct((model_width, rank_two), BF16),
            jax.ShapeDtypeStruct((rank_two, columns), BF16),
            jax.ShapeDtypeStruct((8, LANES), jnp.int32),
        ),
        in_specs=[VMEM()] * 5 + [HBM()] * 4 + [VMEM()] * 3,
        out_specs=(VMEM(),) * 5,
        scratch_shapes=[half_frames] * 4 + [weights, pltpu.SemaphoreType.DMA((4,))],
        compiler_params=params,
        cost_estimate=cost(0.1),
    )(
        got, other, reaching, a0, b0,
        *(pltpu.with_memory_space_constraint(x, pltpu.HBM) for x in (a2, b2, a1, b1)),
        q, w_key, w_value,
    )
    never = LOOK + 1
    ax, a3, reached = lax.optimization_barrier((ax, a3, reached))
    bx, b3 = swap(ax, "cross"), swap(a3, "rest")
    acc, top = pl.pallas_call(
        functools.partial(block_kernel, (1, 3)),
        out_shape=state,
        in_specs=[VMEM()] * 10,
        out_specs=(VMEM(), VMEM()),
        scratch_shapes=[weights],
        input_output_aliases={8: 0, 9: 1},
        compiler_params=params,
        cost_estimate=cost(2),
    )(reached, ax, bx, q, w_key, w_value, down, up, acc, top)
    return pl.pallas_call(
        functools.partial(closing_kernel, (3, never)),
        out_shape=jax.ShapeDtypeStruct((rows, columns), BF16),
        in_specs=[VMEM()] * 10,
        out_specs=VMEM(),
        scratch_shapes=[pltpu.VMEM(s.shape, F32) for s in state] + [weights],
        compiler_params=params,
        cost_estimate=cost(2),
    )(reached, a3, b3, q, w_key, w_value, down, up, acc, top)


def solution(mesh):
    in_specs = (
        P(("parts", "seq"), "head"),
        P(None, "head"),
        P(None, "head"),
        P(None, "head"),
        P(None, "seq", None),
        P(None, "seq", "head"),
        P(),
        P("parts"),
        P("parts"),
        P("parts"),
    )
    out_specs = P(("parts", "seq"), "head")
    return jax.shard_map(body, mesh=mesh, in_specs=in_specs, out_specs=out_specs, check_vma=False)
```

time: 47.4 us -> 34.6 us (0.73)
  the two profiles are of different devices: /device:TPU:11 before, /device:TPU:25 now
where the time goes in v3:
time: 34.6 us; the launch traced here: 34.2 us
  starting transfers between devices  12.2 us (35%)
  Pallas kernels  12.2 us (35%)
  waiting for transfers between devices  7.75 us (22%)
  local copies, waits for them, and re-layouts  1.92 us (6%)
    all_to_all x1, starting transfers between devices, body(): lax.all_to_all(sent[0], 'seq', split_axis=0, concat_axis=0, tiled=True)  5.02 us
    ppermute x4, waiting for transfers between devices, permute(): return lax.ppermute(x, 'seq', route)  3.87 us
    ppermute x4, starting transfers between devices, permute(): return lax.ppermute(x, 'seq', route)  3.74 us
    pallas_call x1, Pallas kernels, body(): pl.pallas_call(functools.partial(opening_kernel, packed), out_shape=state...  3.74 us
    pallas_call x1, Pallas kernels, body(): pl.pallas_call(functools.partial(closing_kernel, (3, never)), out_shape=j...  3.49 us
    ppermute x6, starting transfers between devices, swap(): return lax.ppermute(x, 'head', [(0, 1), (1, 0)])  3.44 us
    pallas_call x1, Pallas kernels, body(): pl.pallas_call(functools.partial(block_kernel, (1, 3)), out_shape=state,...  2.71 us
    ppermute x6, waiting for transfers between devices, swap(): return lax.ppermute(x, 'head', [(0, 1), (1, 0)])  2.36 us
  transfers between devices with their start and end apart: 11, of which 4 were waited for; matrix products, arithmetic and copies ran while one was open for 0% of the time, Pallas kernels for 26%

profile of v3, /device:TPU:25, one launch (start us, length us, event | category | flops | bytes accessed | tf_op | source)
XLA Modules:
  0.0 34.2 jit_solution(9458175840488608385)
XLA Ops:
  0.0 0.0 collective-permute-start
  0.0 1.3 %collective-permute-start.6 = (bf16[256,512]{1,0:T(8,128)(2,1)}, bf16[256,512]{1,0:T(8,128)(2,1)}, u32[]{:S(2)}, u32[]{:S(2)}) collective-permute-start(bf16[256,512]{1,0:T(8,128)(2,1)} %a0.1), channel_id=1, source_target_pairs={{0,2},{2,0},{4,6},{6,4},{8,10},{10,8},{12,14},{14,12},{1,3},{3,1},... | collective-permute-start | bytes 786440 | tf_op jit(solution)/shard_map/near/ppermute | solution.py:258
  1.3 1.1 %collective-permute-start.4 = (bf16[256,512]{1,0:T(8,128)(2,1)}, bf16[256,512]{1,0:T(8,128)(2,1)S(1)}, u32[]{:S(2)}, u32[]{:S(2)}) collective-permute-start(bf16[256,512]{1,0:T(8,128)(2,1)} %a0.1), channel_id=1, source_target_pairs={{0,1},{1,0},{2,3},{3,2},{4,5},{5,4},{6,7},{7,6},{8,9},{9,8},{10,11... | collective-permute-start | bytes 786440 | tf_op jit(solution)/shard_map/own_swap/ppermute | solution.py:262
  2.4 1.8 %shard_map.100 = (s32[8,128]{1,0:T(8,128)S(1)}, bf16[8,128,128]{2,1,0:T(8,128)(2,1)}) custom-call(s32[8]{0:T(128)} %row_hbm.1, s32[8]{0:T(128)} %lang_hbm.1, s32[8]{0:T(128)} %seg_hbm.1, s32[8]{0:T(128)} %look_hbm.1, bf16[8,128,128]{2,1,0:T(8,128)(2,1)} %down_hbm.1, bf16[8,16,512]{2,1,0:T(8,128)(2,1)} %up_hbm.1), custom_call_target="tpu_custom_call" | custom-call | flops 2000000000 | tf_op jit(solution)/shard_map/pallas_call | solution.py:82
  4.2 0.0 copy-start.3
  4.2 5.0 %all-to-all-start = ((bf16[8,128,128]{2,1,0:T(8,128)(2,1)}), bf16[8,128,128]{2,1,0:T(8,128)(2,1)S(1)}, u32[]{:S(2)}, u32[]{:S(2)}) async-start(bf16[8,128,128]{2,1,0:T(8,128)(2,1)} %get-tuple-element.17), calls=%async_computation | async-start | bytes 524288 | tf_op jit(solution)/shard_map/all_to_all | solution.py:286
  9.2 0.6 %collective-permute-start.3 = (bf16[256,512]{1,0:T(8,128)(2,1)}, bf16[256,512]{1,0:T(8,128)(2,1)S(1)}, u32[]{:S(2)}, u32[]{:S(2)}) collective-permute-start(bf16[256,512]{1,0:T(8,128)(2,1)} %collective-permute-done.a2_hbm), channel_id=1, source_target_pairs={{0,1},{1,0},{2,3},{3,2},{4,5},{5,4},{6,7},{7,6},{8,9},{9,8},{10,11... | collective-permute-start | bytes 786440 | tf_op jit(solution)/shard_map/two_swap/ppermute | solution.py:262
  9.8 1.2 %collective-permute-start.1 = (bf16[256,512]{1,0:T(8,128)(2,1)}, bf16[256,512]{1,0:T(8,128)(2,1)}, u32[]{:S(2)}, u32[]{:S(2)}) collective-permute-start(bf16[256,512]{1,0:T(8,128)(2,1)} %collective-permute-done.a2_hbm), channel_id=1, source_target_pairs={{0,2},{2,0},{4,6},{6,4},{8,10},{10,8},{12,14},{14,12},{1,3},{3,1},... | collective-permute-start | bytes 786440 | tf_op jit(solution)/shard_map/cross/ppermute | solution.py:258
  11.0 1.3 %collective-permute-start.2 = (bf16[256,512]{1,0:T(8,128)(2,1)}, bf16[256,512]{1,0:T(8,128)(2,1)}, u32[]{:S(2)}, u32[]{:S(2)}) collective-permute-start(bf16[256,512]{1,0:T(8,128)(2,1)} %collective-permute-done.a2_hbm), channel_id=1, source_target_pairs={{2,4},{6,8},{10,12},{3,5},{7,9},{11,13},{18,20},{22,24},{26,28},{1... | collective-permute-start | bytes 786440 | tf_op jit(solution)/shard_map/rest/ppermute | solution.py:258
  12.3 0.4 %collective-permute-start.7 = (bf16[256,512]{1,0:T(8,128)(2,1)}, bf16[256,512]{1,0:T(8,128)(2,1)}, u32[]{:S(2)}, u32[]{:S(2)}) collective-permute-start(bf16[256,512]{1,0:T(8,128)(2,1)} %collective-permute-done.6.a1_hbm), channel_id=1, source_target_pairs={{0,1},{1,0},{2,3},{3,2},{4,5},{5,4},{6,7},{7,6},{8,9},{9,8},{10,11... | collective-permute-start | bytes 786440 | tf_op jit(solution)/shard_map/near_swap/ppermute | solution.py:262
  12.7 0.0 copy-start.4
  12.7 1.2 %copy-done.4 = bf16[1024,512]{1,0:T(8,128)(2,1)S(1)} copy-done((bf16[1024,512]{1,0:T(8,128)(2,1)S(1)}, bf16[1024,512]{1,0:T(8,128)(2,1)}, u32[]{:S(2)}) %copy-start.4) | copy-done | bytes 1048600
  13.9 0.5 %shard_map.101.q_ref = bf16[512,256]{1,0:T(8,128)(2,1)S(1)} custom-call(bf16[256,512]{1,0:T(8,128)(2,1)S(1)} %copy-done.3, bf16[256,512]{1,0:T(8,128)(2,1)S(1)} %collective-permute-done.4.b.b0, bf16[1024,512]{1,0:T(8,128)(2,1)S(1)} %copy-done.4, bf16[1024,512]{1,0:T(8,128)(2,1)S(1)} %copy-done, bf16[1024,512]{1,0:T(8,128)(2,1)S(1)} %copy-done.1), custom_call_target="tpu_custom_call" | custom-call | flops 10000000000 | tf_op jit(solution)/shard_map/pallas_call | solution.py:266
  14.4 1.5 %all-to-all-done.got = bf16[8,128,128]{2,1,0:T(8,128)(2,1)S(1)} async-done(((bf16[8,128,128]{2,1,0:T(8,128)(2,1)}), bf16[8,128,128]{2,1,0:T(8,128)(2,1)S(1)}, u32[]{:S(2)}, u32[]{:S(2)}) %all-to-all-start) | async-done | bytes 262176 | tf_op jit(solution)/shard_map/all_to_all | solution.py:286
  16.0 0.7 %copy-done.2 = bf16[256,512]{1,0:T(8,128)(2,1)} copy-done((bf16[256,512]{1,0:T(8,128)(2,1)}, bf16[256,512]{1,0:T(8,128)(2,1)S(1)}, u32[]{:S(2)}) %copy-start.2) | copy-done | bytes 262168
  16.7 0.7 %collective-permute-start.5 = (bf16[8,64,128]{2,1,0:T(8,128)(2,1)S(1)}, bf16[8,64,128]{2,1,0:T(8,128)(2,1)S(1)}, u32[]{:S(2)}, u32[]{:S(2)}) collective-permute-start(bf16[8,64,128]{2,1,0:T(8,128)(2,1)S(1)} %shard_map.102), channel_id=1, source_target_pairs={{0,1},{1,0},{2,3},{3,2},{4,5},{5,4},{6,7},{7,6},{8,9},{9,8},{10,11... | collective-permute-start | bytes 393224 | tf_op jit(solution)/shard_map/down_swap/ppermute | solution.py:262
  17.4 1.0 %collective-permute-done.5.other = bf16[8,64,128]{2,1,0:T(8,128)(2,1)S(1)} collective-permute-done((bf16[8,64,128]{2,1,0:T(8,128)(2,1)S(1)}, bf16[8,64,128]{2,1,0:T(8,128)(2,1)S(1)}, u32[]{:S(2)}, u32[]{:S(2)}) %collective-permute-start.5) | collective-permute-done | bytes 131104 | tf_op jit(solution)/shard_map/down_swap/ppermute | solution.py:262
  18.4 3.7 %shard_map.103 = (f32[8,72,256]{2,1,0:T(8,128)S(1)}, f32[8,256]{1,0:T(8,128)S(1)}, bf16[1024,128]{1,0:T(8,128)(2,1)S(1)}, bf16[128,512]{1,0:T(8,128)(2,1)S(1)}, s32[8,128]{1,0:T(8,128)S(1)}) custom-call(bf16[8,128,128]{2,1,0:T(8,128)(2,1)S(1)} %all-to-all-done.got, bf16[8,64,128]{2,1,0:T(8,128)(2,1)S(1)} %collective-permute-done.5.other, ...), custom_call_target="tpu_custom_call" | custom-call | flops 100000000 | tf_op jit(solution)/shard_map/pallas_call | solution.py:313
  22.1 3.9 %collective-permute-done.1.a = bf16[256,512]{1,0:T(8,128)(2,1)} collective-permute-done((bf16[256,512]{1,0:T(8,128)(2,1)}, bf16[256,512]{1,0:T(8,128)(2,1)}, u32[]{:S(2)}, u32[]{:S(2)}) %collective-permute-start.1) | collective-permute-done | bytes 262176 | tf_op jit(solution)/shard_map/cross/ppermute | solution.py:258
  26.0 0.6 %collective-permute-start.9 = (bf16[256,512]{1,0:T(8,128)(2,1)}, bf16[256,512]{1,0:T(8,128)(2,1)S(1)}, u32[]{:S(2)}, u32[]{:S(2)}) collective-permute-start(bf16[256,512]{1,0:T(8,128)(2,1)} %collective-permute-done.1.a), channel_id=1, source_target_pairs={{0,1},{1,0},{2,3},{3,2},{4,5},{5,4},{6,7},{7,6},{8,9},{9,8},{10,11... | collective-permute-start | bytes 786440 | tf_op jit(solution)/shard_map/cross_swap/ppermute | solution.py:262
  26.6 0.0 collective-permute-start.8
  26.6 1.4 %collective-permute-done.9.b = bf16[256,512]{1,0:T(8,128)(2,1)S(1)} collective-permute-done((bf16[256,512]{1,0:T(8,128)(2,1)}, bf16[256,512]{1,0:T(8,128)(2,1)S(1)}, u32[]{:S(2)}, u32[]{:S(2)}) %collective-permute-start.9) | collective-permute-done | bytes 262176 | tf_op jit(solution)/shard_map/cross_swap/ppermute | solution.py:262
  28.0 2.7 %shard_map.104 = (f32[8,72,256]{2,1,0:T(8,128)S(1)}, f32[8,256]{1,0:T(8,128)S(1)}) custom-call(s32[8,128]{1,0:T(8,128)S(1)} %get-tuple-element.20.reach_ref, bf16[256,512]{1,0:T(8,128)(2,1)} %collective-permute-done.1.a, bf16[256,512]{1,0:T(8,128)(2,1)S(1)} %collective-permute-done.9.b, ...), custom_call_target="tpu_custom_call", output_to_operand_aliasing={{0}: (8, {}), {1}: (9, {})} | custom-call | flops 2000000000 | tf_op jit(solution)/shard_map/pallas_call | solution.py:334
  30.7 3.5 %shard_map.105 = bf16[256,512]{1,0:T(8,128)(2,1)} custom-call(s32[8,128]{1,0:T(8,128)S(1)} %get-tuple-element.20.reach_ref, bf16[256,512]{1,0:T(8,128)(2,1)} %collective-permute-done.2.a, bf16[256,512]{1,0:T(8,128)(2,1)S(1)} %collective-permute-done.8.b, bf16[512,256]{1,0:T(8,128)(2,1)S(1)} %shard_map.101.q_ref, bf16[1024,512]{1,0:T(8,128)(2,1)S(1)} %copy-done, ...), custom_call_target="tpu_custom_call" | custom-call | flops 2000000000 | tf_op jit(solution)/shard_map/pallas_call | solution.py:344
  (14 shorter events, 0.0 us)
Async XLA Ops:
  0.0 12.7 %copy-start = (bf16[1024,512]{1,0:T(8,128)(2,1)S(1)}, bf16[1024,512]{1,0:T(8,128)(2,1)}, u32[]{:S(2)}) copy-start(bf16[1024,512]{1,0:T(8,128)(2,1)} %wk.7) | copy-start | bytes 3145732
  0.0 12.7 %copy-start.1 = (bf16[1024,512]{1,0:T(8,128)(2,1)S(1)}, bf16[1024,512]{1,0:T(8,128)(2,1)}, u32[]{:S(2)}) copy-start(bf16[1024,512]{1,0:T(8,128)(2,1)} %wv.7) | copy-start | bytes 3145732
  0.0 9.2 %collective-permute-start = (bf16[256,512]{1,0:T(8,128)(2,1)}, bf16[256,512]{1,0:T(8,128)(2,1)}, u32[]{:S(2)}, u32[]{:S(2)}) collective-permute-start(bf16[256,512]{1,0:T(8,128)(2,1)} %a0.1), channel_id=1, source_target_pairs={{0,4},{2,6},{4,8},{6,10},{8,12},{10,14},{12,0},{14,2},{1,5},{3,7},... | collective-permute-start | bytes 786440 | tf_op jit(solution)/shard_map/two/ppermute | solution.py:258
  0.0 12.2 %collective-permute-start.6 = (bf16[256,512]{1,0:T(8,128)(2,1)}, bf16[256,512]{1,0:T(8,128)(2,1)}, u32[]{:S(2)}, u32[]{:S(2)}) collective-permute-start(bf16[256,512]{1,0:T(8,128)(2,1)} %a0.1), channel_id=1, source_target_pairs={{0,2},{2,0},{4,6},{6,4},{8,10},{10,8},{12,14},{14,12},{1,3},{3,1},... | collective-permute-start | bytes 786440 | tf_op jit(solution)/shard_map/near/ppermute | solution.py:258
  1.3 11.4 %collective-permute-start.4 = (bf16[256,512]{1,0:T(8,128)(2,1)}, bf16[256,512]{1,0:T(8,128)(2,1)S(1)}, u32[]{:S(2)}, u32[]{:S(2)}) collective-permute-start(bf16[256,512]{1,0:T(8,128)(2,1)} %a0.1), channel_id=1, source_target_pairs={{0,1},{1,0},{2,3},{3,2},{4,5},{5,4},{6,7},{7,6},{8,9},{9,8},{10,11... | collective-permute-start | bytes 786440 | tf_op jit(solution)/shard_map/own_swap/ppermute | solution.py:262
  4.2 8.5 %copy-start.3 = (bf16[256,512]{1,0:T(8,128)(2,1)S(1)}, bf16[256,512]{1,0:T(8,128)(2,1)}, u32[]{:S(2)}) copy-start(bf16[256,512]{1,0:T(8,128)(2,1)} %a0.1) | copy-start | bytes 786436
  4.2 11.8 %all-to-all-start = ((bf16[8,128,128]{2,1,0:T(8,128)(2,1)}), bf16[8,128,128]{2,1,0:T(8,128)(2,1)S(1)}, u32[]{:S(2)}, u32[]{:S(2)}) async-start(bf16[8,128,128]{2,1,0:T(8,128)(2,1)} %get-tuple-element.17), calls=%async_computation | async-start | bytes 524288 | tf_op jit(solution)/shard_map/all_to_all | solution.py:286
  9.2 6.8 %collective-permute-start.3 = (bf16[256,512]{1,0:T(8,128)(2,1)}, bf16[256,512]{1,0:T(8,128)(2,1)S(1)}, u32[]{:S(2)}, u32[]{:S(2)}) collective-permute-start(bf16[256,512]{1,0:T(8,128)(2,1)} %collective-permute-done.a2_hbm), channel_id=1, source_target_pairs={{0,1},{1,0},{2,3},{3,2},{4,5},{5,4},{6,7},{7,6},{8,9},{9,8},{10,11... | collective-permute-start | bytes 786440 | tf_op jit(solution)/shard_map/two_swap/ppermute | solution.py:262
  9.8 16.2 %collective-permute-start.1 = (bf16[256,512]{1,0:T(8,128)(2,1)}, bf16[256,512]{1,0:T(8,128)(2,1)}, u32[]{:S(2)}, u32[]{:S(2)}) collective-permute-start(bf16[256,512]{1,0:T(8,128)(2,1)} %collective-permute-done.a2_hbm), channel_id=1, source_target_pairs={{0,2},{2,0},{4,6},{6,4},{8,10},{10,8},{12,14},{14,12},{1,3},{3,1},... | collective-permute-start | bytes 786440 | tf_op jit(solution)/shard_map/cross/ppermute | solution.py:258
  11.0 15.0 %collective-permute-start.2 = (bf16[256,512]{1,0:T(8,128)(2,1)}, bf16[256,512]{1,0:T(8,128)(2,1)}, u32[]{:S(2)}, u32[]{:S(2)}) collective-permute-start(bf16[256,512]{1,0:T(8,128)(2,1)} %collective-permute-done.a2_hbm), channel_id=1, source_target_pairs={{2,4},{6,8},{10,12},{3,5},{7,9},{11,13},{18,20},{22,24},{26,28},{1... | collective-permute-start | bytes 786440 | tf_op jit(solution)/shard_map/rest/ppermute | solution.py:258
  12.3 5.1 %collective-permute-start.7 = (bf16[256,512]{1,0:T(8,128)(2,1)}, bf16[256,512]{1,0:T(8,128)(2,1)}, u32[]{:S(2)}, u32[]{:S(2)}) collective-permute-start(bf16[256,512]{1,0:T(8,128)(2,1)} %collective-permute-done.6.a1_hbm), channel_id=1, source_target_pairs={{0,1},{1,0},{2,3},{3,2},{4,5},{5,4},{6,7},{7,6},{8,9},{9,8},{10,11... | collective-permute-start | bytes 786440 | tf_op jit(solution)/shard_map/near_swap/ppermute | solution.py:262
  12.7 1.2 %copy-start.4 = (bf16[1024,512]{1,0:T(8,128)(2,1)S(1)}, bf16[1024,512]{1,0:T(8,128)(2,1)}, u32[]{:S(2)}) copy-start(bf16[1024,512]{1,0:T(8,128)(2,1)} %wq.1) | copy-start | bytes 3145732
  16.0 0.7 %copy-start.2 = (bf16[256,512]{1,0:T(8,128)(2,1)}, bf16[256,512]{1,0:T(8,128)(2,1)S(1)}, u32[]{:S(2)}) copy-start(bf16[256,512]{1,0:T(8,128)(2,1)S(1)} %collective-permute-done.3.b_ref.b2_hbm) | copy-start | bytes 786436
  16.7 1.7 %collective-permute-start.5 = (bf16[8,64,128]{2,1,0:T(8,128)(2,1)S(1)}, bf16[8,64,128]{2,1,0:T(8,128)(2,1)S(1)}, u32[]{:S(2)}, u32[]{:S(2)}) collective-permute-start(bf16[8,64,128]{2,1,0:T(8,128)(2,1)S(1)} %shard_map.102), channel_id=1, source_target_pairs={{0,1},{1,0},{2,3},{3,2},{4,5},{5,4},{6,7},{7,6},{8,9},{9,8},{10,11... | collective-permute-start | bytes 393224 | tf_op jit(solution)/shard_map/down_swap/ppermute | solution.py:262
  26.0 2.0 %collective-permute-start.9 = (bf16[256,512]{1,0:T(8,128)(2,1)}, bf16[256,512]{1,0:T(8,128)(2,1)S(1)}, u32[]{:S(2)}, u32[]{:S(2)}) collective-permute-start(bf16[256,512]{1,0:T(8,128)(2,1)} %collective-permute-done.1.a), channel_id=1, source_target_pairs={{0,1},{1,0},{2,3},{3,2},{4,5},{5,4},{6,7},{7,6},{8,9},{9,8},{10,11... | collective-permute-start | bytes 786440 | tf_op jit(solution)/shard_map/cross_swap/ppermute | solution.py:262
  26.6 4.1 %collective-permute-start.8 = (bf16[256,512]{1,0:T(8,128)(2,1)}, bf16[256,512]{1,0:T(8,128)(2,1)S(1)}, u32[]{:S(2)}, u32[]{:S(2)}) collective-permute-start(bf16[256,512]{1,0:T(8,128)(2,1)} %collective-permute-done.2.a), channel_id=1, source_target_pairs={{0,1},{1,0},{2,3},{3,2},{4,5},{5,4},{6,7},{7,6},{8,9},{9,8},{10,11... | collective-permute-start | bytes 786440 | tf_op jit(solution)/shard_map/rest_swap/ppermute | solution.py:262

commit v4 on v3

--- a/solution.py
+++ b/solution.py
@@ -15,6 +15,7 @@
 BF16 = jnp.bfloat16
 
 VMEM = functools.partial(pl.BlockSpec, memory_space=pltpu.VMEM)
+ANY = functools.partial(pl.BlockSpec, memory_space=pl.ANY)
 HBM = functools.partial(pl.BlockSpec, memory_space=pltpu.HBM)
 
 
@@ -107,7 +108,8 @@
     q_ref[...] = (queries * jnp.asarray(HD**-0.5, BF16)).T
 
 
-def lower_kernel(got, b_ref, q_ref, half_ref):
+def lower_kernel(got, b_ref, q_ref, reach_ref, half_ref, token_ref):
+    token_ref[...] = reach_ref[...]
     half_ref[...] = got[:, : half_ref.shape[1], :]
 
 
@@ -210,11 +212,12 @@
 
 def block_kernel(
     distances, reach_ref, a, b, q_ref, wk, wv, down_ref, up_ref, acc_in, max_in,
-    acc_ref, max_ref, weights_ref,
+    acc_ref, max_ref, token_ref, weights_ref,
 ):
     odd = lax.axis_index("seq") % 2
     even_distance, odd_distance = distances
     distance = jnp.where(odd == 1, odd_distance, even_distance)
+    token_ref[...] = reach_ref[...]
 
     @pl.when(reach_ref[0, 0] >= distance)
     def _():
@@ -273,7 +276,8 @@
     )(a0, b0, w_query, w_key, w_value)
     near = [(i, i ^ 1) for i in range(count)]
     two = [(i, (i + 2) % count) for i in range(count)]
-    rest = [(i, i + 1) for i in range(1, count - 1, 2)]
+    pairs = [(0, 0), (count - 1, count - 1)]
+    pairs += [(i, i + 1 if i % 2 else i - 1) for i in range(1, count - 1)]
 
     a2 = permute(a0, two, "two")
     b2 = swap(a2, "two")
@@ -284,13 +288,16 @@
     )
     if packed:
         got = lax.all_to_all(sent[0], "seq", split_axis=0, concat_axis=0, tiled=True)
-        half = pl.pallas_call(
+        half, reaching = pl.pallas_call(
             lower_kernel,
-            out_shape=jax.ShapeDtypeStruct((count, down_bank.shape[1] // 2, LANES), BF16),
-            in_specs=[VMEM()] * 3,
-            out_specs=VMEM(),
+            out_shape=(
+                jax.ShapeDtypeStruct((count, down_bank.shape[1] // 2, LANES), BF16),
+                jax.ShapeDtypeStruct((8, LANES), jnp.int32),
+            ),
+            in_specs=[VMEM()] * 4,
+            out_specs=(VMEM(), VMEM()),
             compiler_params=params,
-        )(got, b2, q)
+        )(got, b2, q, reaching)
         other = swap(half, "down")
     else:
         wanted = jnp.take(bank_row, lang_ids, axis=0)
@@ -300,9 +307,13 @@
         other = lax.all_to_all(
             jnp.take(up_bank, wanted, axis=0), "seq", split_axis=0, concat_axis=0, tiled=True
         ).reshape(rank_two, columns)
-    ax = permute(a2, near, "cross")
-    a3 = permute(a2, rest, "rest")
-    b1 = swap(a1, "near")
+    moved = jnp.where(lax.axis_index("head") == 0, a2, a1)
+    ways = [(2 * i, 2 * j) for i, j in near] + [(2 * i + 1, 2 * j + 1) for i, j in two]
+    with jax.named_scope("split"):
+        ax = lax.ppermute(moved, ("seq", "head"), ways)
+    a3 = permute(a2, pairs, "rest")
+    ax, reaching = lax.optimization_barrier((ax, reaching))
+    b1, bx = swap(a1, "near"), swap(ax, "cross")
 
     state = (
         jax.ShapeDtypeStruct((heads, HD + 8, rows), F32),
@@ -318,29 +329,29 @@
             jax.ShapeDtypeStruct((rank_two, columns), BF16),
             jax.ShapeDtypeStruct((8, LANES), jnp.int32),
         ),
-        in_specs=[VMEM()] * 5 + [HBM()] * 4 + [VMEM()] * 3,
+        in_specs=[VMEM()] * 5 + [ANY()] * 4 + [VMEM()] * 3,
         out_specs=(VMEM(),) * 5,
         scratch_shapes=[half_frames] * 4 + [weights, pltpu.SemaphoreType.DMA((4,))],
         compiler_params=params,
         cost_estimate=cost(0.1),
     )(
         got, other, reaching, a0, b0,
-        *(pltpu.with_memory_space_constraint(x, pltpu.HBM) for x in (a2, b2, a1, b1)),
+        *(x for x in (a2, b2, a1, b1)),
         q, w_key, w_value,
     )
     never = LOOK + 1
-    ax, a3, reached = lax.optimization_barrier((ax, a3, reached))
-    bx, b3 = swap(ax, "cross"), swap(a3, "rest")
-    acc, top = pl.pallas_call(
+    a3, reached = lax.optimization_barrier((a3, reached))
+    acc, top, reached = pl.pallas_call(
         functools.partial(block_kernel, (1, 3)),
-        out_shape=state,
+        out_shape=state + (jax.ShapeDtypeStruct((8, LANES), jnp.int32),),
         in_specs=[VMEM()] * 10,
-        out_specs=(VMEM(), VMEM()),
+        out_specs=(VMEM(),) * 3,
         scratch_shapes=[weights],
         input_output_aliases={8: 0, 9: 1},
         compiler_params=params,
-        cost_estimate=cost(2),
+        cost_estimate=cost(0.1),
     )(reached, ax, bx, q, w_key, w_value, down, up, acc, top)
+    b3 = swap(a3, "rest")
     return pl.pallas_call(
         functools.partial(closing_kernel, (3, never)),
         out_shape=jax.ShapeDtypeStruct((rows, columns), BF16),

time: 34.6 us -> 31.9 us (0.922)
  the two profiles are of different devices: /device:TPU:25 before, /device:TPU:9 now
where the time goes in v4:
time: 31.9 us; the launch traced here: 31.3 us
  starting transfers between devices  16.2 us (51%)
  Pallas kernels  10.5 us (33%)
  local copies, waits for them, and re-layouts  2.88 us (9%)
  waiting for transfers between devices  0.92 us (3%)
  other arithmetic  0.73 us (2%)
    ppermute x6, starting transfers between devices, swap(): return lax.ppermute(x, 'head', [(0, 1), (1, 0)])  5.97 us
    ppermute x3, starting transfers between devices, permute(): return lax.ppermute(x, 'seq', route)  5.11 us
    all_to_all x1, starting transfers between devices, body(): lax.all_to_all(sent[0], 'seq', split_axis=0, concat_axis=0, tiled=True)  3.89 us
    pallas_call x1, Pallas kernels, body(): pl.pallas_call(functools.partial(opening_kernel, packed), out_shape=state...  3.57 us
    unnamed x16, local copies, waits for them, and re-layouts  2.88 us
    pallas_call x1, Pallas kernels, body(): pl.pallas_call(functools.partial(block_kernel, (1, 3)), out_shape=state +...  2.71 us
    pallas_call x1, Pallas kernels, rules(): pl.pallas_call(functools.partial(rules_kernel, packed), out_shape=out_sha...  1.86 us
    pallas_call x1, Pallas kernels, body(): pl.pallas_call(functools.partial(closing_kernel, (3, never)), out_shape=j...  1.84 us
  transfers between devices with their start and end apart: 11, of which 1 were waited for; matrix products, arithmetic and copies ran while one was open for 2% of the time, Pallas kernels for 28%

profile of v4, /device:TPU:9, one launch (start us, length us, event | category | flops | bytes accessed | tf_op | source)
XLA Modules:
  0.0 31.3 jit_solution(1948864899887388102)
XLA Ops:
  0.0 1.3 %collective-permute-start = (bf16[256,512]{1,0:T(8,128)(2,1)}, bf16[256,512]{1,0:T(8,128)(2,1)S(1)}, u32[]{:S(2)}, u32[]{:S(2)}) collective-permute-start(bf16[256,512]{1,0:T(8,128)(2,1)} %a0.1), channel_id=1, source_target_pairs={{0,4},{2,6},{4,8},{6,10},{8,12},{10,14},{12,0},{14,2},{1,5},{3,7},... | collective-permute-start | bytes 786440 | tf_op jit(solution)/shard_map/two/ppermute | solution.py:261
  1.3 1.2 %collective-permute-start.5 = (bf16[256,512]{1,0:T(8,128)(2,1)}, bf16[256,512]{1,0:T(8,128)(2,1)S(1)}, u32[]{:S(2)}, u32[]{:S(2)}) collective-permute-start(bf16[256,512]{1,0:T(8,128)(2,1)} %a0.1), channel_id=1, source_target_pairs={{0,2},{2,0},{4,6},{6,4},{8,10},{10,8},{12,14},{14,12},{1,3},{3,1},... | collective-permute-start | bytes 786440 | tf_op jit(solution)/shard_map/near/ppermute | solution.py:261
  2.5 1.2 %collective-permute-start.3 = (bf16[256,512]{1,0:T(8,128)(2,1)}, bf16[256,512]{1,0:T(8,128)(2,1)S(1)}, u32[]{:S(2)}, u32[]{:S(2)}) collective-permute-start(bf16[256,512]{1,0:T(8,128)(2,1)} %a0.1), channel_id=1, source_target_pairs={{0,1},{1,0},{2,3},{3,2},{4,5},{5,4},{6,7},{7,6},{8,9},{9,8},{10,11... | collective-permute-start | bytes 786440 | tf_op jit(solution)/shard_map/own_swap/ppermute | solution.py:265
  3.7 1.9 %shard_map.100 = (s32[8,128]{1,0:T(8,128)S(1)}, bf16[8,128,128]{2,1,0:T(8,128)(2,1)}) custom-call(s32[8]{0:T(128)} %row_hbm.1, s32[8]{0:T(128)} %lang_hbm.1, s32[8]{0:T(128)} %seg_hbm.1, s32[8]{0:T(128)} %look_hbm.1, bf16[8,128,128]{2,1,0:T(8,128)(2,1)} %down_hbm.1, bf16[8,16,512]{2,1,0:T(8,128)(2,1)} %up_hbm.1), custom_call_target="tpu_custom_call" | custom-call | flops 2000000000 | tf_op jit(solution)/shard_map/pallas_call | solution.py:83
  5.6 0.0 copy-start
  5.6 3.9 %all-to-all-start = ((bf16[8,128,128]{2,1,0:T(8,128)(2,1)}), bf16[8,128,128]{2,1,0:T(8,128)(2,1)S(1)}, u32[]{:S(2)}, u32[]{:S(2)}) async-start(bf16[8,128,128]{2,1,0:T(8,128)(2,1)} %get-tuple-element.21), calls=%async_computation | async-start | bytes 524288 | tf_op jit(solution)/shard_map/all_to_all | solution.py:290
  9.5 0.0 collective-permute-done.5.a1_hbm
  9.5 0.7 %broadcast_select_fusion = bf16[256,512]{1,0:T(8,128)(2,1)} fusion(bf16[256,512]{1,0:T(8,128)(2,1)S(1)} %collective-permute-done.a2_hbm, bf16[256,512]{1,0:T(8,128)(2,1)S(1)} %collective-permute-done.5.a1_hbm, pred[]{:T(512)S(6)} %eq.3), kind=kLoop, calls=%fused_computation | loop fusion | flops 131072 | bytes 786433 | tf_op jit(solution)/shard_map/jit(_where)/select_n | solution.py:310
  10.3 1.2 %collective-permute-start.6 = (bf16[256,512]{1,0:T(8,128)(2,1)}, bf16[256,512]{1,0:T(8,128)(2,1)}, u32[]{:S(2)}, u32[]{:S(2)}) collective-permute-start(bf16[256,512]{1,0:T(8,128)(2,1)} %broadcast_select_fusion), channel_id=1, source_target_pairs={{0,2},{2,0},{4,6},{6,4},{8,10},{10,8},{12,14},{14,12},{1,5},{3,7},... | collective-permute-start | bytes 786440 | tf_op jit(solution)/shard_map/split/ppermute | solution.py:313
  11.5 1.0 %collective-permute-start.2 = (bf16[256,512]{1,0:T(8,128)(2,1)S(1)}, bf16[256,512]{1,0:T(8,128)(2,1)S(1)}, u32[]{:S(2)}, u32[]{:S(2)}) collective-permute-start(bf16[256,512]{1,0:T(8,128)(2,1)S(1)} %collective-permute-done.a2_hbm), channel_id=1, source_target_pairs={{0,1},{1,0},{2,3},{3,2},{4,5},{5,4},{6,7},{7,6},{8,9},{9,8},{10,11... | collective-permute-start | bytes 786440 | tf_op jit(solution)/shard_map/two_swap/ppermute | solution.py:265
  12.5 2.6 %collective-permute-start.1 = (bf16[256,512]{1,0:T(8,128)(2,1)S(1)}, bf16[256,512]{1,0:T(8,128)(2,1)}, u32[]{:S(2)}, u32[]{:S(2)}) collective-permute-start(bf16[256,512]{1,0:T(8,128)(2,1)S(1)} %collective-permute-done.a2_hbm), channel_id=1, source_target_pairs={{0,0},{14,14},{2,4},{4,2},{6,8},{8,6},{10,12},{12,10},{1,1},{15,15... | collective-permute-start | bytes 786440 | tf_op jit(solution)/shard_map/rest/ppermute | solution.py:261
  15.1 0.7 %copy-done.4 = bf16[256,512]{1,0:T(8,128)(2,1)} copy-done((bf16[256,512]{1,0:T(8,128)(2,1)}, bf16[256,512]{1,0:T(8,128)(2,1)S(1)}, u32[]{:S(2)}) %copy-start.4) | copy-done | bytes 262168
  15.8 0.9 %copy-done.5 = bf16[256,512]{1,0:T(8,128)(2,1)S(1)} copy-done((bf16[256,512]{1,0:T(8,128)(2,1)S(1)}, bf16[256,512]{1,0:T(8,128)(2,1)}, u32[]{:S(2)}) %copy-start.5) | copy-done | bytes 262168
  16.7 1.2 %copy-done.7 = bf16[1024,512]{1,0:T(8,128)(2,1)S(1)} copy-done((bf16[1024,512]{1,0:T(8,128)(2,1)S(1)}, bf16[1024,512]{1,0:T(8,128)(2,1)}, u32[]{:S(2)}) %copy-start.7) | copy-done | bytes 1048600
  18.0 0.5 %shard_map.101.q_ref = bf16[512,256]{1,0:T(8,128)(2,1)S(1)} custom-call(bf16[256,512]{1,0:T(8,128)(2,1)S(1)} %copy-done.2, bf16[256,512]{1,0:T(8,128)(2,1)S(1)} %copy-done.5, bf16[1024,512]{1,0:T(8,128)(2,1)S(1)} %copy-done.7, bf16[1024,512]{1,0:T(8,128)(2,1)S(1)} %copy-done, bf16[1024,512]{1,0:T(8,128)(2,1)S(1)} %copy-done.1), custom_call_target="tpu_custom_call" | custom-call | flops 10000000000 | tf_op jit(solution)/shard_map/pallas_call | solution.py:269
  18.5 0.0 all-to-all-done.got
  18.5 0.0 copy-start.3
  18.5 3.2 %collective-permute-start.4 = (bf16[8,64,128]{2,1,0:T(8,128)(2,1)S(1)}, bf16[8,64,128]{2,1,0:T(8,128)(2,1)S(1)}, u32[]{:S(2)}, u32[]{:S(2)}) collective-permute-start(bf16[8,64,128]{2,1,0:T(8,128)(2,1)S(1)} %get-tuple-element.23), channel_id=1, source_target_pairs={{0,1},{1,0},{2,3},{3,2},{4,5},{5,4},{6,7},{7,6},{8,9},{9,8},{10,11... | collective-permute-start | bytes 393224 | tf_op jit(solution)/shard_map/down_swap/ppermute | solution.py:265
  21.8 0.1 collective-permute-start.8
  21.9 0.9 %collective-permute-done.4.other = bf16[8,64,128]{2,1,0:T(8,128)(2,1)S(1)} collective-permute-done((bf16[8,64,128]{2,1,0:T(8,128)(2,1)S(1)}, bf16[8,64,128]{2,1,0:T(8,128)(2,1)S(1)}, u32[]{:S(2)}, u32[]{:S(2)}) %collective-permute-start.4) | collective-permute-done | bytes 131104 | tf_op jit(solution)/shard_map/down_swap/ppermute | solution.py:265
  22.8 3.6 %shard_map.103 = (f32[8,72,256]{2,1,0:T(8,128)S(1)}, f32[8,256]{1,0:T(8,128)S(1)}, bf16[1024,128]{1,0:T(8,128)(2,1)S(1)}, bf16[128,512]{1,0:T(8,128)(2,1)S(1)}, s32[8,128]{1,0:T(8,128)S(1)}) custom-call(bf16[8,128,128]{2,1,0:T(8,128)(2,1)S(1)} %all-to-all-done.got, bf16[8,64,128]{2,1,0:T(8,128)(2,1)S(1)} %collective-permute-done.4.other, ...), custom_call_target="tpu_custom_call" | custom-call | flops 100000000 | tf_op jit(solution)/shard_map/pallas_call | solution.py:324
  26.3 0.4 %collective-permute-start.9 = (bf16[256,512]{1,0:T(8,128)(2,1)}, bf16[256,512]{1,0:T(8,128)(2,1)S(1)}, u32[]{:S(2)}, u32[]{:S(2)}) collective-permute-start(bf16[256,512]{1,0:T(8,128)(2,1)} %collective-permute-done.1.a), channel_id=1, source_target_pairs={{0,1},{1,0},{2,3},{3,2},{4,5},{5,4},{6,7},{7,6},{8,9},{9,8},{10,11... | collective-permute-start | bytes 786440 | tf_op jit(solution)/shard_map/rest_swap/ppermute | solution.py:265
  26.8 2.7 %shard_map.104 = (f32[8,72,256]{2,1,0:T(8,128)S(1)}, f32[8,256]{1,0:T(8,128)S(1)}, s32[8,128]{1,0:T(8,128)S(1)}) custom-call(s32[8,128]{1,0:T(8,128)S(1)} %get-tuple-element.27.reach_ref, bf16[256,512]{1,0:T(8,128)(2,1)} %collective-permute-done.6.a, bf16[256,512]{1,0:T(8,128)(2,1)S(1)} %collective-permute-done.8.b, ...), custom_call_target="tpu_custom_call", output_to_operand_aliasing={{0}: (8, {}), {1}: (9, {})} | custom-call | flops 100000000 | tf_op jit(solution)/shard_map/pallas_call | solution.py:344
  29.5 1.8 %shard_map.105 = bf16[256,512]{1,0:T(8,128)(2,1)} custom-call(s32[8,128]{1,0:T(8,128)S(1)} %get-tuple-element.33.reach_ref, bf16[256,512]{1,0:T(8,128)(2,1)} %collective-permute-done.1.a, bf16[256,512]{1,0:T(8,128)(2,1)S(1)} %collective-permute-done.9.b, bf16[512,256]{1,0:T(8,128)(2,1)S(1)} %shard_map.101.q_ref, bf16[1024,512]{1,0:T(8,128)(2,1)S(1)} %copy-done, ...), custom_call_target="tpu_custom_call" | custom-call | flops 2000000000 | tf_op jit(solution)/shard_map/pallas_call | solution.py:355
  (21 shorter events, 0.1 us)
Async XLA Ops:
  0.0 9.5 %collective-permute-start = (bf16[256,512]{1,0:T(8,128)(2,1)}, bf16[256,512]{1,0:T(8,128)(2,1)S(1)}, u32[]{:S(2)}, u32[]{:S(2)}) collective-permute-start(bf16[256,512]{1,0:T(8,128)(2,1)} %a0.1), channel_id=1, source_target_pairs={{0,4},{2,6},{4,8},{6,10},{8,12},{10,14},{12,0},{14,2},{1,5},{3,7},... | collective-permute-start | bytes 786440 | tf_op jit(solution)/shard_map/two/ppermute | solution.py:261
  1.3 8.2 %collective-permute-start.5 = (bf16[256,512]{1,0:T(8,128)(2,1)}, bf16[256,512]{1,0:T(8,128)(2,1)S(1)}, u32[]{:S(2)}, u32[]{:S(2)}) collective-permute-start(bf16[256,512]{1,0:T(8,128)(2,1)} %a0.1), channel_id=1, source_target_pairs={{0,2},{2,0},{4,6},{6,4},{8,10},{10,8},{12,14},{14,12},{1,3},{3,1},... | collective-permute-start | bytes 786440 | tf_op jit(solution)/shard_map/near/ppermute | solution.py:261
  2.5 12.6 %collective-permute-start.3 = (bf16[256,512]{1,0:T(8,128)(2,1)}, bf16[256,512]{1,0:T(8,128)(2,1)S(1)}, u32[]{:S(2)}, u32[]{:S(2)}) collective-permute-start(bf16[256,512]{1,0:T(8,128)(2,1)} %a0.1), channel_id=1, source_target_pairs={{0,1},{1,0},{2,3},{3,2},{4,5},{5,4},{6,7},{7,6},{8,9},{9,8},{10,11... | collective-permute-start | bytes 786440 | tf_op jit(solution)/shard_map/own_swap/ppermute | solution.py:265
  3.7 12.0 %copy-start.1 = (bf16[1024,512]{1,0:T(8,128)(2,1)S(1)}, bf16[1024,512]{1,0:T(8,128)(2,1)}, u32[]{:S(2)}) copy-start(bf16[1024,512]{1,0:T(8,128)(2,1)} %wv.7) | copy-start | bytes 3145732
  5.6 10.2 %copy-start = (bf16[1024,512]{1,0:T(8,128)(2,1)S(1)}, bf16[1024,512]{1,0:T(8,128)(2,1)}, u32[]{:S(2)}) copy-start(bf16[1024,512]{1,0:T(8,128)(2,1)} %wk.7) | copy-start | bytes 3145732
  5.6 12.8 %all-to-all-start = ((bf16[8,128,128]{2,1,0:T(8,128)(2,1)}), bf16[8,128,128]{2,1,0:T(8,128)(2,1)S(1)}, u32[]{:S(2)}, u32[]{:S(2)}) async-start(bf16[8,128,128]{2,1,0:T(8,128)(2,1)} %get-tuple-element.21), calls=%async_computation | async-start | bytes 524288 | tf_op jit(solution)/shard_map/all_to_all | solution.py:290
  9.5 6.3 %copy-start.2 = (bf16[256,512]{1,0:T(8,128)(2,1)S(1)}, bf16[256,512]{1,0:T(8,128)(2,1)}, u32[]{:S(2)}) copy-start(bf16[256,512]{1,0:T(8,128)(2,1)} %a0.1) | copy-start | bytes 786436
  10.3 11.5 %collective-permute-start.6 = (bf16[256,512]{1,0:T(8,128)(2,1)}, bf16[256,512]{1,0:T(8,128)(2,1)}, u32[]{:S(2)}, u32[]{:S(2)}) collective-permute-start(bf16[256,512]{1,0:T(8,128)(2,1)} %broadcast_select_fusion), channel_id=1, source_target_pairs={{0,2},{2,0},{4,6},{6,4},{8,10},{10,8},{12,14},{14,12},{1,5},{3,7},... | collective-permute-start | bytes 786440 | tf_op jit(solution)/shard_map/split/ppermute | solution.py:313
  11.5 7.0 %collective-permute-start.2 = (bf16[256,512]{1,0:T(8,128)(2,1)S(1)}, bf16[256,512]{1,0:T(8,128)(2,1)S(1)}, u32[]{:S(2)}, u32[]{:S(2)}) collective-permute-start(bf16[256,512]{1,0:T(8,128)(2,1)S(1)} %collective-permute-done.a2_hbm), channel_id=1, source_target_pairs={{0,1},{1,0},{2,3},{3,2},{4,5},{5,4},{6,7},{7,6},{8,9},{9,8},{10,11... | collective-permute-start | bytes 786440 | tf_op jit(solution)/shard_map/two_swap/ppermute | solution.py:265
  12.5 9.4 %collective-permute-start.7 = (bf16[256,512]{1,0:T(8,128)(2,1)S(1)}, bf16[256,512]{1,0:T(8,128)(2,1)}, u32[]{:S(2)}, u32[]{:S(2)}) collective-permute-start(bf16[256,512]{1,0:T(8,128)(2,1)S(1)} %collective-permute-done.5.a1_hbm), channel_id=1, source_target_pairs={{0,1},{1,0},{2,3},{3,2},{4,5},{5,4},{6,7},{7,6},{8,9},{9,8},{10,11... | collective-permute-start | bytes 786440 | tf_op jit(solution)/shard_map/near_swap/ppermute | solution.py:265
  12.5 13.9 %collective-permute-start.1 = (bf16[256,512]{1,0:T(8,128)(2,1)S(1)}, bf16[256,512]{1,0:T(8,128)(2,1)}, u32[]{:S(2)}, u32[]{:S(2)}) collective-permute-start(bf16[256,512]{1,0:T(8,128)(2,1)S(1)} %collective-permute-done.a2_hbm), channel_id=1, source_target_pairs={{0,0},{14,14},{2,4},{4,2},{6,8},{8,6},{10,12},{12,10},{1,1},{15,15... | collective-permute-start | bytes 786440 | tf_op jit(solution)/shard_map/rest/ppermute | solution.py:261
  15.1 0.7 %copy-start.4 = (bf16[256,512]{1,0:T(8,128)(2,1)}, bf16[256,512]{1,0:T(8,128)(2,1)S(1)}, u32[]{:S(2)}) copy-start(bf16[256,512]{1,0:T(8,128)(2,1)S(1)} %collective-permute-done.3.b.b0) | copy-start | bytes 786436
  15.8 1.0 %copy-start.5 = (bf16[256,512]{1,0:T(8,128)(2,1)S(1)}, bf16[256,512]{1,0:T(8,128)(2,1)}, u32[]{:S(2)}) copy-start(bf16[256,512]{1,0:T(8,128)(2,1)} %copy-done.4) | copy-start | bytes 786436
  16.7 1.2 %copy-start.7 = (bf16[1024,512]{1,0:T(8,128)(2,1)S(1)}, bf16[1024,512]{1,0:T(8,128)(2,1)}, u32[]{:S(2)}) copy-start(bf16[1024,512]{1,0:T(8,128)(2,1)} %wq.1) | copy-start | bytes 3145732
  18.5 4.3 %copy-start.3 = (bf16[256,512]{1,0:T(8,128)(2,1)S(1)}, bf16[256,512]{1,0:T(8,128)(2,1)}, u32[]{:S(2)}) copy-start(bf16[256,512]{1,0:T(8,128)(2,1)} %a0.1) | copy-start | bytes 786436
  18.5 4.2 %copy-start.6 = (bf16[256,512]{1,0:T(8,128)(2,1)S(1)}, bf16[256,512]{1,0:T(8,128)(2,1)}, u32[]{:S(2)}) copy-start(bf16[256,512]{1,0:T(8,128)(2,1)} %copy-done.4) | copy-start | bytes 786436
  18.5 4.2 %collective-permute-start.4 = (bf16[8,64,128]{2,1,0:T(8,128)(2,1)S(1)}, bf16[8,64,128]{2,1,0:T(8,128)(2,1)S(1)}, u32[]{:S(2)}, u32[]{:S(2)}) collective-permute-start(bf16[8,64,128]{2,1,0:T(8,128)(2,1)S(1)} %get-tuple-element.23), channel_id=1, source_target_pairs={{0,1},{1,0},{2,3},{3,2},{4,5},{5,4},{6,7},{7,6},{8,9},{9,8},{10,11... | collective-permute-start | bytes 393224 | tf_op jit(solution)/shard_map/down_swap/ppermute | solution.py:265
  21.8 5.0 %collective-permute-start.8 = (bf16[256,512]{1,0:T(8,128)(2,1)}, bf16[256,512]{1,0:T(8,128)(2,1)S(1)}, u32[]{:S(2)}, u32[]{:S(2)}) collective-permute-start(bf16[256,512]{1,0:T(8,128)(2,1)} %collective-permute-done.6.a), channel_id=1, source_target_pairs={{0,1},{1,0},{2,3},{3,2},{4,5},{5,4},{6,7},{7,6},{8,9},{9,8},{10,11... | collective-permute-start | bytes 786440 | tf_op jit(solution)/shard_map/cross_swap/ppermute | solution.py:265
  26.3 3.1 %collective-permute-start.9 = (bf16[256,512]{1,0:T(8,128)(2,1)}, bf16[256,512]{1,0:T(8,128)(2,1)S(1)}, u32[]{:S(2)}, u32[]{:S(2)}) collective-permute-start(bf16[256,512]{1,0:T(8,128)(2,1)} %collective-permute-done.1.a), channel_id=1, source_target_pairs={{0,1},{1,0},{2,3},{3,2},{4,5},{5,4},{6,7},{7,6},{8,9},{9,8},{10,11... | collective-permute-start | bytes 786440 | tf_op jit(solution)/shard_map/rest_swap/ppermute | solution.py:265

commit v5 on v4

--- a/solution.py
+++ b/solution.py
@@ -102,13 +102,13 @@
     return mine, other
 
 
-def query_kernel(a, b, wq, wk, wv, q_ref):
+def query_kernel(a, b, wq, q_ref):
     mine, other = halves(lax.axis_index("head"), a.shape[1])
     queries = (mm(a[...], wq[mine, :]) + mm(b[...], wq[other, :])).astype(BF16)
     q_ref[...] = (queries * jnp.asarray(HD**-0.5, BF16)).T
 
 
-def lower_kernel(got, b_ref, q_ref, reach_ref, half_ref, token_ref):
+def lower_kernel(got, b_ref, q_ref, reach_ref, wk, wv, half_ref, token_ref):
     token_ref[...] = reach_ref[...]
     half_ref[...] = got[:, : half_ref.shape[1], :]
 
@@ -126,7 +126,7 @@
         up_ref[:, c * LANES : (c + 1) * LANES] = piece.reshape(up_ref.shape[0], LANES)
 
 
-def keys_values(a, b, wk, wv, down_ref, up_ref):
+def project(a, b, wk, wv, down_ref, up_ref, keys_ref, turned_ref):
     mine, other = halves(lax.axis_index("head"), a.shape[1])
     first, second = a[...], b[...]
     lowrank = mm(first, down_ref[mine, :]) + mm(second, down_ref[other, :])
@@ -139,12 +139,13 @@
     up = up_ref[...]
     keys = mm(first, wk[mine, :]) + mm(second, wk[other, :]) + mm(low_key, up)
     values = mm(first, wv[mine, :]) + mm(second, wv[other, :]) + mm(low_value, up)
-    return keys.astype(BF16), values.astype(BF16)
-
-
-def attend(q_ref, keys, values, before, after, weights_ref):
-    turned = values.T
-    ones = jnp.ones((16, turned.shape[1]), BF16)
+    keys_ref[...] = keys.astype(BF16)
+    turned_ref[...] = values.astype(BF16).T
+
+
+def attend(q_ref, keys_ref, turned_ref, before, after, weights_ref):
+    keys = keys_ref[...]
+    ones = jnp.ones((16, turned_ref.shape[1]), BF16)
     acc_ref, max_ref = after
     heads = acc_ref.shape[0]
     factors = []
@@ -161,11 +162,25 @@
         weights_ref[i] = jnp.exp(scores - top).astype(BF16)
         max_ref[i : i + 1, :] = top
     for i in range(heads):
-        left = jnp.concatenate([turned[i * HD : (i + 1) * HD, :], ones], axis=0)
+        left = jnp.concatenate([turned_ref[i * HD : (i + 1) * HD, :], ones], axis=0)
         update = mm(left, weights_ref[i])[: acc_ref.shape[1], :]
         if before is not None:
             update = before[0][i] * factors[i] + update
         acc_ref[i] = update
+
+
+def loads(pairs, sems):
+    copies = [pltpu.make_async_copy(x, y, sems.at[k]) for k, (x, y) in enumerate(pairs)]
+
+    def start():
+        for copy in copies:
+            copy.start()
+
+    def wait():
+        for copy in copies:
+            copy.wait()
+
+    return start, wait
 
 
 def finish(acc_ref, out_ref):
@@ -179,13 +194,14 @@
 
 
 def opening_kernel(
-    packed, got, other, reach_ref, a0, b0, a2_hbm, b2_hbm, a1_hbm, b1_hbm, q_ref, wk, wv,
-    acc_ref, max_ref, down_ref, up_ref, token_ref, a2, b2, a1, b1, weights_ref, sems,
+    packed, got, other, reach_ref, a0, b0, a2_any, b2_any, a1_any, b1_any, q_ref, wk, wv,
+    acc_ref, max_ref, keys_ref, turned_ref, down_ref, up_ref, token_ref,
+    a2, b2, a1, b1, weights_ref, sems,
 ):
-    pairs = ((a2_hbm, a2), (b2_hbm, b2), (a1_hbm, a1), (b1_hbm, b1))
-    copies = [pltpu.make_async_copy(x, y, sems.at[k]) for k, (x, y) in enumerate(pairs)]
-    for copy in copies:
-        copy.start()
+    count = reach_ref[0, 0]
+    odd = lax.axis_index("seq") % 2 == 1
+    start, wait = loads(((a2_any, a2), (b2_any, b2), (a1_any, a1), (b1_any, b1)), sems)
+    start()
     token_ref[...] = reach_ref[...]
     if packed:
         unpack(got, other, down_ref, up_ref)
@@ -193,54 +209,69 @@
         down_ref[...] = got[...]
         up_ref[...] = other[...]
     state = (acc_ref, max_ref)
-    keys, values = keys_values(a0, b0, wk, wv, down_ref, up_ref)
-    attend(q_ref, keys, values, None, state, weights_ref)
-    for copy in copies:
-        copy.wait()
+    project(a0, b0, wk, wv, down_ref, up_ref, keys_ref, turned_ref)
+    attend(q_ref, keys_ref, turned_ref, None, state, weights_ref)
+    wait()
+
+    @pl.when(count >= 2)
+    def _():
+        project(a2, b2, wk, wv, down_ref, up_ref, keys_ref, turned_ref)
+
+    @pl.when(odd & (count >= 2))
+    def _():
+        attend(q_ref, keys_ref, turned_ref, state, state, weights_ref)
+
+    @pl.when(odd & (count >= 1))
+    def _():
+        project(a1, b1, wk, wv, down_ref, up_ref, keys_ref, turned_ref)
+
+
+def middle_kernel(
+    reach_ref, ax_any, bx_any, q_ref, wk, wv, down_ref, up_ref, acc_in, max_in, keys_in, turned_in,
+    acc_ref, max_ref, keys_ref, turned_ref, token_ref, a, b, weights_ref, sems,
+):
     count = reach_ref[0, 0]
-
-    @pl.when(count >= 2)
-    def _():
-        keys, values = keys_values(a2, b2, wk, wv, down_ref, up_ref)
-        attend(q_ref, keys, values, state, state, weights_ref)
-
-    @pl.when((lax.axis_index("seq") % 2 == 1) & (count >= 1))
-    def _():
-        keys, values = keys_values(a1, b1, wk, wv, down_ref, up_ref)
-        attend(q_ref, keys, values, state, state, weights_ref)
-
-
-def block_kernel(
-    distances, reach_ref, a, b, q_ref, wk, wv, down_ref, up_ref, acc_in, max_in,
-    acc_ref, max_ref, token_ref, weights_ref,
+    odd = lax.axis_index("seq") % 2 == 1
+    needed = count >= jnp.where(odd, 3, 1)
+    start, wait = loads(((ax_any, a), (bx_any, b)), sems)
+    pl.when(needed)(start)
+    token_ref[...] = reach_ref[...]
+
+    @pl.when(count >= jnp.where(odd, 1, 2))
+    def _():
+        attend(q_ref, keys_in, turned_in, (acc_in, max_in), (acc_ref, max_ref), weights_ref)
+
+    @pl.when(needed)
+    def _():
+        wait()
+        project(a, b, wk, wv, down_ref, up_ref, keys_ref, turned_ref)
+
+
+def closing_kernel(
+    reach_ref, a3_any, b3_any, q_ref, wk, wv, down_ref, up_ref, acc_in, max_in, keys_in, turned_in,
+    out_ref, acc_ref, max_ref, keys_ref, turned_ref, a, b, weights_ref, sems,
 ):
-    odd = lax.axis_index("seq") % 2
-    even_distance, odd_distance = distances
-    distance = jnp.where(odd == 1, odd_distance, even_distance)
-    token_ref[...] = reach_ref[...]
-
-    @pl.when(reach_ref[0, 0] >= distance)
-    def _():
-        keys, values = keys_values(a, b, wk, wv, down_ref, up_ref)
-        attend(q_ref, keys, values, (acc_in, max_in), (acc_ref, max_ref), weights_ref)
-
-
-def closing_kernel(
-    distances, reach_ref, a, b, q_ref, wk, wv, down_ref, up_ref, acc_in, max_in,
-    out_ref, acc_ref, max_ref, weights_ref,
-):
-    odd = lax.axis_index("seq") % 2
-    even_distance, odd_distance = distances
-    distance = jnp.where(odd == 1, odd_distance, even_distance)
-    needed = reach_ref[0, 0] >= distance
-
-    @pl.when(needed)
-    def _():
-        keys, values = keys_values(a, b, wk, wv, down_ref, up_ref)
-        attend(q_ref, keys, values, (acc_in, max_in), (acc_ref, max_ref), weights_ref)
+    count = reach_ref[0, 0]
+    odd = lax.axis_index("seq") % 2 == 1
+    pending = count >= jnp.where(odd, 3, 1)
+    needed = (count >= 3) & jnp.logical_not(odd)
+    start, wait = loads(((a3_any, a), (b3_any, b)), sems)
+    state = (acc_ref, max_ref)
+    pl.when(needed)(start)
+
+    @pl.when(pending)
+    def _():
+        attend(q_ref, keys_in, turned_in, (acc_in, max_in), state, weights_ref)
+
+        @pl.when(needed)
+        def _():
+            wait()
+            project(a, b, wk, wv, down_ref, up_ref, keys_ref, turned_ref)
+            attend(q_ref, keys_ref, turned_ref, state, state, weights_ref)
+
         finish(acc_ref, out_ref)
 
-    @pl.when(jnp.logical_not(needed))
+    @pl.when(jnp.logical_not(pending))
     def _():
         finish(acc_in, out_ref)
 
@@ -269,11 +300,11 @@
     q = pl.pallas_call(
         query_kernel,
         out_shape=jax.ShapeDtypeStruct((columns, rows), BF16),
-        in_specs=[VMEM()] * 5,
+        in_specs=[VMEM()] * 3,
         out_specs=VMEM(),
         compiler_params=params,
         cost_estimate=cost(10),
-    )(a0, b0, w_query, w_key, w_value)
+    )(a0, b0, w_query)
     near = [(i, i ^ 1) for i in range(count)]
     two = [(i, (i + 2) % count) for i in range(count)]
     pairs = [(0, 0), (count - 1, count - 1)]
@@ -294,10 +325,10 @@
                 jax.ShapeDtypeStruct((count, down_bank.shape[1] // 2, LANES), BF16),
                 jax.ShapeDtypeStruct((8, LANES), jnp.int32),
             ),
-            in_specs=[VMEM()] * 4,
+            in_specs=[VMEM()] * 6,
             out_specs=(VMEM(), VMEM()),
             compiler_params=params,
-        )(got, b2, q, reaching)
+        )(got, b2, q, reaching, w_key, w_value)
         other = swap(half, "down")
     else:
         wanted = jnp.take(bank_row, lang_ids, axis=0)
@@ -321,46 +352,49 @@
     )
     weights = pltpu.VMEM((heads, rows, rows), BF16)
     half_frames = pltpu.VMEM((rows, width), BF16)
-    acc, top, down, up, reached = pl.pallas_call(
+    projected = (
+        jax.ShapeDtypeStruct((rows, columns), BF16),
+        jax.ShapeDtypeStruct((columns, rows), BF16),
+    )
+    token = jax.ShapeDtypeStruct((8, LANES), jnp.int32)
+    acc, top, keys, turned, down, up, reached = pl.pallas_call(
         functools.partial(opening_kernel, packed),
         out_shape=state
+        + projected
         + (
             jax.ShapeDtypeStruct((model_width, rank_two), BF16),
             jax.ShapeDtypeStruct((rank_two, columns), BF16),
-            jax.ShapeDtypeStruct((8, LANES), jnp.int32),
+            token,
         ),
         in_specs=[VMEM()] * 5 + [ANY()] * 4 + [VMEM()] * 3,
-        out_specs=(VMEM(),) * 5,
+        out_specs=(VMEM(),) * 7,
         scratch_shapes=[half_frames] * 4 + [weights, pltpu.SemaphoreType.DMA((4,))],
         compiler_params=params,
         cost_estimate=cost(0.1),
-    )(
-        got, other, reaching, a0, b0,
-        *(x for x in (a2, b2, a1, b1)),
-        q, w_key, w_value,
-    )
-    never = LOOK + 1
+    )(got, other, reaching, a0, b0, a2, b2, a1, b1, q, w_key, w_value)
     a3, reached = lax.optimization_barrier((a3, reached))
-    acc, top, reached = pl.pallas_call(
-        functools.partial(block_kernel, (1, 3)),
-        out_shape=state + (jax.ShapeDtypeStruct((8, LANES), jnp.int32),),
-        in_specs=[VMEM()] * 10,
-        out_specs=(VMEM(),) * 3,
-        scratch_shapes=[weights],
+    acc, top, keys, turned, reached = pl.pallas_call(
+        middle_kernel,
+        out_shape=state + projected + (token,),
+        in_specs=[VMEM()] + [ANY()] * 2 + [VMEM()] * 9,
+        out_specs=(VMEM(),) * 5,
+        scratch_shapes=[half_frames] * 2 + [weights, pltpu.SemaphoreType.DMA((2,))],
         input_output_aliases={8: 0, 9: 1},
         compiler_params=params,
         cost_estimate=cost(0.1),
-    )(reached, ax, bx, q, w_key, w_value, down, up, acc, top)
+    )(reached, ax, bx, q, w_key, w_value, down, up, acc, top, keys, turned)
     b3 = swap(a3, "rest")
     return pl.pallas_call(
-        functools.partial(closing_kernel, (3, never)),
+        closing_kernel,
         out_shape=jax.ShapeDtypeStruct((rows, columns), BF16),
-        in_specs=[VMEM()] * 10,
+        in_specs=[VMEM()] + [ANY()] * 2 + [VMEM()] * 9,
         out_specs=VMEM(),
-        scratch_shapes=[pltpu.VMEM(s.shape, F32) for s in state] + [weights],
+        scratch_shapes=[pltpu.VMEM(s.shape, s.dtype) for s in state + projected]
+        + [half_frames] * 2
+        + [weights, pltpu.SemaphoreType.DMA((2,))],
         compiler_params=params,
         cost_estimate=cost(2),
-    )(reached, a3, b3, q, w_key, w_value, down, up, acc, top)
+    )(reached, a3, b3, q, w_key, w_value, down, up, acc, top, keys, turned)
 
 
 def solution(mesh):

time: 31.9 us -> 30.6 us (0.959)
  the two profiles are of different devices: /device:TPU:9 before, /device:TPU:15 now
where the time goes in v5:
time: 30.6 us; the launch traced here: 30.4 us
  starting transfers between devices  14.7 us (48%)
  Pallas kernels  11 us (36%)
  local copies, waits for them, and re-layouts  2.88 us (9%)
  waiting for transfers between devices  0.92 us (3%)
  other arithmetic  0.73 us (2%)
    ppermute x3, starting transfers between devices, permute(): return lax.ppermute(x, 'seq', route)  5.47 us
    pallas_call x1, Pallas kernels, body(): pl.pallas_call(functools.partial(opening_kernel, packed), out_shape=state...  4.8 us
    all_to_all x1, starting transfers between devices, body(): lax.all_to_all(sent[0], 'seq', split_axis=0, concat_axis=0, tiled=True)  4.69 us
    ppermute x6, starting transfers between devices, swap(): return lax.ppermute(x, 'head', [(0, 1), (1, 0)])  3.38 us
    unnamed x16, local copies, waits for them, and re-layouts  2.88 us
    pallas_call x1, Pallas kernels, body(): pl.pallas_call(middle_kernel, out_shape=state + projected + (token,), in_...  2.07 us
    pallas_call x1, Pallas kernels, body(): pl.pallas_call(closing_kernel, out_shape=jax.ShapeDtypeStruct((rows, colu...  1.79 us
    pallas_call x1, Pallas kernels, rules(): pl.pallas_call(functools.partial(rules_kernel, packed), out_shape=out_sha...  1.77 us
  transfers between devices with their start and end apart: 11, of which 1 were waited for; matrix products, arithmetic and copies ran while one was open for 2% of the time, Pallas kernels for 30%

profile of v5, /device:TPU:15, one launch (start us, length us, event | category | flops | bytes accessed | tf_op | source)
XLA Modules:
  0.0 30.4 jit_solution(3032765143652701858)
XLA Ops:
  0.0 1.3 %collective-permute-start = (bf16[256,512]{1,0:T(8,128)(2,1)}, bf16[256,512]{1,0:T(8,128)(2,1)S(1)}, u32[]{:S(2)}, u32[]{:S(2)}) collective-permute-start(bf16[256,512]{1,0:T(8,128)(2,1)} %a0.1), channel_id=1, source_target_pairs={{0,4},{2,6},{4,8},{6,10},{8,12},{10,14},{12,0},{14,2},{1,5},{3,7},... | collective-permute-start | bytes 786440 | tf_op jit(solution)/shard_map/two/ppermute | solution.py:292
  1.3 0.3 collective-permute-start.5
  1.6 1.2 %collective-permute-start.3 = (bf16[256,512]{1,0:T(8,128)(2,1)}, bf16[256,512]{1,0:T(8,128)(2,1)S(1)}, u32[]{:S(2)}, u32[]{:S(2)}) collective-permute-start(bf16[256,512]{1,0:T(8,128)(2,1)} %a0.1), channel_id=1, source_target_pairs={{0,1},{1,0},{2,3},{3,2},{4,5},{5,4},{6,7},{7,6},{8,9},{9,8},{10,11... | collective-permute-start | bytes 786440 | tf_op jit(solution)/shard_map/own_swap/ppermute | solution.py:296
  2.8 1.8 %shard_map.100 = (s32[8,128]{1,0:T(8,128)S(1)}, bf16[8,128,128]{2,1,0:T(8,128)(2,1)}) custom-call(s32[8]{0:T(128)} %row_hbm.1, s32[8]{0:T(128)} %lang_hbm.1, s32[8]{0:T(128)} %seg_hbm.1, s32[8]{0:T(128)} %look_hbm.1, bf16[8,128,128]{2,1,0:T(8,128)(2,1)} %down_hbm.1, bf16[8,16,512]{2,1,0:T(8,128)(2,1)} %up_hbm.1), custom_call_target="tpu_custom_call" | custom-call | flops 2000000000 | tf_op jit(solution)/shard_map/pallas_call | solution.py:83
  4.6 4.7 %all-to-all-start = ((bf16[8,128,128]{2,1,0:T(8,128)(2,1)}), bf16[8,128,128]{2,1,0:T(8,128)(2,1)S(1)}, u32[]{:S(2)}, u32[]{:S(2)}) async-start(bf16[8,128,128]{2,1,0:T(8,128)(2,1)} %get-tuple-element.25), calls=%async_computation | async-start | bytes 524288 | tf_op jit(solution)/shard_map/all_to_all | solution.py:321
  9.3 0.0 collective-permute-done.a2_any
  9.3 0.0 collective-permute-done.5.a1_any
  9.3 0.7 %broadcast_select_fusion = bf16[256,512]{1,0:T(8,128)(2,1)} fusion(bf16[256,512]{1,0:T(8,128)(2,1)S(1)} %collective-permute-done.a2_any, bf16[256,512]{1,0:T(8,128)(2,1)S(1)} %collective-permute-done.5.a1_any, pred[]{:T(512)S(6)} %eq.3), kind=kLoop, calls=%fused_computation | loop fusion | flops 131072 | bytes 786433 | tf_op jit(solution)/shard_map/jit(_where)/select_n | solution.py:341
  10.0 1.2 %collective-permute-start.6 = (bf16[256,512]{1,0:T(8,128)(2,1)}, bf16[256,512]{1,0:T(8,128)(2,1)}, u32[]{:S(2)}, u32[]{:S(2)}) collective-permute-start(bf16[256,512]{1,0:T(8,128)(2,1)} %broadcast_select_fusion), channel_id=1, source_target_pairs={{0,2},{2,0},{4,6},{6,4},{8,10},{10,8},{12,14},{14,12},{1,5},{3,7},... | collective-permute-start | bytes 786440 | tf_op jit(solution)/shard_map/split/ppermute | solution.py:344
  11.2 0.3 collective-permute-start.2
  11.5 0.2 collective-permute-start.7
  11.7 3.9 %collective-permute-start.1 = (bf16[256,512]{1,0:T(8,128)(2,1)S(1)}, bf16[256,512]{1,0:T(8,128)(2,1)}, u32[]{:S(2)}, u32[]{:S(2)}) collective-permute-start(bf16[256,512]{1,0:T(8,128)(2,1)S(1)} %collective-permute-done.a2_any), channel_id=1, source_target_pairs={{0,0},{14,14},{2,4},{4,2},{6,8},{8,6},{10,12},{12,10},{1,1},{15,15... | collective-permute-start | bytes 786440 | tf_op jit(solution)/shard_map/rest/ppermute | solution.py:292
  15.7 0.7 %copy-done.4 = bf16[256,512]{1,0:T(8,128)(2,1)} copy-done((bf16[256,512]{1,0:T(8,128)(2,1)}, bf16[256,512]{1,0:T(8,128)(2,1)S(1)}, u32[]{:S(2)}) %copy-start.4) | copy-done | bytes 262168
  16.3 0.9 %copy-done.5 = bf16[256,512]{1,0:T(8,128)(2,1)S(1)} copy-done((bf16[256,512]{1,0:T(8,128)(2,1)S(1)}, bf16[256,512]{1,0:T(8,128)(2,1)}, u32[]{:S(2)}) %copy-start.5) | copy-done | bytes 262168
  17.3 1.2 %copy-done.7 = bf16[1024,512]{1,0:T(8,128)(2,1)S(1)} copy-done((bf16[1024,512]{1,0:T(8,128)(2,1)S(1)}, bf16[1024,512]{1,0:T(8,128)(2,1)}, u32[]{:S(2)}) %copy-start.7) | copy-done | bytes 1048600
  18.5 0.5 %shard_map.101.q_ref = bf16[512,256]{1,0:T(8,128)(2,1)S(1)} custom-call(bf16[256,512]{1,0:T(8,128)(2,1)S(1)} %copy-done.2, bf16[256,512]{1,0:T(8,128)(2,1)S(1)} %copy-done.5, bf16[1024,512]{1,0:T(8,128)(2,1)S(1)} %copy-done.7), custom_call_target="tpu_custom_call" | custom-call | flops 10000000000 | tf_op jit(solution)/shard_map/pallas_call | solution.py:300
  19.1 0.0 copy-start.3
  19.1 0.9 %collective-permute-start.4 = (bf16[8,64,128]{2,1,0:T(8,128)(2,1)S(1)}, bf16[8,64,128]{2,1,0:T(8,128)(2,1)S(1)}, u32[]{:S(2)}, u32[]{:S(2)}) collective-permute-start(bf16[8,64,128]{2,1,0:T(8,128)(2,1)S(1)} %get-tuple-element.27), channel_id=1, source_target_pairs={{0,1},{1,0},{2,3},{3,2},{4,5},{5,4},{6,7},{7,6},{8,9},{9,8},{10,11... | collective-permute-start | bytes 393224 | tf_op jit(solution)/shard_map/down_swap/ppermute | solution.py:296
  20.0 0.1 collective-permute-start.8
  20.1 0.9 %collective-permute-done.4.other = bf16[8,64,128]{2,1,0:T(8,128)(2,1)S(1)} collective-permute-done((bf16[8,64,128]{2,1,0:T(8,128)(2,1)S(1)}, bf16[8,64,128]{2,1,0:T(8,128)(2,1)S(1)}, u32[]{:S(2)}, u32[]{:S(2)}) %collective-permute-start.4) | collective-permute-done | bytes 131104 | tf_op jit(solution)/shard_map/down_swap/ppermute | solution.py:296
  21.0 4.8 %shard_map.103 = (f32[8,72,256]{2,1,0:T(8,128)S(1)}, f32[8,256]{1,0:T(8,128)S(1)}, bf16[256,512]{1,0:T(8,128)(2,1)S(1)}, bf16[512,256]{1,0:T(8,128)(2,1)S(1)}, b...) custom-call(bf16[8,128,128]{2,1,0:T(8,128)(2,1)S(1)} %all-to-all-done.got, ...), custom_call_target="tpu_custom_call" | custom-call | flops 100000000 | tf_op jit(solution)/shard_map/pallas_call | solution.py:360
  25.8 0.7 %collective-permute-start.9 = (bf16[256,512]{1,0:T(8,128)(2,1)}, bf16[256,512]{1,0:T(8,128)(2,1)S(1)}, u32[]{:S(2)}, u32[]{:S(2)}) collective-permute-start(bf16[256,512]{1,0:T(8,128)(2,1)} %collective-permute-done.1.a3_any), channel_id=1, source_target_pairs={{0,1},{1,0},{2,3},{3,2},{4,5},{5,4},{6,7},{7,6},{8,9},{9,8},{10,11... | collective-permute-start | bytes 786440 | tf_op jit(solution)/shard_map/rest_swap/ppermute | solution.py:296
  26.5 2.1 %shard_map.104 = (f32[8,72,256]{2,1,0:T(8,128)S(1)}, f32[8,256]{1,0:T(8,128)S(1)}, bf16[256,512]{1,0:T(8,128)(2,1)S(1)}, bf16[512,256]{1,0:T(8,128)(2,1)S(1)}, s32[8,128]{1,0:T(8,128)S(1)}) custom-call(s32[8,128]{1,0:T(8,128)S(1)} %get-tuple-element.31.reach_ref, ...), custom_call_target="tpu_custom_call", output_to_operand_aliasing={{0}: (8, {}), {1}: (9, {})} | custom-call | flops 100000000 | tf_op jit(solution)/shard_map/pallas_call | solution.py:376
  28.6 1.8 %shard_map.105 = bf16[256,512]{1,0:T(8,128)(2,1)} custom-call(s32[8,128]{1,0:T(8,128)S(1)} %get-tuple-element.39.reach_ref, bf16[256,512]{1,0:T(8,128)(2,1)} %collective-permute-done.1.a3_any, bf16[256,512]{1,0:T(8,128)(2,1)S(1)} %collective-permute-done.9.b3_any, bf16[512,256]{1,0:T(8,128)(2,1)S(1)} %shard_map.101.q_ref, bf16[1024,512]{1,0:T(8,128)(2,1)S(1)} %copy-done, ...), custom_call_target="tpu_custom_call" | custom-call | flops 2000000000 | tf_op jit(solution)/shard_map/pallas_call | solution.py:387
  (21 shorter events, 0.1 us)
Async XLA Ops:
  0.0 9.3 %collective-permute-start = (bf16[256,512]{1,0:T(8,128)(2,1)}, bf16[256,512]{1,0:T(8,128)(2,1)S(1)}, u32[]{:S(2)}, u32[]{:S(2)}) collective-permute-start(bf16[256,512]{1,0:T(8,128)(2,1)} %a0.1), channel_id=1, source_target_pairs={{0,4},{2,6},{4,8},{6,10},{8,12},{10,14},{12,0},{14,2},{1,5},{3,7},... | collective-permute-start | bytes 786440 | tf_op jit(solution)/shard_map/two/ppermute | solution.py:292
  1.3 8.0 %collective-permute-start.5 = (bf16[256,512]{1,0:T(8,128)(2,1)}, bf16[256,512]{1,0:T(8,128)(2,1)S(1)}, u32[]{:S(2)}, u32[]{:S(2)}) collective-permute-start(bf16[256,512]{1,0:T(8,128)(2,1)} %a0.1), channel_id=1, source_target_pairs={{0,2},{2,0},{4,6},{6,4},{8,10},{10,8},{12,14},{14,12},{1,3},{3,1},... | collective-permute-start | bytes 786440 | tf_op jit(solution)/shard_map/near/ppermute | solution.py:292
  1.6 14.1 %collective-permute-start.3 = (bf16[256,512]{1,0:T(8,128)(2,1)}, bf16[256,512]{1,0:T(8,128)(2,1)S(1)}, u32[]{:S(2)}, u32[]{:S(2)}) collective-permute-start(bf16[256,512]{1,0:T(8,128)(2,1)} %a0.1), channel_id=1, source_target_pairs={{0,1},{1,0},{2,3},{3,2},{4,5},{5,4},{6,7},{7,6},{8,9},{9,8},{10,11... | collective-permute-start | bytes 786440 | tf_op jit(solution)/shard_map/own_swap/ppermute | solution.py:296
  4.6 14.5 %all-to-all-start = ((bf16[8,128,128]{2,1,0:T(8,128)(2,1)}), bf16[8,128,128]{2,1,0:T(8,128)(2,1)S(1)}, u32[]{:S(2)}, u32[]{:S(2)}) async-start(bf16[8,128,128]{2,1,0:T(8,128)(2,1)} %get-tuple-element.25), calls=%async_computation | async-start | bytes 524288 | tf_op jit(solution)/shard_map/all_to_all | solution.py:321
  9.3 7.1 %copy-start.2 = (bf16[256,512]{1,0:T(8,128)(2,1)S(1)}, bf16[256,512]{1,0:T(8,128)(2,1)}, u32[]{:S(2)}) copy-start(bf16[256,512]{1,0:T(8,128)(2,1)} %a0.1) | copy-start | bytes 786436
  10.0 9.0 %copy-start = (bf16[1024,512]{1,0:T(8,128)(2,1)S(1)}, bf16[1024,512]{1,0:T(8,128)(2,1)}, u32[]{:S(2)}) copy-start(bf16[1024,512]{1,0:T(8,128)(2,1)} %wk.7) | copy-start | bytes 3145732
  10.0 9.1 %copy-start.1 = (bf16[1024,512]{1,0:T(8,128)(2,1)S(1)}, bf16[1024,512]{1,0:T(8,128)(2,1)}, u32[]{:S(2)}) copy-start(bf16[1024,512]{1,0:T(8,128)(2,1)} %wv.7) | copy-start | bytes 3145732
  10.0 10.0 %collective-permute-start.6 = (bf16[256,512]{1,0:T(8,128)(2,1)}, bf16[256,512]{1,0:T(8,128)(2,1)}, u32[]{:S(2)}, u32[]{:S(2)}) collective-permute-start(bf16[256,512]{1,0:T(8,128)(2,1)} %broadcast_select_fusion), channel_id=1, source_target_pairs={{0,2},{2,0},{4,6},{6,4},{8,10},{10,8},{12,14},{14,12},{1,5},{3,7},... | collective-permute-start | bytes 786440 | tf_op jit(solution)/shard_map/split/ppermute | solution.py:344
  11.2 7.8 %collective-permute-start.2 = (bf16[256,512]{1,0:T(8,128)(2,1)S(1)}, bf16[256,512]{1,0:T(8,128)(2,1)S(1)}, u32[]{:S(2)}, u32[]{:S(2)}) collective-permute-start(bf16[256,512]{1,0:T(8,128)(2,1)S(1)} %collective-permute-done.a2_any), channel_id=1, source_target_pairs={{0,1},{1,0},{2,3},{3,2},{4,5},{5,4},{6,7},{7,6},{8,9},{9,8},{10,11... | collective-permute-start | bytes 786440 | tf_op jit(solution)/shard_map/two_swap/ppermute | solution.py:296
  11.5 8.6 %collective-permute-start.7 = (bf16[256,512]{1,0:T(8,128)(2,1)S(1)}, bf16[256,512]{1,0:T(8,128)(2,1)}, u32[]{:S(2)}, u32[]{:S(2)}) collective-permute-start(bf16[256,512]{1,0:T(8,128)(2,1)S(1)} %collective-permute-done.5.a1_any), channel_id=1, source_target_pairs={{0,1},{1,0},{2,3},{3,2},{4,5},{5,4},{6,7},{7,6},{8,9},{9,8},{10,11... | collective-permute-start | bytes 786440 | tf_op jit(solution)/shard_map/near_swap/ppermute | solution.py:296
  11.7 14.1 %collective-permute-start.1 = (bf16[256,512]{1,0:T(8,128)(2,1)S(1)}, bf16[256,512]{1,0:T(8,128)(2,1)}, u32[]{:S(2)}, u32[]{:S(2)}) collective-permute-start(bf16[256,512]{1,0:T(8,128)(2,1)S(1)} %collective-permute-done.a2_any), channel_id=1, source_target_pairs={{0,0},{14,14},{2,4},{4,2},{6,8},{8,6},{10,12},{12,10},{1,1},{15,15... | collective-permute-start | bytes 786440 | tf_op jit(solution)/shard_map/rest/ppermute | solution.py:292
  15.6 0.7 %copy-start.4 = (bf16[256,512]{1,0:T(8,128)(2,1)}, bf16[256,512]{1,0:T(8,128)(2,1)S(1)}, u32[]{:S(2)}) copy-start(bf16[256,512]{1,0:T(8,128)(2,1)S(1)} %collective-permute-done.3.b.b0) | copy-start | bytes 786436
  16.3 1.0 %copy-start.5 = (bf16[256,512]{1,0:T(8,128)(2,1)S(1)}, bf16[256,512]{1,0:T(8,128)(2,1)}, u32[]{:S(2)}) copy-start(bf16[256,512]{1,0:T(8,128)(2,1)} %copy-done.4) | copy-start | bytes 786436
  17.3 1.2 %copy-start.7 = (bf16[1024,512]{1,0:T(8,128)(2,1)S(1)}, bf16[1024,512]{1,0:T(8,128)(2,1)}, u32[]{:S(2)}) copy-start(bf16[1024,512]{1,0:T(8,128)(2,1)} %wq.1) | copy-start | bytes 3145732
  19.1 1.9 %copy-start.3 = (bf16[256,512]{1,0:T(8,128)(2,1)S(1)}, bf16[256,512]{1,0:T(8,128)(2,1)}, u32[]{:S(2)}) copy-start(bf16[256,512]{1,0:T(8,128)(2,1)} %a0.1) | copy-start | bytes 786436
  19.1 1.9 %copy-start.6 = (bf16[256,512]{1,0:T(8,128)(2,1)S(1)}, bf16[256,512]{1,0:T(8,128)(2,1)}, u32[]{:S(2)}) copy-start(bf16[256,512]{1,0:T(8,128)(2,1)} %copy-done.4) | copy-start | bytes 786436
  19.1 1.8 %collective-permute-start.4 = (bf16[8,64,128]{2,1,0:T(8,128)(2,1)S(1)}, bf16[8,64,128]{2,1,0:T(8,128)(2,1)S(1)}, u32[]{:S(2)}, u32[]{:S(2)}) collective-permute-start(bf16[8,64,128]{2,1,0:T(8,128)(2,1)S(1)} %get-tuple-element.27), channel_id=1, source_target_pairs={{0,1},{1,0},{2,3},{3,2},{4,5},{5,4},{6,7},{7,6},{8,9},{9,8},{10,11... | collective-permute-start | bytes 393224 | tf_op jit(solution)/shard_map/down_swap/ppermute | solution.py:296
  20.0 6.5 %collective-permute-start.8 = (bf16[256,512]{1,0:T(8,128)(2,1)}, bf16[256,512]{1,0:T(8,128)(2,1)S(1)}, u32[]{:S(2)}, u32[]{:S(2)}) collective-permute-start(bf16[256,512]{1,0:T(8,128)(2,1)} %collective-permute-done.6.ax_any), channel_id=1, source_target_pairs={{0,1},{1,0},{2,3},{3,2},{4,5},{5,4},{6,7},{7,6},{8,9},{9,8},{10,11... | collective-permute-start | bytes 786440 | tf_op jit(solution)/shard_map/cross_swap/ppermute | solution.py:296
  25.8 2.8 %collective-permute-start.9 = (bf16[256,512]{1,0:T(8,128)(2,1)}, bf16[256,512]{1,0:T(8,128)(2,1)S(1)}, u32[]{:S(2)}, u32[]{:S(2)}) collective-permute-start(bf16[256,512]{1,0:T(8,128)(2,1)} %collective-permute-done.1.a3_any), channel_id=1, source_target_pairs={{0,1},{1,0},{2,3},{3,2},{4,5},{5,4},{6,7},{7,6},{8,9},{9,8},{10,11... | collective-permute-start | bytes 786440 | tf_op jit(solution)/shard_map/rest_swap/ppermute | solution.py:296

commit v6 on v5

--- a/solution.py
+++ b/solution.py
@@ -102,13 +102,19 @@
     return mine, other
 
 
-def query_kernel(a, b, wq, q_ref):
+def query_kernel(a_hbm, b_hbm, wq_hbm, q_ref, b, a, wq, sems):
+    pairs = ((a_hbm, a), (b_hbm, b), (wq_hbm, wq))
+    copies = [pltpu.make_async_copy(x, y, sems.at[k]) for k, (x, y) in enumerate(pairs)]
+    for copy in copies:
+        copy.start()
+    for copy in copies:
+        copy.wait()
     mine, other = halves(lax.axis_index("head"), a.shape[1])
     queries = (mm(a[...], wq[mine, :]) + mm(b[...], wq[other, :])).astype(BF16)
     q_ref[...] = (queries * jnp.asarray(HD**-0.5, BF16)).T
 
 
-def lower_kernel(got, b_ref, q_ref, reach_ref, wk, wv, half_ref, token_ref):
+def lower_kernel(got, q_ref, reach_ref, wk, wv, half_ref, token_ref):
     token_ref[...] = reach_ref[...]
     half_ref[...] = got[:, : half_ref.shape[1], :]
 
@@ -297,18 +303,23 @@
 
     a0 = frames
     b0 = swap(a0, "own")
-    q = pl.pallas_call(
+    q, b0 = pl.pallas_call(
         query_kernel,
-        out_shape=jax.ShapeDtypeStruct((columns, rows), BF16),
-        in_specs=[VMEM()] * 3,
-        out_specs=VMEM(),
+        out_shape=(
+            jax.ShapeDtypeStruct((columns, rows), BF16),
+            jax.ShapeDtypeStruct((rows, width), BF16),
+        ),
+        in_specs=[HBM()] * 3,
+        out_specs=(VMEM(), VMEM()),
+        scratch_shapes=[pltpu.VMEM((rows, width), BF16)]
+        + [pltpu.VMEM(w_query.shape, BF16), pltpu.SemaphoreType.DMA((3,))],
         compiler_params=params,
-        cost_estimate=cost(10),
-    )(a0, b0, w_query)
+        cost_estimate=cost(2),
+    )(*(pltpu.with_memory_space_constraint(x, pltpu.HBM) for x in (a0, b0, w_query)))
     near = [(i, i ^ 1) for i in range(count)]
     two = [(i, (i + 2) % count) for i in range(count)]
-    pairs = [(0, 0), (count - 1, count - 1)]
-    pairs += [(i, i + 1 if i % 2 else i - 1) for i in range(1, count - 1)]
+    pairs = [(i, i) for i in (0, 1, 2, count - 1)]
+    pairs += [(i, i + 1 if i % 2 else i - 1) for i in range(3, count - 1)]
 
     a2 = permute(a0, two, "two")
     b2 = swap(a2, "two")
@@ -325,10 +336,10 @@
                 jax.ShapeDtypeStruct((count, down_bank.shape[1] // 2, LANES), BF16),
                 jax.ShapeDtypeStruct((8, LANES), jnp.int32),
             ),
-            in_specs=[VMEM()] * 6,
+            in_specs=[VMEM()] * 5,
             out_specs=(VMEM(), VMEM()),
             compiler_params=params,
-        )(got, b2, q, reaching, w_key, w_value)
+        )(got, q, reaching, w_key, w_value)
         other = swap(half, "down")
     else:
         wanted = jnp.take(bank_row, lang_ids, axis=0)
@@ -393,7 +404,7 @@
         + [half_frames] * 2
         + [weights, pltpu.SemaphoreType.DMA((2,))],
         compiler_params=params,
-        cost_estimate=cost(2),
+        cost_estimate=cost(0.1),
     )(reached, a3, b3, q, w_key, w_value, down, up, acc, top, keys, turned)
 
 

time: 30.6 us -> 31.1 us (1.016)
  the two profiles are of different devices: /device:TPU:15 before, /device:TPU:17 now
where the time goes in v6:
time: 31.1 us; the launch traced here: 30.8 us
  starting transfers between devices  14.6 us (47%)
  Pallas kernels  12.2 us (39%)
  waiting for transfers between devices  3.11 us (10%)
  other arithmetic  0.73 us (2%)
    ppermute x3, starting transfers between devices, permute(): return lax.ppermute(x, 'seq', route)  5.45 us
    ppermute x6, starting transfers between devices, swap(): return lax.ppermute(x, 'head', [(0, 1), (1, 0)])  4.15 us
    all_to_all x1, starting transfers between devices, body(): lax.all_to_all(sent[0], 'seq', split_axis=0, concat_axis=0, tiled=True)  3.78 us
    pallas_call x1, Pallas kernels, body(): pl.pallas_call(closing_kernel, out_shape=jax.ShapeDtypeStruct((rows, colu...  3.58 us
    pallas_call x1, Pallas kernels, body(): pl.pallas_call(functools.partial(opening_kernel, packed), out_shape=state...  2.87 us
    ppermute x3, waiting for transfers between devices, permute(): return lax.ppermute(x, 'seq', route)  2.2 us
    pallas_call x1, Pallas kernels, body(): pl.pallas_call(middle_kernel, out_shape=state + projected + (token,), in_...  2.05 us
    pallas_call x1, Pallas kernels, body(): pl.pallas_call(query_kernel, out_shape=(jax.ShapeDtypeStruct((columns, ro...  1.93 us
  transfers between devices with their start and end apart: 11, of which 2 were waited for; matrix products, arithmetic and copies ran while one was open for 2% of the time, Pallas kernels for 28%

profile of v6, /device:TPU:17, one launch (start us, length us, event | category | flops | bytes accessed | tf_op | source)
XLA Modules:
  0.0 30.8 jit_solution(15584777170889465352)
XLA Ops:
  0.0 1.3 %collective-permute-start = (bf16[256,512]{1,0:T(8,128)(2,1)}, bf16[256,512]{1,0:T(8,128)(2,1)S(1)}, u32[]{:S(2)}, u32[]{:S(2)}) collective-permute-start(bf16[256,512]{1,0:T(8,128)(2,1)} %a0.1), channel_id=1, source_target_pairs={{0,4},{2,6},{4,8},{6,10},{8,12},{10,14},{12,0},{14,2},{1,5},{3,7},... | collective-permute-start | bytes 786440 | tf_op jit(solution)/shard_map/two/ppermute | solution.py:298
  1.3 1.2 %collective-permute-start.4 = (bf16[256,512]{1,0:T(8,128)(2,1)}, bf16[256,512]{1,0:T(8,128)(2,1)S(1)}, u32[]{:S(2)}, u32[]{:S(2)}) collective-permute-start(bf16[256,512]{1,0:T(8,128)(2,1)} %a0.1), channel_id=1, source_target_pairs={{0,2},{2,0},{4,6},{6,4},{8,10},{10,8},{12,14},{14,12},{1,3},{3,1},... | collective-permute-start | bytes 786440 | tf_op jit(solution)/shard_map/near/ppermute | solution.py:298
  2.5 1.8 %shard_map.100 = (s32[8,128]{1,0:T(8,128)S(1)}, bf16[8,128,128]{2,1,0:T(8,128)(2,1)}) custom-call(s32[8]{0:T(128)} %row_hbm.1, s32[8]{0:T(128)} %lang_hbm.1, s32[8]{0:T(128)} %seg_hbm.1, s32[8]{0:T(128)} %look_hbm.1, bf16[8,128,128]{2,1,0:T(8,128)(2,1)} %down_hbm.1, bf16[8,16,512]{2,1,0:T(8,128)(2,1)} %up_hbm.1), custom_call_target="tpu_custom_call" | custom-call | flops 2000000000 | tf_op jit(solution)/shard_map/pallas_call | solution.py:83
  4.3 0.0 copy-start.2
  4.3 3.8 %all-to-all-start = ((bf16[8,128,128]{2,1,0:T(8,128)(2,1)}), bf16[8,128,128]{2,1,0:T(8,128)(2,1)S(1)}, u32[]{:S(2)}, u32[]{:S(2)}) async-start(bf16[8,128,128]{2,1,0:T(8,128)(2,1)} %get-tuple-element.27), calls=%async_computation | async-start | bytes 524288 | tf_op jit(solution)/shard_map/all_to_all | solution.py:332
  8.1 1.8 %collective-permute-start.2 = (bf16[256,512]{1,0:T(8,128)(2,1)S(1)}, bf16[256,512]{1,0:T(8,128)(2,1)}, u32[]{:S(2)}, u32[]{:S(2)}) collective-permute-start(bf16[256,512]{1,0:T(8,128)(2,1)S(1)} %copy-done.2), channel_id=1, source_target_pairs={{0,1},{1,0},{2,3},{3,2},{4,5},{5,4},{6,7},{7,6},{8,9},{9,8},{10,11... | collective-permute-start | bytes 786440 | tf_op jit(solution)/shard_map/own_swap/ppermute | solution.py:302
  9.9 0.0 collective-permute-done.a2_any
  9.9 0.0 collective-permute-done.4.a1_any
  9.9 0.7 %broadcast_select_fusion = bf16[256,512]{1,0:T(8,128)(2,1)} fusion(bf16[256,512]{1,0:T(8,128)(2,1)S(1)} %collective-permute-done.a2_any, bf16[256,512]{1,0:T(8,128)(2,1)S(1)} %collective-permute-done.4.a1_any, pred[]{:T(512)S(6)} %eq.3), kind=kLoop, calls=%fused_computation | loop fusion | flops 131072 | bytes 786433 | tf_op jit(solution)/shard_map/jit(_where)/select_n | solution.py:352
  10.6 1.2 %collective-permute-start.5 = (bf16[256,512]{1,0:T(8,128)(2,1)}, bf16[256,512]{1,0:T(8,128)(2,1)}, u32[]{:S(2)}, u32[]{:S(2)}) collective-permute-start(bf16[256,512]{1,0:T(8,128)(2,1)} %broadcast_select_fusion), channel_id=1, source_target_pairs={{0,2},{2,0},{4,6},{6,4},{8,10},{10,8},{12,14},{14,12},{1,5},{3,7},... | collective-permute-start | bytes 786440 | tf_op jit(solution)/shard_map/split/ppermute | solution.py:355
  11.8 0.6 %collective-permute-start.6 = (bf16[256,512]{1,0:T(8,128)(2,1)S(1)}, bf16[256,512]{1,0:T(8,128)(2,1)}, u32[]{:S(2)}, u32[]{:S(2)}) collective-permute-start(bf16[256,512]{1,0:T(8,128)(2,1)S(1)} %collective-permute-done.a2_any), channel_id=1, source_target_pairs={{0,1},{1,0},{2,3},{3,2},{4,5},{5,4},{6,7},{7,6},{8,9},{9,8},{10,11... | collective-permute-start | bytes 786440 | tf_op jit(solution)/shard_map/two_swap/ppermute | solution.py:302
  12.5 0.0 collective-permute-start.7
  12.5 2.9 %collective-permute-start.1 = (bf16[256,512]{1,0:T(8,128)(2,1)S(1)}, bf16[256,512]{1,0:T(8,128)(2,1)}, u32[]{:S(2)}, u32[]{:S(2)}) collective-permute-start(bf16[256,512]{1,0:T(8,128)(2,1)S(1)} %collective-permute-done.a2_any), channel_id=1, source_target_pairs={{0,0},{2,2},{4,4},{14,14},{6,8},{8,6},{10,12},{12,10},{1,1},{3,3},... | collective-permute-start | bytes 786440 | tf_op jit(solution)/shard_map/rest/ppermute | solution.py:298
  15.4 1.9 %shard_map.101 = (bf16[512,256]{1,0:T(8,128)(2,1)S(1)}, bf16[256,512]{1,0:T(8,128)(2,1)S(1)}) custom-call(bf16[256,512]{1,0:T(8,128)(2,1)} %a0.1, bf16[256,512]{1,0:T(8,128)(2,1)} %collective-permute-done.2.b_hbm, bf16[1024,512]{1,0:T(8,128)(2,1)} %wq_hbm.1), custom_call_target="tpu_custom_call" | custom-call | flops 2000000000 | tf_op jit(solution)/shard_map/pallas_call | solution.py:306
  17.4 0.0 all-to-all-done.got
  17.4 0.0 copy-start.3
  17.4 1.2 %collective-permute-start.3 = (bf16[8,64,128]{2,1,0:T(8,128)(2,1)S(1)}, bf16[8,64,128]{2,1,0:T(8,128)(2,1)S(1)}, u32[]{:S(2)}, u32[]{:S(2)}) collective-permute-start(bf16[8,64,128]{2,1,0:T(8,128)(2,1)S(1)} %get-tuple-element.30), channel_id=1, source_target_pairs={{0,1},{1,0},{2,3},{3,2},{4,5},{5,4},{6,7},{7,6},{8,9},{9,8},{10,11... | collective-permute-start | bytes 393224 | tf_op jit(solution)/shard_map/down_swap/ppermute | solution.py:302
  18.6 0.1 collective-permute-start.8
  18.7 0.9 %collective-permute-done.3.other = bf16[8,64,128]{2,1,0:T(8,128)(2,1)S(1)} collective-permute-done((bf16[8,64,128]{2,1,0:T(8,128)(2,1)S(1)}, bf16[8,64,128]{2,1,0:T(8,128)(2,1)S(1)}, u32[]{:S(2)}, u32[]{:S(2)}) %collective-permute-start.3) | collective-permute-done | bytes 131104 | tf_op jit(solution)/shard_map/down_swap/ppermute | solution.py:302
  19.6 2.9 %shard_map.103 = (f32[8,72,256]{2,1,0:T(8,128)S(1)}, f32[8,256]{1,0:T(8,128)S(1)}, bf16[256,512]{1,0:T(8,128)(2,1)S(1)}, bf16[512,256]{1,0:T(8,128)(2,1)S(1)}, b...) custom-call(bf16[8,128,128]{2,1,0:T(8,128)(2,1)S(1)} %all-to-all-done.got, ...), custom_call_target="tpu_custom_call" | custom-call | flops 100000000 | tf_op jit(solution)/shard_map/pallas_call | solution.py:371
  22.5 2.2 %collective-permute-done.1.a3_any = bf16[256,512]{1,0:T(8,128)(2,1)} collective-permute-done((bf16[256,512]{1,0:T(8,128)(2,1)S(1)}, bf16[256,512]{1,0:T(8,128)(2,1)}, u32[]{:S(2)}, u32[]{:S(2)}) %collective-permute-start.1) | collective-permute-done | bytes 262176 | tf_op jit(solution)/shard_map/rest/ppermute | solution.py:298
  24.7 0.4 %collective-permute-start.9 = (bf16[256,512]{1,0:T(8,128)(2,1)}, bf16[256,512]{1,0:T(8,128)(2,1)S(1)}, u32[]{:S(2)}, u32[]{:S(2)}) collective-permute-start(bf16[256,512]{1,0:T(8,128)(2,1)} %collective-permute-done.1.a3_any), channel_id=1, source_target_pairs={{0,1},{1,0},{2,3},{3,2},{4,5},{5,4},{6,7},{7,6},{8,9},{9,8},{10,11... | collective-permute-start | bytes 786440 | tf_op jit(solution)/shard_map/rest_swap/ppermute | solution.py:302
  25.1 2.1 %shard_map.104 = (f32[8,72,256]{2,1,0:T(8,128)S(1)}, f32[8,256]{1,0:T(8,128)S(1)}, bf16[256,512]{1,0:T(8,128)(2,1)S(1)}, bf16[512,256]{1,0:T(8,128)(2,1)S(1)}, s32[8,128]{1,0:T(8,128)S(1)}) custom-call(s32[8,128]{1,0:T(8,128)S(1)} %get-tuple-element.35.reach_ref, ...), custom_call_target="tpu_custom_call", output_to_operand_aliasing={{0}: (8, {}), {1}: (9, {})} | custom-call | flops 100000000 | tf_op jit(solution)/shard_map/pallas_call | solution.py:387
  27.2 3.6 %shard_map.105 = bf16[256,512]{1,0:T(8,128)(2,1)} custom-call(s32[8,128]{1,0:T(8,128)S(1)} %get-tuple-element.43.reach_ref, bf16[256,512]{1,0:T(8,128)(2,1)} %collective-permute-done.1.a3_any, bf16[256,512]{1,0:T(8,128)(2,1)S(1)} %collective-permute-done.9.b3_any, bf16[512,256]{1,0:T(8,128)(2,1)S(1)} %get-tuple-element.28.q_ref, ...), custom_call_target="tpu_custom_call" | custom-call | flops 100000000 | tf_op jit(solution)/shard_map/pallas_call | solution.py:398
  (13 shorter events, 0.0 us)
Async XLA Ops:
  0.0 9.9 %collective-permute-start = (bf16[256,512]{1,0:T(8,128)(2,1)}, bf16[256,512]{1,0:T(8,128)(2,1)S(1)}, u32[]{:S(2)}, u32[]{:S(2)}) collective-permute-start(bf16[256,512]{1,0:T(8,128)(2,1)} %a0.1), channel_id=1, source_target_pairs={{0,4},{2,6},{4,8},{6,10},{8,12},{10,14},{12,0},{14,2},{1,5},{3,7},... | collective-permute-start | bytes 786440 | tf_op jit(solution)/shard_map/two/ppermute | solution.py:298
  1.3 8.6 %collective-permute-start.4 = (bf16[256,512]{1,0:T(8,128)(2,1)}, bf16[256,512]{1,0:T(8,128)(2,1)S(1)}, u32[]{:S(2)}, u32[]{:S(2)}) collective-permute-start(bf16[256,512]{1,0:T(8,128)(2,1)} %a0.1), channel_id=1, source_target_pairs={{0,2},{2,0},{4,6},{6,4},{8,10},{10,8},{12,14},{14,12},{1,3},{3,1},... | collective-permute-start | bytes 786440 | tf_op jit(solution)/shard_map/near/ppermute | solution.py:298
  4.3 3.8 %copy-start.2 = (bf16[256,512]{1,0:T(8,128)(2,1)S(1)}, bf16[256,512]{1,0:T(8,128)(2,1)}, u32[]{:S(2)}) copy-start(bf16[256,512]{1,0:T(8,128)(2,1)} %a0.1) | copy-start | bytes 786436
  4.3 13.1 %all-to-all-start = ((bf16[8,128,128]{2,1,0:T(8,128)(2,1)}), bf16[8,128,128]{2,1,0:T(8,128)(2,1)S(1)}, u32[]{:S(2)}, u32[]{:S(2)}) async-start(bf16[8,128,128]{2,1,0:T(8,128)(2,1)} %get-tuple-element.27), calls=%async_computation | async-start | bytes 524288 | tf_op jit(solution)/shard_map/all_to_all | solution.py:332
  8.1 7.3 %collective-permute-start.2 = (bf16[256,512]{1,0:T(8,128)(2,1)S(1)}, bf16[256,512]{1,0:T(8,128)(2,1)}, u32[]{:S(2)}, u32[]{:S(2)}) collective-permute-start(bf16[256,512]{1,0:T(8,128)(2,1)S(1)} %copy-done.2), channel_id=1, source_target_pairs={{0,1},{1,0},{2,3},{3,2},{4,5},{5,4},{6,7},{7,6},{8,9},{9,8},{10,11... | collective-permute-start | bytes 786440 | tf_op jit(solution)/shard_map/own_swap/ppermute | solution.py:302
  10.6 6.7 %copy-start = (bf16[1024,512]{1,0:T(8,128)(2,1)S(1)}, bf16[1024,512]{1,0:T(8,128)(2,1)}, u32[]{:S(2)}) copy-start(bf16[1024,512]{1,0:T(8,128)(2,1)} %wk.7) | copy-start | bytes 3145732
  10.6 6.8 %copy-start.1 = (bf16[1024,512]{1,0:T(8,128)(2,1)S(1)}, bf16[1024,512]{1,0:T(8,128)(2,1)}, u32[]{:S(2)}) copy-start(bf16[1024,512]{1,0:T(8,128)(2,1)} %wv.7) | copy-start | bytes 3145732
  10.6 8.0 %collective-permute-start.5 = (bf16[256,512]{1,0:T(8,128)(2,1)}, bf16[256,512]{1,0:T(8,128)(2,1)}, u32[]{:S(2)}, u32[]{:S(2)}) collective-permute-start(bf16[256,512]{1,0:T(8,128)(2,1)} %broadcast_select_fusion), channel_id=1, source_target_pairs={{0,2},{2,0},{4,6},{6,4},{8,10},{10,8},{12,14},{14,12},{1,5},{3,7},... | collective-permute-start | bytes 786440 | tf_op jit(solution)/shard_map/split/ppermute | solution.py:355
  11.8 6.9 %collective-permute-start.6 = (bf16[256,512]{1,0:T(8,128)(2,1)S(1)}, bf16[256,512]{1,0:T(8,128)(2,1)}, u32[]{:S(2)}, u32[]{:S(2)}) collective-permute-start(bf16[256,512]{1,0:T(8,128)(2,1)S(1)} %collective-permute-done.a2_any), channel_id=1, source_target_pairs={{0,1},{1,0},{2,3},{3,2},{4,5},{5,4},{6,7},{7,6},{8,9},{9,8},{10,11... | collective-permute-start | bytes 786440 | tf_op jit(solution)/shard_map/two_swap/ppermute | solution.py:302
  12.5 6.3 %collective-permute-start.7 = (bf16[256,512]{1,0:T(8,128)(2,1)S(1)}, bf16[256,512]{1,0:T(8,128)(2,1)}, u32[]{:S(2)}, u32[]{:S(2)}) collective-permute-start(bf16[256,512]{1,0:T(8,128)(2,1)S(1)} %collective-permute-done.4.a1_any), channel_id=1, source_target_pairs={{0,1},{1,0},{2,3},{3,2},{4,5},{5,4},{6,7},{7,6},{8,9},{9,8},{10,11... | collective-permute-start | bytes 786440 | tf_op jit(solution)/shard_map/near_swap/ppermute | solution.py:302
  12.5 12.2 %collective-permute-start.1 = (bf16[256,512]{1,0:T(8,128)(2,1)S(1)}, bf16[256,512]{1,0:T(8,128)(2,1)}, u32[]{:S(2)}, u32[]{:S(2)}) collective-permute-start(bf16[256,512]{1,0:T(8,128)(2,1)S(1)} %collective-permute-done.a2_any), channel_id=1, source_target_pairs={{0,0},{2,2},{4,4},{14,14},{6,8},{8,6},{10,12},{12,10},{1,1},{3,3},... | collective-permute-start | bytes 786440 | tf_op jit(solution)/shard_map/rest/ppermute | solution.py:298
  17.4 2.2 %copy-start.3 = (bf16[256,512]{1,0:T(8,128)(2,1)S(1)}, bf16[256,512]{1,0:T(8,128)(2,1)}, u32[]{:S(2)}) copy-start(bf16[256,512]{1,0:T(8,128)(2,1)} %a0.1) | copy-start | bytes 786436
  17.4 2.2 %collective-permute-start.3 = (bf16[8,64,128]{2,1,0:T(8,128)(2,1)S(1)}, bf16[8,64,128]{2,1,0:T(8,128)(2,1)S(1)}, u32[]{:S(2)}, u32[]{:S(2)}) collective-permute-start(bf16[8,64,128]{2,1,0:T(8,128)(2,1)S(1)} %get-tuple-element.30), channel_id=1, source_target_pairs={{0,1},{1,0},{2,3},{3,2},{4,5},{5,4},{6,7},{7,6},{8,9},{9,8},{10,11... | collective-permute-start | bytes 393224 | tf_op jit(solution)/shard_map/down_swap/ppermute | solution.py:302
  18.6 6.5 %collective-permute-start.8 = (bf16[256,512]{1,0:T(8,128)(2,1)}, bf16[256,512]{1,0:T(8,128)(2,1)S(1)}, u32[]{:S(2)}, u32[]{:S(2)}) collective-permute-start(bf16[256,512]{1,0:T(8,128)(2,1)} %collective-permute-done.5.ax_any), channel_id=1, source_target_pairs={{0,1},{1,0},{2,3},{3,2},{4,5},{5,4},{6,7},{7,6},{8,9},{9,8},{10,11... | collective-permute-start | bytes 786440 | tf_op jit(solution)/shard_map/cross_swap/ppermute | solution.py:302
  24.7 2.5 %collective-permute-start.9 = (bf16[256,512]{1,0:T(8,128)(2,1)}, bf16[256,512]{1,0:T(8,128)(2,1)S(1)}, u32[]{:S(2)}, u32[]{:S(2)}) collective-permute-start(bf16[256,512]{1,0:T(8,128)(2,1)} %collective-permute-done.1.a3_any), channel_id=1, source_target_pairs={{0,1},{1,0},{2,3},{3,2},{4,5},{5,4},{6,7},{7,6},{8,9},{9,8},{10,11... | collective-permute-start | bytes 786440 | tf_op jit(solution)/shard_map/rest_swap/ppermute | solution.py:302

commit v7 on v6

--- a/solution.py
+++ b/solution.py
@@ -132,10 +132,14 @@
         up_ref[:, c * LANES : (c + 1) * LANES] = piece.reshape(up_ref.shape[0], LANES)
 
 
-def project(a, b, wk, wv, down_ref, up_ref, keys_ref, turned_ref):
+def project(a, b, wk, wv, down_ref, up_ref, keys_ref, turned_ref, wait=lambda: None):
     mine, other = halves(lax.axis_index("head"), a.shape[1])
-    first, second = a[...], b[...]
-    lowrank = mm(first, down_ref[mine, :]) + mm(second, down_ref[other, :])
+    first = a[...]
+    keys, values = mm(first, wk[mine, :]), mm(first, wv[mine, :])
+    lowrank = mm(first, down_ref[mine, :])
+    wait()
+    second = b[...]
+    lowrank = lowrank + mm(second, down_ref[other, :])
     lowrank = lowrank.astype(BF16)
     lane = lax.broadcasted_iota(jnp.int32, lowrank.shape, 1)
     split = lowrank.shape[1] // 2
@@ -143,8 +147,8 @@
     low_key = jnp.where(lane < split, lowrank, zero)
     low_value = jnp.where(lane < split, zero, lowrank)
     up = up_ref[...]
-    keys = mm(first, wk[mine, :]) + mm(second, wk[other, :]) + mm(low_key, up)
-    values = mm(first, wv[mine, :]) + mm(second, wv[other, :]) + mm(low_value, up)
+    keys = keys + mm(second, wk[other, :]) + mm(low_key, up)
+    values = values + mm(second, wv[other, :]) + mm(low_value, up)
     keys_ref[...] = keys.astype(BF16)
     turned_ref[...] = values.astype(BF16).T
 
@@ -159,14 +163,19 @@
         q = q_ref[i * HD : (i + 1) * HD, :]
         zero = jnp.zeros_like(q)
         q = jnp.concatenate([q, zero] if i % 2 == 0 else [zero, q], axis=0)
-        scores = mm(keys[:, i // 2 * LANES : (i // 2 + 1) * LANES], q)
-        top = jnp.max(scores, axis=0, keepdims=True)
+        parts = []
+        for first in range(0, q.shape[1], LANES):
+            cols = slice(first, first + LANES)
+            scores = mm(keys[:, i // 2 * LANES : (i // 2 + 1) * LANES], q[:, cols])
+            top = jnp.max(scores, axis=0, keepdims=True)
+            if before is not None:
+                old = before[1][i : i + 1, cols]
+                top = jnp.maximum(top, old)
+                parts.append(jnp.exp(old - top))
+            weights_ref[i, :, cols] = jnp.exp(scores - top).astype(BF16)
+            max_ref[i : i + 1, cols] = top
         if before is not None:
-            old = before[1][i : i + 1, :]
-            top = jnp.maximum(top, old)
-            factors.append(jnp.exp(old - top))
-        weights_ref[i] = jnp.exp(scores - top).astype(BF16)
-        max_ref[i : i + 1, :] = top
+            factors.append(jnp.concatenate(parts, axis=1))
     for i in range(heads):
         left = jnp.concatenate([turned_ref[i * HD : (i + 1) * HD, :], ones], axis=0)
         update = mm(left, weights_ref[i])[: acc_ref.shape[1], :]
@@ -200,14 +209,16 @@
 
 
 def opening_kernel(
-    packed, got, other, reach_ref, a0, b0, a2_any, b2_any, a1_any, b1_any, q_ref, wk, wv,
-    acc_ref, max_ref, keys_ref, turned_ref, down_ref, up_ref, token_ref,
-    a2, b2, a1, b1, weights_ref, sems,
+    packed, got, other, reach_ref, a0, b0, a2_any, b2_any, a1_any, b1_any, ax_any, q_ref, wk, wv,
+    acc_ref, max_ref, down_ref, up_ref, ax_ref, token_ref,
+    a2, b2, a1, b1, keys_ref, turned_ref, weights_ref, sems, sems_x,
 ):
     count = reach_ref[0, 0]
     odd = lax.axis_index("seq") % 2 == 1
     start, wait = loads(((a2_any, a2), (b2_any, b2), (a1_any, a1), (b1_any, b1)), sems)
+    start_x, wait_x = loads(((ax_any, ax_ref),), sems_x)
     start()
+    start_x()
     token_ref[...] = reach_ref[...]
     if packed:
         unpack(got, other, down_ref, up_ref)
@@ -223,34 +234,27 @@
     def _():
         project(a2, b2, wk, wv, down_ref, up_ref, keys_ref, turned_ref)
 
-    @pl.when(odd & (count >= 2))
-    def _():
         attend(q_ref, keys_ref, turned_ref, state, state, weights_ref)
 
     @pl.when(odd & (count >= 1))
     def _():
         project(a1, b1, wk, wv, down_ref, up_ref, keys_ref, turned_ref)
+        attend(q_ref, keys_ref, turned_ref, state, state, weights_ref)
+
+    wait_x()
 
 
 def middle_kernel(
-    reach_ref, ax_any, bx_any, q_ref, wk, wv, down_ref, up_ref, acc_in, max_in, keys_in, turned_in,
-    acc_ref, max_ref, keys_ref, turned_ref, token_ref, a, b, weights_ref, sems,
+    reach_ref, ax, bx_any, wk, wv, down_ref, up_ref, keys_ref, turned_ref, token_ref, b, sems
 ):
-    count = reach_ref[0, 0]
     odd = lax.axis_index("seq") % 2 == 1
-    needed = count >= jnp.where(odd, 3, 1)
-    start, wait = loads(((ax_any, a), (bx_any, b)), sems)
-    pl.when(needed)(start)
     token_ref[...] = reach_ref[...]
 
-    @pl.when(count >= jnp.where(odd, 1, 2))
+    @pl.when(reach_ref[0, 0] >= jnp.where(odd, 3, 1))
     def _():
-        attend(q_ref, keys_in, turned_in, (acc_in, max_in), (acc_ref, max_ref), weights_ref)
-
-    @pl.when(needed)
-    def _():
-        wait()
-        project(a, b, wk, wv, down_ref, up_ref, keys_ref, turned_ref)
+        start, wait = loads(((bx_any, b),), sems)
+        start()
+        project(ax, b, wk, wv, down_ref, up_ref, keys_ref, turned_ref, wait)
 
 
 def closing_kernel(
@@ -368,32 +372,33 @@
         jax.ShapeDtypeStruct((columns, rows), BF16),
     )
     token = jax.ShapeDtypeStruct((8, LANES), jnp.int32)
-    acc, top, keys, turned, down, up, reached = pl.pallas_call(
+    acc, top, down, up, ax, reached = pl.pallas_call(
         functools.partial(opening_kernel, packed),
         out_shape=state
-        + projected
         + (
             jax.ShapeDtypeStruct((model_width, rank_two), BF16),
             jax.ShapeDtypeStruct((rank_two, columns), BF16),
+            jax.ShapeDtypeStruct((rows, width), BF16),
             token,
         ),
-        in_specs=[VMEM()] * 5 + [ANY()] * 4 + [VMEM()] * 3,
-        out_specs=(VMEM(),) * 7,
-        scratch_shapes=[half_frames] * 4 + [weights, pltpu.SemaphoreType.DMA((4,))],
+        in_specs=[VMEM()] * 5 + [ANY()] * 5 + [VMEM()] * 3,
+        out_specs=(VMEM(),) * 6,
+        scratch_shapes=[half_frames] * 4
+        + [pltpu.VMEM(s.shape, s.dtype) for s in projected]
+        + [weights, pltpu.SemaphoreType.DMA((4,)), pltpu.SemaphoreType.DMA((1,))],
         compiler_params=params,
         cost_estimate=cost(0.1),
-    )(got, other, reaching, a0, b0, a2, b2, a1, b1, q, w_key, w_value)
+    )(got, other, reaching, a0, b0, a2, b2, a1, b1, ax, q, w_key, w_value)
     a3, reached = lax.optimization_barrier((a3, reached))
-    acc, top, keys, turned, reached = pl.pallas_call(
+    keys, turned, reached = pl.pallas_call(
         middle_kernel,
-        out_shape=state + projected + (token,),
-        in_specs=[VMEM()] + [ANY()] * 2 + [VMEM()] * 9,
-        out_specs=(VMEM(),) * 5,
-        scratch_shapes=[half_frames] * 2 + [weights, pltpu.SemaphoreType.DMA((2,))],
-        input_output_aliases={8: 0, 9: 1},
+        out_shape=projected + (token,),
+        in_specs=[VMEM()] * 2 + [ANY()] + [VMEM()] * 4,
+        out_specs=(VMEM(),) * 3,
+        scratch_shapes=[half_frames, pltpu.SemaphoreType.DMA((1,))],
         compiler_params=params,
         cost_estimate=cost(0.1),
-    )(reached, ax, bx, q, w_key, w_value, down, up, acc, top, keys, turned)
+    )(reached, ax, bx, w_key, w_value, down, up)
     b3 = swap(a3, "rest")
     return pl.pallas_call(
         closing_kernel,

time: 31.1 us -> 30.3 us (0.974)
  waiting for transfers between devices: 3.11 us -> 2.67 us
    pallas_call x1, Pallas kernels: 2.05 us -> 1.2 us  [body(): pl.pallas_call(middle_kernel, out_shape=projected + (token,), in_specs=[V...]
    ppermute x3, waiting for transfers between devices: 2.2 us -> 1.6 us  [permute(): return lax.ppermute(x, 'seq', route)]
    pallas_call x1, Pallas kernels: 2.87 us -> 3.47 us  [body(): pl.pallas_call(functools.partial(opening_kernel, packed), out_shape=state...]
  transfers between devices with their start and end apart: 11 -> 11, of which waited for: 2 -> 3; matrix products, arithmetic and copies ran while one was open for 2% -> 2% of each run, Pallas kernels for 28% -> 28%
where the time goes in v7:
time: 30.3 us; the launch traced here: 30 us
  starting transfers between devices  14.6 us (48%)
  Pallas kernels  11.9 us (39%)
  waiting for transfers between devices  2.67 us (9%)
  other arithmetic  0.73 us (2%)
    ppermute x3, starting transfers between devices, permute(): return lax.ppermute(x, 'seq', route)  5.45 us
    ppermute x6, starting transfers between devices, swap(): return lax.ppermute(x, 'head', [(0, 1), (1, 0)])  4.15 us
    all_to_all x1, starting transfers between devices, body(): lax.all_to_all(sent[0], 'seq', split_axis=0, concat_axis=0, tiled=True)  3.78 us
    pallas_call x1, Pallas kernels, body(): pl.pallas_call(closing_kernel, out_shape=jax.ShapeDtypeStruct((rows, colu...  3.49 us
    pallas_call x1, Pallas kernels, body(): pl.pallas_call(functools.partial(opening_kernel, packed), out_shape=state...  3.47 us
    pallas_call x1, Pallas kernels, body(): pl.pallas_call(query_kernel, out_shape=(jax.ShapeDtypeStruct((columns, ro...  1.93 us
    pallas_call x1, Pallas kernels, rules(): pl.pallas_call(functools.partial(rules_kernel, packed), out_shape=out_sha...  1.77 us
    ppermute x3, waiting for transfers between devices, permute(): return lax.ppermute(x, 'seq', route)  1.6 us
  transfers between devices with their start and end apart: 11, of which 3 were waited for; matrix products, arithmetic and copies ran while one was open for 2% of the time, Pallas kernels for 28%

profile of v7, /device:TPU:17, one launch (start us, length us, event | category | flops | bytes accessed | tf_op | source)
XLA Modules:
  0.0 30.0 jit_solution(8708567469363707939)
XLA Ops:
  0.0 1.3 %collective-permute-start = (bf16[256,512]{1,0:T(8,128)(2,1)}, bf16[256,512]{1,0:T(8,128)(2,1)S(1)}, u32[]{:S(2)}, u32[]{:S(2)}) collective-permute-start(bf16[256,512]{1,0:T(8,128)(2,1)} %a0.1), channel_id=1, source_target_pairs={{0,4},{2,6},{4,8},{6,10},{8,12},{10,14},{12,0},{14,2},{1,5},{3,7},... | collective-permute-start | bytes 786440 | tf_op jit(solution)/shard_map/two/ppermute | solution.py:302
  1.3 1.2 %collective-permute-start.4 = (bf16[256,512]{1,0:T(8,128)(2,1)}, bf16[256,512]{1,0:T(8,128)(2,1)S(1)}, u32[]{:S(2)}, u32[]{:S(2)}) collective-permute-start(bf16[256,512]{1,0:T(8,128)(2,1)} %a0.1), channel_id=1, source_target_pairs={{0,2},{2,0},{4,6},{6,4},{8,10},{10,8},{12,14},{14,12},{1,3},{3,1},... | collective-permute-start | bytes 786440 | tf_op jit(solution)/shard_map/near/ppermute | solution.py:302
  2.5 1.8 %shard_map.100 = (s32[8,128]{1,0:T(8,128)S(1)}, bf16[8,128,128]{2,1,0:T(8,128)(2,1)}) custom-call(s32[8]{0:T(128)} %row_hbm.1, s32[8]{0:T(128)} %lang_hbm.1, s32[8]{0:T(128)} %seg_hbm.1, s32[8]{0:T(128)} %look_hbm.1, bf16[8,128,128]{2,1,0:T(8,128)(2,1)} %down_hbm.1, bf16[8,16,512]{2,1,0:T(8,128)(2,1)} %up_hbm.1), custom_call_target="tpu_custom_call" | custom-call | flops 2000000000 | tf_op jit(solution)/shard_map/pallas_call | solution.py:83
  4.3 0.0 copy-start.2
  4.3 3.8 %all-to-all-start = ((bf16[8,128,128]{2,1,0:T(8,128)(2,1)}), bf16[8,128,128]{2,1,0:T(8,128)(2,1)S(1)}, u32[]{:S(2)}, u32[]{:S(2)}) async-start(bf16[8,128,128]{2,1,0:T(8,128)(2,1)} %get-tuple-element.24), calls=%async_computation | async-start | bytes 524288 | tf_op jit(solution)/shard_map/all_to_all | solution.py:336
  8.1 1.8 %collective-permute-start.2 = (bf16[256,512]{1,0:T(8,128)(2,1)S(1)}, bf16[256,512]{1,0:T(8,128)(2,1)}, u32[]{:S(2)}, u32[]{:S(2)}) collective-permute-start(bf16[256,512]{1,0:T(8,128)(2,1)S(1)} %copy-done.2), channel_id=1, source_target_pairs={{0,1},{1,0},{2,3},{3,2},{4,5},{5,4},{6,7},{7,6},{8,9},{9,8},{10,11... | collective-permute-start | bytes 786440 | tf_op jit(solution)/shard_map/own_swap/ppermute | solution.py:306
  9.9 0.0 collective-permute-done.a2_any
  9.9 0.0 collective-permute-done.4.a1_any
  9.9 0.7 %broadcast_select_fusion = bf16[256,512]{1,0:T(8,128)(2,1)} fusion(bf16[256,512]{1,0:T(8,128)(2,1)S(1)} %collective-permute-done.a2_any, bf16[256,512]{1,0:T(8,128)(2,1)S(1)} %collective-permute-done.4.a1_any, pred[]{:T(512)S(6)} %eq.3), kind=kLoop, calls=%fused_computation | loop fusion | flops 131072 | bytes 786433 | tf_op jit(solution)/shard_map/jit(_where)/select_n | solution.py:356
  10.6 1.2 %collective-permute-start.5 = (bf16[256,512]{1,0:T(8,128)(2,1)}, bf16[256,512]{1,0:T(8,128)(2,1)}, u32[]{:S(2)}, u32[]{:S(2)}) collective-permute-start(bf16[256,512]{1,0:T(8,128)(2,1)} %broadcast_select_fusion), channel_id=1, source_target_pairs={{0,2},{2,0},{4,6},{6,4},{8,10},{10,8},{12,14},{14,12},{1,5},{3,7},... | collective-permute-start | bytes 786440 | tf_op jit(solution)/shard_map/split/ppermute | solution.py:359
  11.8 0.6 %collective-permute-start.6 = (bf16[256,512]{1,0:T(8,128)(2,1)S(1)}, bf16[256,512]{1,0:T(8,128)(2,1)}, u32[]{:S(2)}, u32[]{:S(2)}) collective-permute-start(bf16[256,512]{1,0:T(8,128)(2,1)S(1)} %collective-permute-done.a2_any), channel_id=1, source_target_pairs={{0,1},{1,0},{2,3},{3,2},{4,5},{5,4},{6,7},{7,6},{8,9},{9,8},{10,11... | collective-permute-start | bytes 786440 | tf_op jit(solution)/shard_map/two_swap/ppermute | solution.py:306
  12.5 0.0 collective-permute-start.7
  12.5 2.9 %collective-permute-start.1 = (bf16[256,512]{1,0:T(8,128)(2,1)S(1)}, bf16[256,512]{1,0:T(8,128)(2,1)}, u32[]{:S(2)}, u32[]{:S(2)}) collective-permute-start(bf16[256,512]{1,0:T(8,128)(2,1)S(1)} %collective-permute-done.a2_any), channel_id=1, source_target_pairs={{0,0},{2,2},{4,4},{14,14},{6,8},{8,6},{10,12},{12,10},{1,1},{3,3},... | collective-permute-start | bytes 786440 | tf_op jit(solution)/shard_map/rest/ppermute | solution.py:302
  15.4 1.9 %shard_map.101 = (bf16[512,256]{1,0:T(8,128)(2,1)S(1)}, bf16[256,512]{1,0:T(8,128)(2,1)S(1)}) custom-call(bf16[256,512]{1,0:T(8,128)(2,1)} %a0.1, bf16[256,512]{1,0:T(8,128)(2,1)} %collective-permute-done.2.b_hbm, bf16[1024,512]{1,0:T(8,128)(2,1)} %wq_hbm.1), custom_call_target="tpu_custom_call" | custom-call | flops 2000000000 | tf_op jit(solution)/shard_map/pallas_call | solution.py:310
  17.4 0.0 copy-start.3
  17.4 1.2 %collective-permute-start.3 = (bf16[8,64,128]{2,1,0:T(8,128)(2,1)S(1)}, bf16[8,64,128]{2,1,0:T(8,128)(2,1)S(1)}, u32[]{:S(2)}, u32[]{:S(2)}) collective-permute-start(bf16[8,64,128]{2,1,0:T(8,128)(2,1)S(1)} %get-tuple-element.27), channel_id=1, source_target_pairs={{0,1},{1,0},{2,3},{3,2},{4,5},{5,4},{6,7},{7,6},{8,9},{9,8},{10,11... | collective-permute-start | bytes 393224 | tf_op jit(solution)/shard_map/down_swap/ppermute | solution.py:306
  18.6 0.1 collective-permute-start.8
  18.7 0.9 %collective-permute-done.3.other = bf16[8,64,128]{2,1,0:T(8,128)(2,1)S(1)} collective-permute-done((bf16[8,64,128]{2,1,0:T(8,128)(2,1)S(1)}, bf16[8,64,128]{2,1,0:T(8,128)(2,1)S(1)}, u32[]{:S(2)}, u32[]{:S(2)}) %collective-permute-start.3) | collective-permute-done | bytes 131104 | tf_op jit(solution)/shard_map/down_swap/ppermute | solution.py:306
  19.6 3.5 %shard_map.103 = (f32[8,72,256]{2,1,0:T(8,128)S(1)}, f32[8,256]{1,0:T(8,128)S(1)}, bf16[1024,128]{1,0:T(8,128)(2,1)S(1)}, bf16[128,512]{1,0:T(8,128)(2,1)S(1)}, ...) custom-call(bf16[8,128,128]{2,1,0:T(8,128)(2,1)S(1)} %all-to-all-done.got, ...), custom_call_target="tpu_custom_call" | custom-call | flops 100000000 | tf_op jit(solution)/shard_map/pallas_call | solution.py:375
  23.1 1.6 %collective-permute-done.1.a3_any = bf16[256,512]{1,0:T(8,128)(2,1)} collective-permute-done((bf16[256,512]{1,0:T(8,128)(2,1)S(1)}, bf16[256,512]{1,0:T(8,128)(2,1)}, u32[]{:S(2)}, u32[]{:S(2)}) %collective-permute-start.1) | collective-permute-done | bytes 262176 | tf_op jit(solution)/shard_map/rest/ppermute | solution.py:302
  24.7 0.4 %collective-permute-start.9 = (bf16[256,512]{1,0:T(8,128)(2,1)}, bf16[256,512]{1,0:T(8,128)(2,1)S(1)}, u32[]{:S(2)}, u32[]{:S(2)}) collective-permute-start(bf16[256,512]{1,0:T(8,128)(2,1)} %collective-permute-done.1.a3_any), channel_id=1, source_target_pairs={{0,1},{1,0},{2,3},{3,2},{4,5},{5,4},{6,7},{7,6},{8,9},{9,8},{10,11... | collective-permute-start | bytes 786440 | tf_op jit(solution)/shard_map/rest_swap/ppermute | solution.py:306
  25.1 1.2 %shard_map.104 = (bf16[256,512]{1,0:T(8,128)(2,1)S(1)}, bf16[512,256]{1,0:T(8,128)(2,1)S(1)}, s32[8,128]{1,0:T(8,128)S(1)}) custom-call(s32[8,128]{1,0:T(8,128)S(1)} %get-tuple-element.33.reach_ref, bf16[256,512]{1,0:T(8,128)(2,1)S(1)} %get-tuple-element.34.ax, bf16[256,512]{1,0:T(8,128)(2,1)S(1)} %collective-permute-done.8.bx_any, ...), custom_call_target="tpu_custom_call" | custom-call | flops 100000000 | tf_op jit(solution)/shard_map/pallas_call | solution.py:393
  26.3 0.2 collective-permute-done.9.b3_any
  26.5 3.5 %shard_map.105 = bf16[256,512]{1,0:T(8,128)(2,1)} custom-call(s32[8,128]{1,0:T(8,128)S(1)} %get-tuple-element.37.reach_ref, bf16[256,512]{1,0:T(8,128)(2,1)} %collective-permute-done.1.a3_any, bf16[256,512]{1,0:T(8,128)(2,1)S(1)} %collective-permute-done.9.b3_any, bf16[512,256]{1,0:T(8,128)(2,1)S(1)} %get-tuple-element.25.q_ref, ...), custom_call_target="tpu_custom_call" | custom-call | flops 100000000 | tf_op jit(solution)/shard_map/pallas_call | solution.py:403
  (13 shorter events, 0.0 us)
Async XLA Ops:
  0.0 9.9 %collective-permute-start = (bf16[256,512]{1,0:T(8,128)(2,1)}, bf16[256,512]{1,0:T(8,128)(2,1)S(1)}, u32[]{:S(2)}, u32[]{:S(2)}) collective-permute-start(bf16[256,512]{1,0:T(8,128)(2,1)} %a0.1), channel_id=1, source_target_pairs={{0,4},{2,6},{4,8},{6,10},{8,12},{10,14},{12,0},{14,2},{1,5},{3,7},... | collective-permute-start | bytes 786440 | tf_op jit(solution)/shard_map/two/ppermute | solution.py:302
  1.3 8.6 %collective-permute-start.4 = (bf16[256,512]{1,0:T(8,128)(2,1)}, bf16[256,512]{1,0:T(8,128)(2,1)S(1)}, u32[]{:S(2)}, u32[]{:S(2)}) collective-permute-start(bf16[256,512]{1,0:T(8,128)(2,1)} %a0.1), channel_id=1, source_target_pairs={{0,2},{2,0},{4,6},{6,4},{8,10},{10,8},{12,14},{14,12},{1,3},{3,1},... | collective-permute-start | bytes 786440 | tf_op jit(solution)/shard_map/near/ppermute | solution.py:302
  4.3 3.8 %copy-start.2 = (bf16[256,512]{1,0:T(8,128)(2,1)S(1)}, bf16[256,512]{1,0:T(8,128)(2,1)}, u32[]{:S(2)}) copy-start(bf16[256,512]{1,0:T(8,128)(2,1)} %a0.1) | copy-start | bytes 786436
  4.3 13.1 %all-to-all-start = ((bf16[8,128,128]{2,1,0:T(8,128)(2,1)}), bf16[8,128,128]{2,1,0:T(8,128)(2,1)S(1)}, u32[]{:S(2)}, u32[]{:S(2)}) async-start(bf16[8,128,128]{2,1,0:T(8,128)(2,1)} %get-tuple-element.24), calls=%async_computation | async-start | bytes 524288 | tf_op jit(solution)/shard_map/all_to_all | solution.py:336
  8.1 7.3 %collective-permute-start.2 = (bf16[256,512]{1,0:T(8,128)(2,1)S(1)}, bf16[256,512]{1,0:T(8,128)(2,1)}, u32[]{:S(2)}, u32[]{:S(2)}) collective-permute-start(bf16[256,512]{1,0:T(8,128)(2,1)S(1)} %copy-done.2), channel_id=1, source_target_pairs={{0,1},{1,0},{2,3},{3,2},{4,5},{5,4},{6,7},{7,6},{8,9},{9,8},{10,11... | collective-permute-start | bytes 786440 | tf_op jit(solution)/shard_map/own_swap/ppermute | solution.py:306
  10.6 6.7 %copy-start = (bf16[1024,512]{1,0:T(8,128)(2,1)S(1)}, bf16[1024,512]{1,0:T(8,128)(2,1)}, u32[]{:S(2)}) copy-start(bf16[1024,512]{1,0:T(8,128)(2,1)} %wk.7) | copy-start | bytes 3145732
  10.6 6.8 %copy-start.1 = (bf16[1024,512]{1,0:T(8,128)(2,1)S(1)}, bf16[1024,512]{1,0:T(8,128)(2,1)}, u32[]{:S(2)}) copy-start(bf16[1024,512]{1,0:T(8,128)(2,1)} %wv.7) | copy-start | bytes 3145732
  10.6 8.0 %collective-permute-start.5 = (bf16[256,512]{1,0:T(8,128)(2,1)}, bf16[256,512]{1,0:T(8,128)(2,1)}, u32[]{:S(2)}, u32[]{:S(2)}) collective-permute-start(bf16[256,512]{1,0:T(8,128)(2,1)} %broadcast_select_fusion), channel_id=1, source_target_pairs={{0,2},{2,0},{4,6},{6,4},{8,10},{10,8},{12,14},{14,12},{1,5},{3,7},... | collective-permute-start | bytes 786440 | tf_op jit(solution)/shard_map/split/ppermute | solution.py:359
  11.8 6.9 %collective-permute-start.6 = (bf16[256,512]{1,0:T(8,128)(2,1)S(1)}, bf16[256,512]{1,0:T(8,128)(2,1)}, u32[]{:S(2)}, u32[]{:S(2)}) collective-permute-start(bf16[256,512]{1,0:T(8,128)(2,1)S(1)} %collective-permute-done.a2_any), channel_id=1, source_target_pairs={{0,1},{1,0},{2,3},{3,2},{4,5},{5,4},{6,7},{7,6},{8,9},{9,8},{10,11... | collective-permute-start | bytes 786440 | tf_op jit(solution)/shard_map/two_swap/ppermute | solution.py:306
  12.5 6.3 %collective-permute-start.7 = (bf16[256,512]{1,0:T(8,128)(2,1)S(1)}, bf16[256,512]{1,0:T(8,128)(2,1)}, u32[]{:S(2)}, u32[]{:S(2)}) collective-permute-start(bf16[256,512]{1,0:T(8,128)(2,1)S(1)} %collective-permute-done.4.a1_any), channel_id=1, source_target_pairs={{0,1},{1,0},{2,3},{3,2},{4,5},{5,4},{6,7},{7,6},{8,9},{9,8},{10,11... | collective-permute-start | bytes 786440 | tf_op jit(solution)/shard_map/near_swap/ppermute | solution.py:306
  12.5 12.2 %collective-permute-start.1 = (bf16[256,512]{1,0:T(8,128)(2,1)S(1)}, bf16[256,512]{1,0:T(8,128)(2,1)}, u32[]{:S(2)}, u32[]{:S(2)}) collective-permute-start(bf16[256,512]{1,0:T(8,128)(2,1)S(1)} %collective-permute-done.a2_any), channel_id=1, source_target_pairs={{0,0},{2,2},{4,4},{14,14},{6,8},{8,6},{10,12},{12,10},{1,1},{3,3},... | collective-permute-start | bytes 786440 | tf_op jit(solution)/shard_map/rest/ppermute | solution.py:302
  17.4 2.2 %copy-start.3 = (bf16[256,512]{1,0:T(8,128)(2,1)S(1)}, bf16[256,512]{1,0:T(8,128)(2,1)}, u32[]{:S(2)}) copy-start(bf16[256,512]{1,0:T(8,128)(2,1)} %a0.1) | copy-start | bytes 786436
  17.4 2.2 %collective-permute-start.3 = (bf16[8,64,128]{2,1,0:T(8,128)(2,1)S(1)}, bf16[8,64,128]{2,1,0:T(8,128)(2,1)S(1)}, u32[]{:S(2)}, u32[]{:S(2)}) collective-permute-start(bf16[8,64,128]{2,1,0:T(8,128)(2,1)S(1)} %get-tuple-element.27), channel_id=1, source_target_pairs={{0,1},{1,0},{2,3},{3,2},{4,5},{5,4},{6,7},{7,6},{8,9},{9,8},{10,11... | collective-permute-start | bytes 393224 | tf_op jit(solution)/shard_map/down_swap/ppermute | solution.py:306
  18.6 6.5 %collective-permute-start.8 = (bf16[256,512]{1,0:T(8,128)(2,1)}, bf16[256,512]{1,0:T(8,128)(2,1)S(1)}, u32[]{:S(2)}, u32[]{:S(2)}) collective-permute-start(bf16[256,512]{1,0:T(8,128)(2,1)} %collective-permute-done.5.ax_any), channel_id=1, source_target_pairs={{0,1},{1,0},{2,3},{3,2},{4,5},{5,4},{6,7},{7,6},{8,9},{9,8},{10,11... | collective-permute-start | bytes 786440 | tf_op jit(solution)/shard_map/cross_swap/ppermute | solution.py:306
  24.7 1.8 %collective-permute-start.9 = (bf16[256,512]{1,0:T(8,128)(2,1)}, bf16[256,512]{1,0:T(8,128)(2,1)S(1)}, u32[]{:S(2)}, u32[]{:S(2)}) collective-permute-start(bf16[256,512]{1,0:T(8,128)(2,1)} %collective-permute-done.1.a3_any), channel_id=1, source_target_pairs={{0,1},{1,0},{2,3},{3,2},{4,5},{5,4},{6,7},{7,6},{8,9},{9,8},{10,11... | collective-permute-start | bytes 786440 | tf_op jit(solution)/shard_map/rest_swap/ppermute | solution.py:306
